TPU v7x, 128 devices: a whole 4x4x4 slice. The times are simulated.
128 devices in a mesh: pipe: 8 (over z_lo, x), tensor: 4 (over z_hi, core), dp: 4 (over y).
Axes of the slice: x: 4, y: 4, z: 4 (z_hi: 2, z_lo: 2; z = z_hi * 2 + z_lo), core: 2. Of those that a mesh axis runs over, the one named last changes fastest.
Arguments:
- encoded: bfloat16 [4, 1024, 4096], P('dp', 'pipe'), may hold values from -6 to 6
- kv_weight: bfloat16 [8, 2, 4096, 2048], P('pipe', None, None, 'tensor'), may hold values from -0.09375 to 0.09375
- queries: bfloat16 [4, 8, 512, 2048], P('dp', 'pipe', None, 'tensor'), may hold values from -70 to 70
- cotangent: bfloat16 [4, 8, 512, 2048], P('dp', 'pipe', None, 'tensor'), may hold values from -6 to 6
Outputs:
- attended: bfloat16 [4, 8, 512, 2048], P('dp', 'pipe', None, 'tensor')
- query_grad: bfloat16 [4, 8, 512, 2048], P('dp', 'pipe', None, 'tensor')
- encoded_grad: bfloat16 [4, 1024, 4096], P('dp', 'pipe')
- weight_grad: bfloat16 [8, 2, 4096, 2048], P('pipe', None, 'dp', 'tensor')
All inputs are finite; a program needn't handle non-finite values.
Results may differ from a plain program's by a relative error of at most 0.03.
The roundings to bfloat16 on the way count: a program that leaves them out, or rounds other values in their place, can miss the bound.
Values may be sent and summed in bfloat16 or wider, within the bound.
No kernel may reach another device: no remote copies, remote signals or barrier semaphores. Data moves between devices by JAX's collectives and lax.ppermute only.
A program may use at most 128 MiB of HBM per device.

v0:
```python
import functools

import jax
import jax.numpy as jnp
from jax import lax
from jax.experimental import pallas as pl
from jax.experimental.pallas import tpu as pltpu
from jax.sharding import PartitionSpec as P

HEAD_DIM = 256
ALL = ("pipe", "tensor", "dp")
F32, BF16 = jnp.float32, jnp.bfloat16
NT = (((1,), (1,)), ((), ()))
TN = (((0,), (0,)), ((), ()))
TILE = 512
WHOLE = pl.BlockSpec(memory_space=pltpu.VMEM)
SCALARS = pl.BlockSpec(memory_space=pltpu.SMEM)


LITTLE = pl.CostEstimate(flops=1000, bytes_accessed=1000, transcendentals=0)


def call(body, operands, shapes, scratch=(), index=0, after=(), room=8):
    many = isinstance(shapes, (list, tuple))
    count = len(operands)
    operands = [*operands, *after]

    def reads(*refs):
        body(*refs[:count], *refs[count + len(after) :])

    return pl.pallas_call(
        reads,
        in_specs=[SCALARS] * index
        + [WHOLE] * (count - index)
        + [pl.BlockSpec(memory_space=pl.ANY)] * len(after),
        out_specs=[WHOLE] * len(shapes) if many else WHOLE,
        out_shape=shapes,
        scratch_shapes=scratch,
        compiler_params=pltpu.CompilerParams(vmem_limit_bytes=room * 1024 * 1024),
        cost_estimate=LITTLE,
    )(*operands)


def bf16(*shape):
    return jax.ShapeDtypeStruct(shape, BF16)


def pairs(move):
    def index(x, y, z, core):
        pipe = (z % 2) * 4 + x
        tensor = (z // 2) * 2 + core
        return (pipe * 4 + tensor) * 4 + y

    found = []
    for x in range(4):
        for y in range(4):
            for z in range(4):
                for core in range(2):
                    to_x, to_y, to_z, to_core = move(x, y, z, core)
                    found.append((index(x, y, z, core), index(to_x, to_y, to_z % 4, to_core)))
    return found


def partner(place, core, which):
    return place ^ 1 if core == which else 3 - place


X_FIRST = pairs(lambda x, y, z, core: (partner(x, core, 0), y, z, core))
X_SECOND = pairs(lambda x, y, z, core: (partner(x, core, 1), y, z, core))
Y_FIRST = pairs(lambda x, y, z, core: (x, partner(y, core, 0), z, core))
Y_SECOND = pairs(lambda x, y, z, core: (x, partner(y, core, 1), z, core))
ALONG_Z = pairs(lambda x, y, z, core: (x, y, z + 1 - 2 * core, core))
BACK_Z = pairs(lambda x, y, z, core: (x, y, z - 1 + 2 * core, core))
ACROSS_Z = pairs(lambda x, y, z, core: (x, y, z + 2, core))
SWAP = pairs(lambda x, y, z, core: (x, y, z, 1 - core))


def send(array, route):
    return lax.ppermute(array, ALL, route)


def project_body(a, b, c, d, w, keys, values):
    x = jnp.concatenate([a[...], b[...], c[...], d[...]], 0)
    keys[...] = jnp.dot(x, w[0, 0], preferred_element_type=F32).astype(BF16)
    values[...] = jnp.dot(x, w[0, 1], preferred_element_type=F32).astype(BF16)


def project(pieces, kv_weight):
    shape = bf16(4 * pieces[0].shape[0], kv_weight.shape[3])
    return call(project_body, [*pieces, kv_weight], [shape, shape])


def arrange(groups):
    quarter = groups[0].shape[0] // 4

    def at(group, place):
        return groups[group][place * quarter : (place + 1) * quarter, :]

    order = [(0, 0), (1, 0), (1, 2), (3, 0), (0, 2), (2, 0), (2, 2), (3, 2)]
    return jnp.concatenate(
        [at(g, p) for g, p in order] + [at(g, p + 1) for g, p in order], 0
    )


def attend_body(q, g, k0, k1, k2, k3, v0, v1, v2, v3, att, dq, kg, vg, kgt, vgt, low, dlow):
    scale = HEAD_DIM ** (-0.5)
    total = q.shape[2]
    chunk = total // 2
    for head in range(q.shape[3] // HEAD_DIM):
        cols = slice(head * HEAD_DIM, (head + 1) * HEAD_DIM)
        k = arrange([ref[:, cols] for ref in (k0, k1, k2, k3)])
        v = arrange([ref[:, cols] for ref in (v0, v1, v2, v3)])
        for part in range(2):
            rows = slice(part * chunk, (part + 1) * chunk)
            g_rows = g[0, 0, rows, cols]
            scores = scale * lax.dot_general(
                q[0, 0, rows, cols], k, NT, preferred_element_type=F32
            )
            expd = jnp.exp(scores - jnp.max(scores, axis=-1, keepdims=True))
            probs = expd * (1.0 / jnp.sum(expd, axis=-1, keepdims=True))
            probs_low = probs.astype(BF16)
            low[head, rows, :] = probs_low
            out = jnp.dot(probs_low, v, preferred_element_type=F32).astype(BF16)
            att[0, 0, rows, cols] = out
            dprobs = lax.dot_general(g_rows, v, NT, preferred_element_type=F32)
            delta = jnp.sum(g_rows.astype(F32) * out.astype(F32), axis=-1, keepdims=True)
            ds_low = (probs * (dprobs - delta)).astype(BF16)
            dlow[head, rows, :] = ds_low
            dq[0, 0, rows, cols] = (
                scale * jnp.dot(ds_low, k, preferred_element_type=F32)
            ).astype(BF16)
        value_t = lax.dot_general(g[0, 0, :, cols], low[head], TN, preferred_element_type=F32)
        vgt[cols, :] = value_t.astype(BF16)
        vg[:, cols] = value_t.T.astype(BF16)
        key_t = scale * lax.dot_general(
            q[0, 0, :, cols], dlow[head], TN, preferred_element_type=F32
        )
        kgt[cols, :] = key_t.astype(BF16)
        kg[:, cols] = key_t.T.astype(BF16)


def attend(queries, cotangent, keys, values):
    _, _, total, width = queries.shape
    span = 4 * keys[0].shape[0]
    same = bf16(*queries.shape)
    return call(
        attend_body,
        [queries, cotangent, *keys, *values],
        [same, same, bf16(span, width), bf16(span, width), bf16(width, span), bf16(width, span)],
        [pltpu.VMEM((width // HEAD_DIM, total, span), BF16)] * 2,
        room=16,
    )


def weight_body(count, index, grad_t, *refs):
    pieces, out = refs[:count], refs[count]
    for i in range(index.shape[0]):
        start = pl.multiple_of(index[i], TILE)
        rows = jnp.concatenate([piece[:, pl.ds(start, TILE)] for piece in pieces], 0)
        out[:, i * TILE : (i + 1) * TILE] = jnp.dot(
            grad_t[...], rows, preferred_element_type=F32
        ).astype(BF16)


def weight_part(index, grad_t, pieces, after=()):
    return call(
        functools.partial(weight_body, len(pieces)),
        [index, grad_t, *pieces],
        bf16(grad_t.shape[0], index.shape[0] * TILE),
        index=1,
        after=after,
    )


def share_body(part, keep, first, second, *refs):
    out, terms, turned, sems = refs[-4:]
    span = second.shape[1]
    step = TILE // 2
    sources = (keep.at[:, span:], first.at[:, :span], second)
    coming = [
        pltpu.make_async_copy(source, terms.at[i], sems.at[i])
        for i, source in enumerate(sources)
    ]
    for copy in coming:
        copy.start()
    for copy in coming:
        copy.wait()
    going = []
    for i in range(span // step):
        cols = slice(i * step, (i + 1) * step)
        total = terms[0, :, cols].astype(F32) + terms[1, :, cols].astype(F32)
        total = total + terms[2, :, cols].astype(F32)
        turned[cols, :] = total.T.astype(BF16)
        going.append(
            pltpu.make_async_copy(turned.at[cols, :], out.at[0, part, cols, :], sems.at[3 + i])
        )
        going[-1].start()
    for copy in going:
        copy.wait()


def share(part, keep, first, second, into=None):
    width, span = second.shape
    given = [] if into is None else [into]
    return pl.pallas_call(
        functools.partial(share_body, part),
        in_specs=[pl.BlockSpec(memory_space=pl.ANY)] * (3 + len(given)),
        out_specs=pl.BlockSpec(memory_space=pl.ANY),
        out_shape=bf16(1, 2, span, width),
        scratch_shapes=[
            pltpu.VMEM((3, width, span), BF16),
            pltpu.VMEM((span, width), BF16),
            pltpu.SemaphoreType.DMA((3 + 2 * span // TILE,)),
        ],
        input_output_aliases={3: 0} if given else {},
        compiler_params=pltpu.CompilerParams(vmem_limit_bytes=40 * 1024 * 1024),
        cost_estimate=LITTLE,
    )(keep, first, second, *given)


def place_body(core, mine, theirs, out, sems):
    half = mine.shape[0]
    low = pl.multiple_of(core[0] * half, half)
    high = pl.multiple_of((1 - core[0]) * half, half)
    copies = [
        pltpu.make_async_copy(mine, out.at[0, pl.ds(low, half), :], sems.at[0]),
        pltpu.make_async_copy(theirs, out.at[0, pl.ds(high, half), :], sems.at[1]),
    ]
    for copy in copies:
        copy.start()
    for copy in copies:
        copy.wait()


def place(core, mine, theirs):
    half, depth = mine.shape
    return pl.pallas_call(
        place_body,
        in_specs=[SCALARS, WHOLE, WHOLE],
        out_specs=pl.BlockSpec(memory_space=pl.ANY),
        out_shape=bf16(1, 2 * half, depth),
        scratch_shapes=[pltpu.SemaphoreType.DMA((2,))],
        compiler_params=pltpu.CompilerParams(vmem_limit_bytes=4 * 1024 * 1024),
        cost_estimate=LITTLE,
    )(core[None], mine, theirs)


def load_body(*refs):
    count = len(refs) // 2
    sems = refs[-1]
    copies = [
        pltpu.make_async_copy(refs[i], refs[count + i], sems.at[i]) for i in range(count)
    ]
    for copy in copies:
        copy.start()
    for copy in copies:
        copy.wait()


def load(*arrays):
    return pl.pallas_call(
        load_body,
        in_specs=[pl.BlockSpec(memory_space=pl.ANY)] * len(arrays),
        out_specs=[WHOLE] * len(arrays),
        out_shape=[bf16(*array.shape) for array in arrays],
        scratch_shapes=[pltpu.SemaphoreType.DMA((len(arrays),))],
        compiler_params=pltpu.CompilerParams(vmem_limit_bytes=4 * 1024 * 1024),
        cost_estimate=LITTLE,
    )(*arrays)


def encoder_body(low, left, kg, vg, w, *refs):
    outs = refs[-1:] if len(refs) == 1 else refs[-2:]
    rows = slice(low, low + kg.shape[0] // 2)
    half = outs[0].shape[0]
    for i in range(outs[0].shape[1] // TILE):
        cols = slice(i * TILE, (i + 1) * TILE)
        from_w = slice(left + i * TILE, left + (i + 1) * TILE)
        total = lax.dot_general(kg[rows, :], w[0, 0, from_w, :], NT, preferred_element_type=F32)
        total = total + lax.dot_general(
            vg[rows, :], w[0, 1, from_w, :], NT, preferred_element_type=F32
        )
        if len(refs) > 1:
            total = total + refs[0][:, cols].astype(F32)
        for j, out in enumerate(outs):
            out[:, cols] = total[j * half : (j + 1) * half].astype(BF16)


def encoder_part(key_grad, value_grad, kv_weight, side, columns, moved=None, after=()):
    rows, depth = key_grad.shape[0] // 2, kv_weight.shape[2] // 2
    return call(
        functools.partial(encoder_body, side * rows, columns * depth),
        [key_grad, value_grad, kv_weight] + ([] if moved is None else [moved]),
        bf16(rows, depth) if moved is None else [bf16(rows // 2, depth)] * 2,
        after=after,
        room=12,
    )


def tie(array, *others):
    return lax.optimization_barrier((array, *others))[0]


def on_device(encoded, kv_weight, queries, cotangent):
    core = lax.axis_index("tensor") % 2
    y = lax.axis_index("dp")
    block = encoded[0]
    half = block.shape[0] // 2

    one, other = y ^ 1, 3 - y
    first = jnp.where(core == 0, one, other)
    second = jnp.where(core == 0, other, one)

    def starts(*places):
        index = jnp.stack([2 * TILE * place + low for place in places for low in (0, TILE)])
        return index.astype(jnp.int32)

    own = lax.dynamic_slice_in_dim(block, core * half, half, 0)
    too = lax.dynamic_slice_in_dim(block, (1 - core) * half, half, 0)
    own, too, go, stay = lax.optimization_barrier(
        (own, too, starts(first, (y + 2) % 4), starts(second, y))
    )
    h, h_too = {"o": own}, {"o": too}
    g, g_too = {}, {}
    h["a"] = send(h["o"], X_FIRST)
    h["b"] = send(h["o"], X_SECOND)
    g["o"] = send(h["o"], ALONG_Z)
    kv_weight, queries, cotangent = load(kv_weight, queries, cotangent)
    g["a"] = send(tie(h["a"], kv_weight, queries), ALONG_Z)
    h["d"] = send(h["a"], X_SECOND)
    g["b"] = send(h["b"], ALONG_Z)
    h_too["a"] = send(h["a"], SWAP)
    h_too["b"] = send(h["b"], SWAP)
    g_too["o"] = send(g["o"], SWAP)
    done = [
        project((h["o"], h_too["o"], h["a"], h_too["a"]), kv_weight),
        project((g["o"], g_too["o"], h["b"], h_too["b"]), kv_weight),
    ]
    g["d"] = send(tie(g["a"], done[0][0], done[1][0]), X_SECOND)
    h_too["d"] = send(h["d"], SWAP)
    g_too["a"] = send(g["a"], SWAP)
    g_too["b"] = send(g["b"], SWAP)
    done.append(project((g["a"], g_too["a"], h["d"], h_too["d"]), kv_weight))
    g_too["d"] = send(tie(g["d"], done[2][0]), SWAP)
    done.append(project((g["b"], g_too["b"], g["d"], g_too["d"]), kv_weight))
    keys, values = zip(*done)
    order = ["ho", "go", "hb", "gb", "ha", "ga", "hd", "gd"]
    pieces = [{"h": h, "g": g}[name[0]][name[1]] for name in order]
    pieces += [{"h": h_too, "g": g_too}[name[0]][name[1]] for name in order]

    attended, query_grad, key_grad, value_grad, key_grad_t, value_grad_t = attend(
        queries, cotangent, keys, values
    )

    grads = (key_grad, value_grad, kv_weight)
    moved = [encoder_part(*grads, 1, i) for i in range(2)]
    value_out = weight_part(go, value_grad_t, pieces, moved)
    moved = [send(part, SWAP) for part in moved]
    early = (value_out,)
    kept, x_out = zip(*[encoder_part(*grads, 0, i, moved[i], early) for i in range(2)])
    key_out = weight_part(go, key_grad_t, pieces, x_out)
    value_keep = weight_part(stay, value_grad_t, pieces, (key_out,))
    key_keep = weight_part(stay, key_grad_t, pieces, (value_keep,))

    def onward(keep, moved):
        span = keep.shape[1] // 2
        return (keep[:, :span].astype(F32) + moved[:, span:].astype(F32)).astype(BF16)

    value_in = send(value_out, Y_FIRST)
    key_in = send(tie(key_out, value_in), Y_FIRST)
    value_two = send(tie(onward(value_keep, value_in), key_in), Y_SECOND)
    key_two = send(tie(onward(key_keep, key_in), value_two), Y_SECOND)

    last = []
    for keep, out in zip(kept, x_out):
        came = send(out, X_FIRST)
        total = tie(keep, key_keep).astype(F32) + came.astype(F32)
        came = send(total[2 * half :].astype(BF16), X_SECOND)
        total = total[: 2 * half] + came.astype(F32)
        here = total[:half] + send(total[half:].astype(BF16), BACK_Z).astype(F32)
        here = here.astype(BF16)
        came = send(here, ACROSS_Z)
        last.append((tie(here, key_in).astype(F32) + came.astype(F32)).astype(BF16))
    last = jnp.concatenate(last, 1)
    enc_grad = place(core, last, send(last, SWAP))

    weight_grad = share(1, value_keep, value_in, value_two)
    weight_grad = share(0, key_keep, key_in, key_two, weight_grad)
    return (attended, query_grad, enc_grad, weight_grad)


def solution(mesh):
    return jax.shard_map(
        on_device,
        mesh=mesh,
        in_specs=(
            P("dp", "pipe", None),
            P("pipe", None, None, "tensor"),
            P("dp", "pipe", None, "tensor"),
            P("dp", "pipe", None, "tensor"),
        ),
        out_specs=(
            P("dp", "pipe", None, "tensor"),
            P("dp", "pipe", None, "tensor"),
            P("dp", "pipe", None),
            P("pipe", None, "dp", "tensor"),
        ),
        check_vma=False,
    )
```

profile of v0, /device:TPU:0, one launch (start us, length us, event | category | flops | bytes accessed | tf_op | source)
XLA Modules:
  0.0 146.6 jit_solution(15755431882725402322)
XLA Ops:
  0.7 1.4 dynamic-slice_bitcast_fusion
  2.2 2.0 %collective-permute-start.2 = (bf16[64,4096]{1,0:T(8,128)(2,1)S(1)}, bf16[64,4096]{1,0:T(8,128)(2,1)S(1)}, u32[]{:S(2)}, u32[]{:S(2)}) collective-permute-start(bf16[64,4096]{1,0:T(8,128)(2,1)S(1)} %get-tuple-element.41.refs_0_.refs_2_), channel_id=1, source_target_pairs={{0,64},{4,76},{64,8},{68,4},{8,72},{12,68},{72,0},{76,12},{1,65},{... | collective-permute-start | bytes 1572872 | tf_op jit(solution)/shard_map/ppermute | solution.py:79
  4.2 2.8 %collective-permute-start.4 = (bf16[64,4096]{1,0:T(8,128)(2,1)S(1)}, bf16[64,4096]{1,0:T(8,128)(2,1)S(1)}, u32[]{:S(2)}, u32[]{:S(2)}) collective-permute-start(bf16[64,4096]{1,0:T(8,128)(2,1)S(1)} %get-tuple-element.41.refs_0_.refs_2_), channel_id=1, source_target_pairs={{0,48},{4,20},{64,112},{68,84},{8,56},{12,28},{72,120},{76,92},{1,... | collective-permute-start | bytes 1572872 | tf_op jit(solution)/shard_map/ppermute | solution.py:79
  7.2 3.4 %copy-done = bf16[1,2,4096,512]{3,2,1,0:T(8,128)(2,1)S(1)} copy-done((bf16[1,2,4096,512]{3,2,1,0:T(8,128)(2,1)S(1)}, bf16[1,2,4096,512]{3,2,1,0:T(8,128)(2,1)}, u32[]{:S(2)}) %copy-start) | copy-done | bytes 8388632
  11.2 2.2 %collective-permute-done.2.refs_0_.refs_3_ = bf16[64,4096]{1,0:T(8,128)(2,1)S(1)} collective-permute-done((bf16[64,4096]{1,0:T(8,128)(2,1)S(1)}, bf16[64,4096]{1,0:T(8,128)(2,1)S(1)}, u32[]{:S(2)}, u32[]{:S(2)}) %collective-permute-start.2) | collective-permute-done | bytes 524320 | tf_op jit(solution)/shard_map/ppermute | solution.py:79
  13.5 4.7 %collective-permute-done.4.refs_2_.refs_4_ = bf16[64,4096]{1,0:T(8,128)(2,1)S(1)} collective-permute-done((bf16[64,4096]{1,0:T(8,128)(2,1)S(1)}, bf16[64,4096]{1,0:T(8,128)(2,1)S(1)}, u32[]{:S(2)}, u32[]{:S(2)}) %collective-permute-start.4) | collective-permute-done | bytes 524320 | tf_op jit(solution)/shard_map/ppermute | solution.py:79
  18.2 1.5 %collective-permute-done.refs_2_.refs_6_ = bf16[64,4096]{1,0:T(8,128)(2,1)S(1)} collective-permute-done((bf16[64,4096]{1,0:T(8,128)(2,1)S(1)}, bf16[64,4096]{1,0:T(8,128)(2,1)S(1)}, u32[]{:S(2)}, u32[]{:S(2)}) %collective-permute-start) | collective-permute-done | bytes 524320 | tf_op jit(solution)/shard_map/ppermute | solution.py:79
  20.0 0.9 collective-permute-start.6
  20.9 2.1 %collective-permute-start.8 = (bf16[64,4096]{1,0:T(8,128)(2,1)S(1)}, bf16[64,4096]{1,0:T(8,128)(2,1)S(1)}, u32[]{:S(2)}, u32[]{:S(2)}) collective-permute-start(bf16[64,4096]{1,0:T(8,128)(2,1)S(1)} %collective-permute-done.refs_2_.refs_6_), channel_id=1, source_target_pairs={{0,48},{4,20},{64,112},{68,84},{8,56},{12,28},{72,120},{76,92},{1,... | collective-permute-start | bytes 1572872 | tf_op jit(solution)/shard_map/ppermute | solution.py:79
  23.0 1.9 %collective-permute-start.10 = (bf16[64,4096]{1,0:T(8,128)(2,1)S(1)}, bf16[64,4096]{1,0:T(8,128)(2,1)S(1)}, u32[]{:S(2)}, u32[]{:S(2)}) collective-permute-start(bf16[64,4096]{1,0:T(8,128)(2,1)S(1)} %collective-permute-done.4.refs_2_.refs_4_), channel_id=1, source_target_pairs={{0,64},{4,76},{64,8},{68,4},{8,72},{12,68},{72,0},{76,12},{1,65},{... | collective-permute-start | bytes 1572872 | tf_op jit(solution)/shard_map/ppermute | solution.py:79
  24.9 2.3 %shard_map.77 = (bf16[256,512]{1,0:T(8,128)(2,1)S(1)}, bf16[256,512]{1,0:T(8,128)(2,1)S(1)}) custom-call(bf16[64,4096]{1,0:T(8,128)(2,1)S(1)} %collective-permute-done.2.refs_0_.refs_3_, bf16[64,4096]{1,0:T(8,128)(2,1)S(1)} %collective-permute-done.3.refs_1_.refs_11_, bf16[64,4096]{1,0:T(8,128)(2,1)S(1)} %collective-permute-done.4.refs_2_.refs_4_, ...), custom_call_target="tpu_custom_call" | custom-call | flops 1000 | bytes 1000 | tf_op jit(solution)/shard_map/pallas_call | solution.py:31
  27.2 2.3 %shard_map.76 = (bf16[256,512]{1,0:T(8,128)(2,1)S(1)}, bf16[256,512]{1,0:T(8,128)(2,1)S(1)}) custom-call(bf16[64,4096]{1,0:T(8,128)(2,1)S(1)} %get-tuple-element.41.refs_0_.refs_2_, bf16[64,4096]{1,0:T(8,128)(2,1)S(1)} %get-tuple-element.42.refs_1_.refs_10_, bf16[64,4096]{1,0:T(8,128)(2,1)S(1)} %collective-permute-done.refs_2_.refs_6_, ...), custom_call_target="tpu_custom_call" | custom-call | flops 1000 | bytes 1000 | tf_op jit(solution)/shard_map/pallas_call | solution.py:31
  30.4 0.9 collective-permute-done.8.refs_2_.refs_8_
  31.3 2.4 %collective-permute-start.12 = (bf16[64,4096]{1,0:T(8,128)(2,1)S(1)}, bf16[64,4096]{1,0:T(8,128)(2,1)S(1)}, u32[]{:S(2)}, u32[]{:S(2)}) collective-permute-start(bf16[64,4096]{1,0:T(8,128)(2,1)S(1)} %collective-permute-done.6.refs_0_.refs_7_), channel_id=1, source_target_pairs={{0,48},{4,20},{64,112},{68,84},{8,56},{12,28},{72,120},{76,92},{1,... | collective-permute-start | bytes 1572872 | tf_op jit(solution)/shard_map/ppermute | solution.py:79
  33.7 2.3 %collective-permute-done.10.refs_0_.refs_5_ = bf16[64,4096]{1,0:T(8,128)(2,1)S(1)} collective-permute-done((bf16[64,4096]{1,0:T(8,128)(2,1)S(1)}, bf16[64,4096]{1,0:T(8,128)(2,1)S(1)}, u32[]{:S(2)}, u32[]{:S(2)}) %collective-permute-start.10) | collective-permute-done | bytes 524320 | tf_op jit(solution)/shard_map/ppermute | solution.py:79
  36.0 2.3 %shard_map.78 = (bf16[256,512]{1,0:T(8,128)(2,1)S(1)}, bf16[256,512]{1,0:T(8,128)(2,1)S(1)}) custom-call(bf16[64,4096]{1,0:T(8,128)(2,1)S(1)} %collective-permute-done.6.refs_0_.refs_7_, bf16[64,4096]{1,0:T(8,128)(2,1)S(1)} %collective-permute-done.7.refs_1_.refs_15_, bf16[64,4096]{1,0:T(8,128)(2,1)S(1)} %collective-permute-done.8.refs_2_.refs_8_, ...), custom_call_target="tpu_custom_call" | custom-call | flops 1000 | bytes 1000 | tf_op jit(solution)/shard_map/pallas_call | solution.py:31
  38.4 3.3 %collective-permute-done.12.refs_2_.refs_9_ = bf16[64,4096]{1,0:T(8,128)(2,1)S(1)} collective-permute-done((bf16[64,4096]{1,0:T(8,128)(2,1)S(1)}, bf16[64,4096]{1,0:T(8,128)(2,1)S(1)}, u32[]{:S(2)}, u32[]{:S(2)}) %collective-permute-start.12) | collective-permute-done | bytes 524320 | tf_op jit(solution)/shard_map/ppermute | solution.py:79
  41.7 1.9 %collective-permute-done.13.refs_3_.refs_17_ = bf16[64,4096]{1,0:T(8,128)(2,1)S(1)} collective-permute-done((bf16[64,4096]{1,0:T(8,128)(2,1)S(1)}, bf16[64,4096]{1,0:T(8,128)(2,1)S(1)}, u32[]{:S(2)}, u32[]{:S(2)}) %collective-permute-start.13) | collective-permute-done | bytes 524320 | tf_op jit(solution)/shard_map/ppermute | solution.py:79
  43.6 2.3 %shard_map.79 = (bf16[256,512]{1,0:T(8,128)(2,1)S(1)}, bf16[256,512]{1,0:T(8,128)(2,1)S(1)}) custom-call(bf16[64,4096]{1,0:T(8,128)(2,1)S(1)} %collective-permute-done.10.refs_0_.refs_5_, bf16[64,4096]{1,0:T(8,128)(2,1)S(1)} %collective-permute-done.11.refs_1_.refs_13_, bf16[64,4096]{1,0:T(8,128)(2,1)S(1)} %collective-permute-done.12.refs_2_.refs_9_, ...), custom_call_target="tpu_custom_call" | custom-call | flops 1000 | bytes 1000 | tf_op jit(solution)/shard_map/pallas_call | solution.py:31
  45.9 6.0 %shard_map.80 = (bf16[1,1,512,512]{3,2,1,0:T(8,128)(2,1)}, bf16[1,1,512,512]{3,2,1,0:T(8,128)(2,1)}, bf16[1024,512]{1,0:T(8,128)(2,1)S(1)}, bf16[1024,512]{1,0:T...) custom-call(bf16[1,1,512,512]{3,2,1,0:T(8,128)(2,1)S(1)} %get-tuple-element.39.refs_0_, ...), custom_call_target="tpu_custom_call" | custom-call | flops 1000 | bytes 1000 | tf_op jit(solution)/shard_map/pallas_call | solution.py:31
  51.9 2.4 %shard_map.81.refs_18_ = bf16[512,2048]{1,0:T(8,128)(2,1)S(1)} custom-call(bf16[1024,512]{1,0:T(8,128)(2,1)S(1)} %get-tuple-element.57.refs_0_, bf16[1024,512]{1,0:T(8,128)(2,1)S(1)} %get-tuple-element.58.refs_1_, bf16[1,2,4096,512]{3,2,1,0:T(8,128)(2,1)S(1)} %get-tuple-element.43.refs_4_.refs_2_), custom_call_target="tpu_custom_call" | custom-call | flops 1000 | bytes 1000 | tf_op jit(solution)/shard_map/pallas_call | solution.py:31
  54.4 2.4 %shard_map.82.refs_19_ = bf16[512,2048]{1,0:T(8,128)(2,1)S(1)} custom-call(bf16[1024,512]{1,0:T(8,128)(2,1)S(1)} %get-tuple-element.57.refs_0_, bf16[1024,512]{1,0:T(8,128)(2,1)S(1)} %get-tuple-element.58.refs_1_, bf16[1,2,4096,512]{3,2,1,0:T(8,128)(2,1)S(1)} %get-tuple-element.43.refs_4_.refs_2_), custom_call_target="tpu_custom_call" | custom-call | flops 1000 | bytes 1000 | tf_op jit(solution)/shard_map/pallas_call | solution.py:31
  57.3 2.9 %shard_map.83.refs_4_ = bf16[512,2048]{1,0:T(8,128)(2,1)S(1)} custom-call(s32[4]{0:T(128)S(1)} %get-tuple-element.59.refs_0_, bf16[512,1024]{1,0:T(8,128)(2,1)S(1)} %get-tuple-element.60.refs_1_, bf16[64,4096]{1,0:T(8,128)(2,1)S(1)} %get-tuple-element.41.refs_0_.refs_2_, bf16[64,4096]{1,0:T(8,128)(2,1)S(1)} %collective-permute-done.2.refs_0_.refs_3_, ...), custom_call_target="tpu_custom_call" | custom-call | flops 1000 | bytes 1000 | tf_op jit(solution)/shard_map/pallas_call | solution.py:31
  60.2 1.9 %collective-permute-start.19 = (bf16[512,2048]{1,0:T(8,128)(2,1)S(1)}, bf16[512,2048]{1,0:T(8,128)(2,1)S(1)}, u32[]{:S(2)}, u32[]{:S(2)}) collective-permute-start(bf16[512,2048]{1,0:T(8,128)(2,1)S(1)} %shard_map.83.refs_4_), channel_id=1, source_target_pairs={{0,1},{4,7},{64,65},{68,71},{8,9},{12,15},{72,73},{76,79},{1,0},{5... | collective-permute-start | bytes 6291464 | tf_op jit(solution)/shard_map/ppermute | solution.py:79
  62.1 2.4 %shard_map.84 = (bf16[256,2048]{1,0:T(8,128)(2,1)S(1)}, bf16[256,2048]{1,0:T(8,128)(2,1)S(1)}) custom-call(bf16[1024,512]{1,0:T(8,128)(2,1)S(1)} %get-tuple-element.57.refs_0_, bf16[1024,512]{1,0:T(8,128)(2,1)S(1)} %get-tuple-element.58.refs_1_, bf16[1,2,4096,512]{3,2,1,0:T(8,128)(2,1)S(1)} %get-tuple-element.43.refs_4_.refs_2_, ...), custom_call_target="tpu_custom_call" | custom-call | flops 1000 | bytes 1000 | tf_op jit(solution)/shard_map/pallas_call | solution.py:31
  64.6 2.4 %shard_map.85 = (bf16[256,2048]{1,0:T(8,128)(2,1)S(1)}, bf16[256,2048]{1,0:T(8,128)(2,1)S(1)}) custom-call(bf16[1024,512]{1,0:T(8,128)(2,1)S(1)} %get-tuple-element.57.refs_0_, bf16[1024,512]{1,0:T(8,128)(2,1)S(1)} %get-tuple-element.58.refs_1_, bf16[1,2,4096,512]{3,2,1,0:T(8,128)(2,1)S(1)} %get-tuple-element.43.refs_4_.refs_2_, ...), custom_call_target="tpu_custom_call" | custom-call | flops 1000 | bytes 1000 | tf_op jit(solution)/shard_map/pallas_call | solution.py:31
  66.9 2.1 %collective-permute-start.22 = (bf16[256,2048]{1,0:T(8,128)(2,1)S(1)}, bf16[256,2048]{1,0:T(8,128)(2,1)S(1)}, u32[]{:S(2)}, u32[]{:S(2)}) collective-permute-start(bf16[256,2048]{1,0:T(8,128)(2,1)S(1)} %get-tuple-element.65.refs_19_), channel_id=1, source_target_pairs={{0,16},{4,52},{64,80},{68,116},{8,24},{12,60},{72,88},{76,124},{1,... | collective-permute-start | bytes 3145736 | tf_op jit(solution)/shard_map/ppermute | solution.py:79
  69.0 2.9 %shard_map.86.refs_18_ = bf16[512,2048]{1,0:T(8,128)(2,1)S(1)} custom-call(s32[4]{0:T(128)S(1)} %get-tuple-element.59.refs_0_, bf16[512,1024]{1,0:T(8,128)(2,1)S(1)} %get-tuple-element.63.refs_1_, bf16[64,4096]{1,0:T(8,128)(2,1)S(1)} %get-tuple-element.41.refs_0_.refs_2_, bf16[64,4096]{1,0:T(8,128)(2,1)S(1)} %collective-permute-done.2.refs_0_.refs_3_, ...), custom_call_target="tpu_custom_call" | custom-call | flops 1000 | bytes 1000 | tf_op jit(solution)/shard_map/pallas_call | solution.py:31
  71.9 2.9 %shard_map.87.refs_18_.keep = bf16[512,2048]{1,0:T(8,128)(2,1)S(1)} custom-call(s32[4]{0:T(128)S(1)} %get-tuple-element.62.refs_0_, bf16[512,1024]{1,0:T(8,128)(2,1)S(1)} %get-tuple-element.60.refs_1_, bf16[64,4096]{1,0:T(8,128)(2,1)S(1)} %get-tuple-element.41.refs_0_.refs_2_, bf16[64,4096]{1,0:T(8,128)(2,1)S(1)} %collective-permute-done.2.refs_0_.refs_3_, ...), custom_call_target="tpu_custom_call" | custom-call | flops 1000 | bytes 1000 | tf_op jit(solution)/shard_map/pallas_call | solution.py:31
  74.8 11.7 %collective-permute-done.19.first = bf16[512,2048]{1,0:T(8,128)(2,1)S(1)} collective-permute-done((bf16[512,2048]{1,0:T(8,128)(2,1)S(1)}, bf16[512,2048]{1,0:T(8,128)(2,1)S(1)}, u32[]{:S(2)}, u32[]{:S(2)}) %collective-permute-start.19) | collective-permute-done | bytes 2097184 | tf_op jit(solution)/shard_map/ppermute | solution.py:79
  86.5 1.6 %collective-permute-start.20 = (bf16[512,2048]{1,0:T(8,128)(2,1)S(1)}, bf16[512,2048]{1,0:T(8,128)(2,1)S(1)}, u32[]{:S(2)}, u32[]{:S(2)}) collective-permute-start(bf16[512,2048]{1,0:T(8,128)(2,1)S(1)} %shard_map.86.refs_18_), channel_id=1, source_target_pairs={{0,1},{4,7},{64,65},{68,71},{8,9},{12,15},{72,73},{76,79},{1,0},{5... | collective-permute-start | bytes 6291464 | tf_op jit(solution)/shard_map/ppermute | solution.py:79
  88.1 2.9 %shard_map.88.keep = bf16[512,2048]{1,0:T(8,128)(2,1)S(1)} custom-call(s32[4]{0:T(128)S(1)} %get-tuple-element.62.refs_0_, bf16[512,1024]{1,0:T(8,128)(2,1)S(1)} %get-tuple-element.63.refs_1_, bf16[64,4096]{1,0:T(8,128)(2,1)S(1)} %get-tuple-element.41.refs_0_.refs_2_, bf16[64,4096]{1,0:T(8,128)(2,1)S(1)} %collective-permute-done.2.refs_0_.refs_3_, ...), custom_call_target="tpu_custom_call" | custom-call | flops 1000 | bytes 1000 | tf_op jit(solution)/shard_map/pallas_call | solution.py:31
  91.5 2.5 %collective-permute-start.17 = (bf16[128,2048]{1,0:T(8,128)(2,1)S(1)}, bf16[128,2048]{1,0:T(8,128)(2,1)S(1)}, u32[]{:S(2)}, u32[]{:S(2)}) collective-permute-start(bf16[128,2048]{1,0:T(8,128)(2,1)S(1)} %slice.81), channel_id=1, source_target_pairs={{0,48},{4,20},{64,112},{68,84},{8,56},{12,28},{72,120},{76,92},{1,... | collective-permute-start | bytes 1572872 | tf_op jit(solution)/shard_map/ppermute | solution.py:79
  94.4 0.9 collective-permute-start.23
  95.7 6.2 %collective-permute-done.17 = bf16[128,2048]{1,0:T(8,128)(2,1)S(1)} collective-permute-done((bf16[128,2048]{1,0:T(8,128)(2,1)S(1)}, bf16[128,2048]{1,0:T(8,128)(2,1)S(1)}, u32[]{:S(2)}, u32[]{:S(2)}) %collective-permute-start.17) | collective-permute-done | bytes 524320 | tf_op jit(solution)/shard_map/ppermute | solution.py:79
  102.1 2.4 %collective-permute-start.18 = (bf16[64,2048]{1,0:T(8,128)(2,1)S(1)}, bf16[64,2048]{1,0:T(8,128)(2,1)S(1)}, u32[]{:S(2)}, u32[]{:S(2)}) collective-permute-start(bf16[64,2048]{1,0:T(8,128)(2,1)S(1)} %slice.83), channel_id=1, source_target_pairs={{0,72},{4,68},{64,0},{68,12},{8,64},{12,76},{72,8},{76,4},{1,73},{... | collective-permute-start | bytes 786440 | tf_op jit(solution)/shard_map/ppermute | solution.py:79
  104.5 3.0 %collective-permute-done.23 = bf16[128,2048]{1,0:T(8,128)(2,1)S(1)} collective-permute-done((bf16[128,2048]{1,0:T(8,128)(2,1)S(1)}, bf16[128,2048]{1,0:T(8,128)(2,1)S(1)}, u32[]{:S(2)}, u32[]{:S(2)}) %collective-permute-start.23) | collective-permute-done | bytes 524320 | tf_op jit(solution)/shard_map/ppermute | solution.py:79
  107.7 2.4 %collective-permute-start.24 = (bf16[64,2048]{1,0:T(8,128)(2,1)S(1)}, bf16[64,2048]{1,0:T(8,128)(2,1)S(1)}, u32[]{:S(2)}, u32[]{:S(2)}) collective-permute-start(bf16[64,2048]{1,0:T(8,128)(2,1)S(1)} %slice.82), channel_id=1, source_target_pairs={{0,72},{4,68},{64,0},{68,12},{8,64},{12,76},{72,8},{76,4},{1,73},{... | collective-permute-start | bytes 786440 | tf_op jit(solution)/shard_map/ppermute | solution.py:79
  110.2 1.8 %collective-permute-start.21 = (bf16[64,2048]{1,0:T(8,128)(2,1)S(1)}, bf16[64,2048]{1,0:T(8,128)(2,1)S(1)}, u32[]{:S(2)}, u32[]{:S(2)}) collective-permute-start(bf16[64,2048]{1,0:T(8,128)(2,1)S(1)} %fusion.1), channel_id=1, source_target_pairs={{0,8},{4,12},{64,72},{68,76},{8,0},{12,4},{72,64},{76,68},{1,9},{5... | collective-permute-start | bytes 786440 | tf_op jit(solution)/shard_map/ppermute | solution.py:79
  112.6 3.0 %collective-permute-start.27 = (bf16[512,1024]{1,0:T(8,128)(2,1)S(1)}, bf16[512,1024]{1,0:T(8,128)(2,1)S(1)}, u32[]{:S(2)}, u32[]{:S(2)}) collective-permute-start(bf16[512,1024]{1,0:T(8,128)(2,1)S(1)} %add_convert_fusion), channel_id=1, source_target_pairs={{0,3},{4,5},{64,67},{68,69},{8,11},{12,13},{72,75},{76,77},{1,2},{... | collective-permute-start | bytes 3145736 | tf_op jit(solution)/shard_map/ppermute | solution.py:79
  115.6 6.6 %collective-permute-done.24 = bf16[64,2048]{1,0:T(8,128)(2,1)S(1)} collective-permute-done((bf16[64,2048]{1,0:T(8,128)(2,1)S(1)}, bf16[64,2048]{1,0:T(8,128)(2,1)S(1)}, u32[]{:S(2)}, u32[]{:S(2)}) %collective-permute-start.24) | collective-permute-done | bytes 262176 | tf_op jit(solution)/shard_map/ppermute | solution.py:79
  123.1 5.5 %collective-permute-done.27.second = bf16[512,1024]{1,0:T(8,128)(2,1)S(1)} collective-permute-done((bf16[512,1024]{1,0:T(8,128)(2,1)S(1)}, bf16[512,1024]{1,0:T(8,128)(2,1)S(1)}, u32[]{:S(2)}, u32[]{:S(2)}) %collective-permute-start.27) | collective-permute-done | bytes 1048608 | tf_op jit(solution)/shard_map/ppermute | solution.py:79
  128.6 3.0 %collective-permute-start.28 = (bf16[512,1024]{1,0:T(8,128)(2,1)S(1)}, bf16[512,1024]{1,0:T(8,128)(2,1)S(1)}, u32[]{:S(2)}, u32[]{:S(2)}) collective-permute-start(bf16[512,1024]{1,0:T(8,128)(2,1)S(1)} %add_convert_fusion.1), channel_id=1, source_target_pairs={{0,3},{4,5},{64,67},{68,69},{8,11},{12,13},{72,75},{76,77},{1,2},{... | collective-permute-start | bytes 3145736 | tf_op jit(solution)/shard_map/ppermute | solution.py:79
  131.8 1.9 %collective-permute-done.26.theirs = bf16[64,4096]{1,0:T(8,128)(2,1)S(1)} collective-permute-done((bf16[64,4096]{1,0:T(8,128)(2,1)S(1)}, bf16[64,4096]{1,0:T(8,128)(2,1)S(1)}, u32[]{:S(2)}, u32[]{:S(2)}) %collective-permute-start.26) | collective-permute-done | bytes 524320 | tf_op jit(solution)/shard_map/ppermute | solution.py:79
  133.7 1.0 shard_map.89
  134.7 1.8 %shard_map.90.refs_0_ = bf16[1,2,1024,512]{3,2,1,0:T(8,128)(2,1)} custom-call(bf16[512,2048]{1,0:T(8,128)(2,1)S(1)} %shard_map.87.refs_18_.keep, bf16[512,2048]{1,0:T(8,128)(2,1)S(1)} %collective-permute-done.19.first, bf16[512,1024]{1,0:T(8,128)(2,1)S(1)} %collective-permute-done.27.second), custom_call_target="tpu_custom_call" | custom-call | flops 1000 | bytes 1000 | tf_op jit(solution)/shard_map/pallas_call | solution.py:205
  136.5 8.1 %collective-permute-done.28.second = bf16[512,1024]{1,0:T(8,128)(2,1)S(1)} collective-permute-done((bf16[512,1024]{1,0:T(8,128)(2,1)S(1)}, bf16[512,1024]{1,0:T(8,128)(2,1)S(1)}, u32[]{:S(2)}, u32[]{:S(2)}) %collective-permute-start.28) | collective-permute-done | bytes 1048608 | tf_op jit(solution)/shard_map/ppermute | solution.py:79
  144.6 1.8 %shard_map.91 = bf16[1,2,1024,512]{3,2,1,0:T(8,128)(2,1)} custom-call(bf16[512,2048]{1,0:T(8,128)(2,1)S(1)} %shard_map.88.keep, bf16[512,2048]{1,0:T(8,128)(2,1)S(1)} %collective-permute-done.20.first, bf16[512,1024]{1,0:T(8,128)(2,1)S(1)} %collective-permute-done.28.second, bf16[1,2,1024,512]{3,2,1,0:T(8,128)(2,1)} %shard_map.90.refs_0_), custom_call_target="tpu_custom_call", output_to_operand_aliasing={{}: (3, {})} | custom-call | flops 1000 | bytes 1000 | tf_op jit(solution)/shard_map/pallas_call | solution.py:205
  (50 shorter events, 6.1 us)
Async XLA Ops:
  0.6 6.5 %copy-start.1 = (bf16[1,1,512,512]{3,2,1,0:T(8,128)(2,1)S(1)}, bf16[1,1,512,512]{3,2,1,0:T(8,128)(2,1)}, u32[]{:S(2)}) copy-start(bf16[1,1,512,512]{3,2,1,0:T(8,128)(2,1)} %refs_1_.1) | copy-start | bytes 1572868
  0.6 6.5 %copy-start.2 = (bf16[1,1,512,512]{3,2,1,0:T(8,128)(2,1)S(1)}, bf16[1,1,512,512]{3,2,1,0:T(8,128)(2,1)}, u32[]{:S(2)}) copy-start(bf16[1,1,512,512]{3,2,1,0:T(8,128)(2,1)} %refs_2_.1) | copy-start | bytes 1572868
  2.2 11.3 %collective-permute-start.2 = (bf16[64,4096]{1,0:T(8,128)(2,1)S(1)}, bf16[64,4096]{1,0:T(8,128)(2,1)S(1)}, u32[]{:S(2)}, u32[]{:S(2)}) collective-permute-start(bf16[64,4096]{1,0:T(8,128)(2,1)S(1)} %get-tuple-element.41.refs_0_.refs_2_), channel_id=1, source_target_pairs={{0,64},{4,76},{64,8},{68,4},{8,72},{12,68},{72,0},{76,12},{1,65},{... | collective-permute-start | bytes 1572872 | tf_op jit(solution)/shard_map/ppermute | solution.py:79
  4.2 14.0 %collective-permute-start.4 = (bf16[64,4096]{1,0:T(8,128)(2,1)S(1)}, bf16[64,4096]{1,0:T(8,128)(2,1)S(1)}, u32[]{:S(2)}, u32[]{:S(2)}) collective-permute-start(bf16[64,4096]{1,0:T(8,128)(2,1)S(1)} %get-tuple-element.41.refs_0_.refs_2_), channel_id=1, source_target_pairs={{0,48},{4,20},{64,112},{68,84},{8,56},{12,28},{72,120},{76,92},{1,... | collective-permute-start | bytes 1572872 | tf_op jit(solution)/shard_map/ppermute | solution.py:79
  6.9 12.7 %collective-permute-start = (bf16[64,4096]{1,0:T(8,128)(2,1)S(1)}, bf16[64,4096]{1,0:T(8,128)(2,1)S(1)}, u32[]{:S(2)}, u32[]{:S(2)}) collective-permute-start(bf16[64,4096]{1,0:T(8,128)(2,1)S(1)} %get-tuple-element.41.refs_0_.refs_2_), channel_id=1, source_target_pairs={{0,16},{4,52},{64,80},{68,116},{8,24},{12,60},{72,88},{76,124},{1,... | collective-permute-start | bytes 1572872 | tf_op jit(solution)/shard_map/ppermute | solution.py:79
  7.2 3.4 %copy-start = (bf16[1,2,4096,512]{3,2,1,0:T(8,128)(2,1)S(1)}, bf16[1,2,4096,512]{3,2,1,0:T(8,128)(2,1)}, u32[]{:S(2)}) copy-start(bf16[1,2,4096,512]{3,2,1,0:T(8,128)(2,1)} %refs_0_.1) | copy-start | bytes 25165828
  13.5 9.5 %collective-permute-start.3 = (bf16[64,4096]{1,0:T(8,128)(2,1)S(1)}, bf16[64,4096]{1,0:T(8,128)(2,1)S(1)}, u32[]{:S(2)}, u32[]{:S(2)}) collective-permute-start(bf16[64,4096]{1,0:T(8,128)(2,1)S(1)} %collective-permute-done.2.refs_0_.refs_3_), channel_id=1, source_target_pairs={{0,4},{4,0},{64,68},{68,64},{8,12},{12,8},{72,76},{76,72},{1,5},{5... | collective-permute-start | bytes 1572872 | tf_op jit(solution)/shard_map/ppermute | solution.py:79
  18.2 6.7 %collective-permute-start.5 = (bf16[64,4096]{1,0:T(8,128)(2,1)S(1)}, bf16[64,4096]{1,0:T(8,128)(2,1)S(1)}, u32[]{:S(2)}, u32[]{:S(2)}) collective-permute-start(bf16[64,4096]{1,0:T(8,128)(2,1)S(1)} %collective-permute-done.4.refs_2_.refs_4_), channel_id=1, source_target_pairs={{0,4},{4,0},{64,68},{68,64},{8,12},{12,8},{72,76},{76,72},{1,5},{5... | collective-permute-start | bytes 1572872 | tf_op jit(solution)/shard_map/ppermute | solution.py:79
  19.7 7.5 %collective-permute-start.1 = (bf16[64,4096]{1,0:T(8,128)(2,1)S(1)}, bf16[64,4096]{1,0:T(8,128)(2,1)S(1)}, u32[]{:S(2)}, u32[]{:S(2)}) collective-permute-start(bf16[64,4096]{1,0:T(8,128)(2,1)S(1)} %collective-permute-done.refs_2_.refs_6_), channel_id=1, source_target_pairs={{0,4},{4,0},{64,68},{68,64},{8,12},{12,8},{72,76},{76,72},{1,5},{5... | collective-permute-start | bytes 1572872 | tf_op jit(solution)/shard_map/ppermute | solution.py:79
  20.0 10.4 %collective-permute-start.6 = (bf16[64,4096]{1,0:T(8,128)(2,1)S(1)}, bf16[64,4096]{1,0:T(8,128)(2,1)S(1)}, u32[]{:S(2)}, u32[]{:S(2)}) collective-permute-start(bf16[64,4096]{1,0:T(8,128)(2,1)S(1)} %collective-permute-done.refs_2_.refs_6_), channel_id=1, source_target_pairs={{0,64},{4,76},{64,8},{68,4},{8,72},{12,68},{72,0},{76,12},{1,65},{... | collective-permute-start | bytes 1572872 | tf_op jit(solution)/shard_map/ppermute | solution.py:79
  20.9 10.4 %collective-permute-start.8 = (bf16[64,4096]{1,0:T(8,128)(2,1)S(1)}, bf16[64,4096]{1,0:T(8,128)(2,1)S(1)}, u32[]{:S(2)}, u32[]{:S(2)}) collective-permute-start(bf16[64,4096]{1,0:T(8,128)(2,1)S(1)} %collective-permute-done.refs_2_.refs_6_), channel_id=1, source_target_pairs={{0,48},{4,20},{64,112},{68,84},{8,56},{12,28},{72,120},{76,92},{1,... | collective-permute-start | bytes 1572872 | tf_op jit(solution)/shard_map/ppermute | solution.py:79
  23.0 13.0 %collective-permute-start.10 = (bf16[64,4096]{1,0:T(8,128)(2,1)S(1)}, bf16[64,4096]{1,0:T(8,128)(2,1)S(1)}, u32[]{:S(2)}, u32[]{:S(2)}) collective-permute-start(bf16[64,4096]{1,0:T(8,128)(2,1)S(1)} %collective-permute-done.4.refs_2_.refs_4_), channel_id=1, source_target_pairs={{0,64},{4,76},{64,8},{68,4},{8,72},{12,68},{72,0},{76,12},{1,65},{... | collective-permute-start | bytes 1572872 | tf_op jit(solution)/shard_map/ppermute | solution.py:79
  30.4 5.6 %collective-permute-start.7 = (bf16[64,4096]{1,0:T(8,128)(2,1)S(1)}, bf16[64,4096]{1,0:T(8,128)(2,1)S(1)}, u32[]{:S(2)}, u32[]{:S(2)}) collective-permute-start(bf16[64,4096]{1,0:T(8,128)(2,1)S(1)} %collective-permute-done.6.refs_0_.refs_7_), channel_id=1, source_target_pairs={{0,4},{4,0},{64,68},{68,64},{8,12},{12,8},{72,76},{76,72},{1,5},{5... | collective-permute-start | bytes 1572872 | tf_op jit(solution)/shard_map/ppermute | solution.py:79
  31.3 4.8 %collective-permute-start.9 = (bf16[64,4096]{1,0:T(8,128)(2,1)S(1)}, bf16[64,4096]{1,0:T(8,128)(2,1)S(1)}, u32[]{:S(2)}, u32[]{:S(2)}) collective-permute-start(bf16[64,4096]{1,0:T(8,128)(2,1)S(1)} %collective-permute-done.8.refs_2_.refs_8_), channel_id=1, source_target_pairs={{0,4},{4,0},{64,68},{68,64},{8,12},{12,8},{72,76},{76,72},{1,5},{5... | collective-permute-start | bytes 1572872 | tf_op jit(solution)/shard_map/ppermute | solution.py:79
  31.3 10.4 %collective-permute-start.12 = (bf16[64,4096]{1,0:T(8,128)(2,1)S(1)}, bf16[64,4096]{1,0:T(8,128)(2,1)S(1)}, u32[]{:S(2)}, u32[]{:S(2)}) collective-permute-start(bf16[64,4096]{1,0:T(8,128)(2,1)S(1)} %collective-permute-done.6.refs_0_.refs_7_), channel_id=1, source_target_pairs={{0,48},{4,20},{64,112},{68,84},{8,56},{12,28},{72,120},{76,92},{1,... | collective-permute-start | bytes 1572872 | tf_op jit(solution)/shard_map/ppermute | solution.py:79
  36.0 5.6 %collective-permute-start.11 = (bf16[64,4096]{1,0:T(8,128)(2,1)S(1)}, bf16[64,4096]{1,0:T(8,128)(2,1)S(1)}, u32[]{:S(2)}, u32[]{:S(2)}) collective-permute-start(bf16[64,4096]{1,0:T(8,128)(2,1)S(1)} %collective-permute-done.10.refs_0_.refs_5_), channel_id=1, source_target_pairs={{0,4},{4,0},{64,68},{68,64},{8,12},{12,8},{72,76},{76,72},{1,5},{5... | collective-permute-start | bytes 1572872 | tf_op jit(solution)/shard_map/ppermute | solution.py:79
  41.7 1.9 %collective-permute-start.13 = (bf16[64,4096]{1,0:T(8,128)(2,1)S(1)}, bf16[64,4096]{1,0:T(8,128)(2,1)S(1)}, u32[]{:S(2)}, u32[]{:S(2)}) collective-permute-start(bf16[64,4096]{1,0:T(8,128)(2,1)S(1)} %collective-permute-done.12.refs_2_.refs_9_), channel_id=1, source_target_pairs={{0,4},{4,0},{64,68},{68,64},{8,12},{12,8},{72,76},{76,72},{1,5},{5... | collective-permute-start | bytes 1572872 | tf_op jit(solution)/shard_map/ppermute | solution.py:79
  54.2 7.8 %collective-permute-start.14 = (bf16[512,2048]{1,0:T(8,128)(2,1)S(1)}, bf16[512,2048]{1,0:T(8,128)(2,1)S(1)}, u32[]{:S(2)}, u32[]{:S(2)}) collective-permute-start(bf16[512,2048]{1,0:T(8,128)(2,1)S(1)} %shard_map.81.refs_18_), channel_id=1, source_target_pairs={{0,4},{4,0},{64,68},{68,64},{8,12},{12,8},{72,76},{76,72},{1,5},{5... | collective-permute-start | bytes 6291464 | tf_op jit(solution)/shard_map/ppermute | solution.py:79
  56.8 7.7 %collective-permute-start.15 = (bf16[512,2048]{1,0:T(8,128)(2,1)S(1)}, bf16[512,2048]{1,0:T(8,128)(2,1)S(1)}, u32[]{:S(2)}, u32[]{:S(2)}) collective-permute-start(bf16[512,2048]{1,0:T(8,128)(2,1)S(1)} %shard_map.82.refs_19_), channel_id=1, source_target_pairs={{0,4},{4,0},{64,68},{68,64},{8,12},{12,8},{72,76},{76,72},{1,5},{5... | collective-permute-start | bytes 6291464 | tf_op jit(solution)/shard_map/ppermute | solution.py:79
  60.2 26.3 %collective-permute-start.19 = (bf16[512,2048]{1,0:T(8,128)(2,1)S(1)}, bf16[512,2048]{1,0:T(8,128)(2,1)S(1)}, u32[]{:S(2)}, u32[]{:S(2)}) collective-permute-start(bf16[512,2048]{1,0:T(8,128)(2,1)S(1)} %shard_map.83.refs_4_), channel_id=1, source_target_pairs={{0,1},{4,7},{64,65},{68,71},{8,9},{12,15},{72,73},{76,79},{1,0},{5... | collective-permute-start | bytes 6291464 | tf_op jit(solution)/shard_map/ppermute | solution.py:79
  64.4 26.6 %collective-permute-start.16 = (bf16[256,2048]{1,0:T(8,128)(2,1)S(1)}, bf16[256,2048]{1,0:T(8,128)(2,1)S(1)}, u32[]{:S(2)}, u32[]{:S(2)}) collective-permute-start(bf16[256,2048]{1,0:T(8,128)(2,1)S(1)} %get-tuple-element.64.refs_18_), channel_id=1, source_target_pairs={{0,16},{4,52},{64,80},{68,116},{8,24},{12,60},{72,88},{76,124},{1,... | collective-permute-start | bytes 3145736 | tf_op jit(solution)/shard_map/ppermute | solution.py:79
  66.9 27.0 %collective-permute-start.22 = (bf16[256,2048]{1,0:T(8,128)(2,1)S(1)}, bf16[256,2048]{1,0:T(8,128)(2,1)S(1)}, u32[]{:S(2)}, u32[]{:S(2)}) collective-permute-start(bf16[256,2048]{1,0:T(8,128)(2,1)S(1)} %get-tuple-element.65.refs_19_), channel_id=1, source_target_pairs={{0,16},{4,52},{64,80},{68,116},{8,24},{12,60},{72,88},{76,124},{1,... | collective-permute-start | bytes 3145736 | tf_op jit(solution)/shard_map/ppermute | solution.py:79
  86.5 26.0 %collective-permute-start.20 = (bf16[512,2048]{1,0:T(8,128)(2,1)S(1)}, bf16[512,2048]{1,0:T(8,128)(2,1)S(1)}, u32[]{:S(2)}, u32[]{:S(2)}) collective-permute-start(bf16[512,2048]{1,0:T(8,128)(2,1)S(1)} %shard_map.86.refs_18_), channel_id=1, source_target_pairs={{0,1},{4,7},{64,65},{68,71},{8,9},{12,15},{72,73},{76,79},{1,0},{5... | collective-permute-start | bytes 6291464 | tf_op jit(solution)/shard_map/ppermute | solution.py:79
  91.5 10.5 %collective-permute-start.17 = (bf16[128,2048]{1,0:T(8,128)(2,1)S(1)}, bf16[128,2048]{1,0:T(8,128)(2,1)S(1)}, u32[]{:S(2)}, u32[]{:S(2)}) collective-permute-start(bf16[128,2048]{1,0:T(8,128)(2,1)S(1)} %slice.81), channel_id=1, source_target_pairs={{0,48},{4,20},{64,112},{68,84},{8,56},{12,28},{72,120},{76,92},{1,... | collective-permute-start | bytes 1572872 | tf_op jit(solution)/shard_map/ppermute | solution.py:79
  94.4 13.2 %collective-permute-start.23 = (bf16[128,2048]{1,0:T(8,128)(2,1)S(1)}, bf16[128,2048]{1,0:T(8,128)(2,1)S(1)}, u32[]{:S(2)}, u32[]{:S(2)}) collective-permute-start(bf16[128,2048]{1,0:T(8,128)(2,1)S(1)} %slice.80), channel_id=1, source_target_pairs={{0,48},{4,20},{64,112},{68,84},{8,56},{12,28},{72,120},{76,92},{1,... | collective-permute-start | bytes 1572872 | tf_op jit(solution)/shard_map/ppermute | solution.py:79
  102.1 8.1 %collective-permute-start.18 = (bf16[64,2048]{1,0:T(8,128)(2,1)S(1)}, bf16[64,2048]{1,0:T(8,128)(2,1)S(1)}, u32[]{:S(2)}, u32[]{:S(2)}) collective-permute-start(bf16[64,2048]{1,0:T(8,128)(2,1)S(1)} %slice.83), channel_id=1, source_target_pairs={{0,72},{4,68},{64,0},{68,12},{8,64},{12,76},{72,8},{76,4},{1,73},{... | collective-permute-start | bytes 786440 | tf_op jit(solution)/shard_map/ppermute | solution.py:79
  107.7 14.5 %collective-permute-start.24 = (bf16[64,2048]{1,0:T(8,128)(2,1)S(1)}, bf16[64,2048]{1,0:T(8,128)(2,1)S(1)}, u32[]{:S(2)}, u32[]{:S(2)}) collective-permute-start(bf16[64,2048]{1,0:T(8,128)(2,1)S(1)} %slice.82), channel_id=1, source_target_pairs={{0,72},{4,68},{64,0},{68,12},{8,64},{12,76},{72,8},{76,4},{1,73},{... | collective-permute-start | bytes 786440 | tf_op jit(solution)/shard_map/ppermute | solution.py:79
  110.2 12.8 %collective-permute-start.21 = (bf16[64,2048]{1,0:T(8,128)(2,1)S(1)}, bf16[64,2048]{1,0:T(8,128)(2,1)S(1)}, u32[]{:S(2)}, u32[]{:S(2)}) collective-permute-start(bf16[64,2048]{1,0:T(8,128)(2,1)S(1)} %fusion.1), channel_id=1, source_target_pairs={{0,8},{4,12},{64,72},{68,76},{8,0},{12,4},{72,64},{76,68},{1,9},{5... | collective-permute-start | bytes 786440 | tf_op jit(solution)/shard_map/ppermute | solution.py:79
  112.6 16.0 %collective-permute-start.27 = (bf16[512,1024]{1,0:T(8,128)(2,1)S(1)}, bf16[512,1024]{1,0:T(8,128)(2,1)S(1)}, u32[]{:S(2)}, u32[]{:S(2)}) collective-permute-start(bf16[512,1024]{1,0:T(8,128)(2,1)S(1)} %add_convert_fusion), channel_id=1, source_target_pairs={{0,3},{4,5},{64,67},{68,69},{8,11},{12,13},{72,75},{76,77},{1,2},{... | collective-permute-start | bytes 3145736 | tf_op jit(solution)/shard_map/ppermute | solution.py:79
  122.2 9.4 %collective-permute-start.25 = (bf16[64,2048]{1,0:T(8,128)(2,1)S(1)}, bf16[64,2048]{1,0:T(8,128)(2,1)S(1)}, u32[]{:S(2)}, u32[]{:S(2)}) collective-permute-start(bf16[64,2048]{1,0:T(8,128)(2,1)S(1)} %fusion), channel_id=1, source_target_pairs={{0,8},{4,12},{64,72},{68,76},{8,0},{12,4},{72,64},{76,68},{1,9},{5... | collective-permute-start | bytes 786440 | tf_op jit(solution)/shard_map/ppermute | solution.py:79
  128.6 16.0 %collective-permute-start.28 = (bf16[512,1024]{1,0:T(8,128)(2,1)S(1)}, bf16[512,1024]{1,0:T(8,128)(2,1)S(1)}, u32[]{:S(2)}, u32[]{:S(2)}) collective-permute-start(bf16[512,1024]{1,0:T(8,128)(2,1)S(1)} %add_convert_fusion.1), channel_id=1, source_target_pairs={{0,3},{4,5},{64,67},{68,69},{8,11},{12,13},{72,75},{76,77},{1,2},{... | collective-permute-start | bytes 3145736 | tf_op jit(solution)/shard_map/ppermute | solution.py:79
  131.7 2.0 %collective-permute-start.26 = (bf16[64,4096]{1,0:T(8,128)(2,1)S(1)}, bf16[64,4096]{1,0:T(8,128)(2,1)S(1)}, u32[]{:S(2)}, u32[]{:S(2)}) collective-permute-start(bf16[64,4096]{1,0:T(8,128)(2,1)S(1)} %pad_maximum_fusion.mine), channel_id=1, source_target_pairs={{0,4},{4,0},{64,68},{68,64},{8,12},{12,8},{72,76},{76,72},{1,5},{5... | collective-permute-start | bytes 1572872 | tf_op jit(solution)/shard_map/ppermute | solution.py:79
where the time goes:
time: 147 us
  waiting for transfers between devices  61.3 us (42%)
  Pallas kernels  41.5 us (28%)
  starting transfers between devices  35.5 us (24%)
  local copies, waits for them, and re-layouts  4.95 us (3%)
  other arithmetic  2.1 us (1%)
    ppermute x29, waiting for transfers between devices, send(): return lax.ppermute(array, ALL, route)  61.3 us
    pallas_call x13, Pallas kernels, call(): pl.pallas_call(reads, in_specs=[SCALARS] * index + [WHOLE] * (count - ind...  36.3 us
    ppermute x29, starting transfers between devices, send(): return lax.ppermute(array, ALL, route)  35.5 us
    pallas_call x2, Pallas kernels, share(): pl.pallas_call(functools.partial(share_body, part), in_specs=[pl.BlockSpe...  3.54 us
    unnamed x6, local copies, waits for them, and re-layouts  3.39 us
  transfers between devices with their start and end apart: 29, of which 16 were waited for; matrix products, arithmetic and copies ran while one was open for 2% of the time, Pallas kernels for 20%

commit v1 on v0

--- a/solution.py
+++ b/solution.py
@@ -102,7 +102,33 @@
     )
 
 
-def attend_body(q, g, k0, k1, k2, k3, v0, v1, v2, v3, att, dq, kg, vg, kgt, vgt, low, dlow):
+def forward_body(q, g, k0, k1, k2, k3, v0, v1, v2, v3, att, probs_out, vg, vgt, low):
+    scale = HEAD_DIM ** (-0.5)
+    total = q.shape[2]
+    chunk = total // 2
+    for head in range(q.shape[3] // HEAD_DIM):
+        cols = slice(head * HEAD_DIM, (head + 1) * HEAD_DIM)
+        k = arrange([ref[:, cols] for ref in (k0, k1, k2, k3)])
+        v = arrange([ref[:, cols] for ref in (v0, v1, v2, v3)])
+        for part in range(2):
+            rows = slice(part * chunk, (part + 1) * chunk)
+            scores = scale * lax.dot_general(
+                q[0, 0, rows, cols], k, NT, preferred_element_type=F32
+            )
+            expd = jnp.exp(scores - jnp.max(scores, axis=-1, keepdims=True))
+            probs = expd * (1.0 / jnp.sum(expd, axis=-1, keepdims=True))
+            probs_out[head, rows, :] = probs
+            probs_low = probs.astype(BF16)
+            low[head, rows, :] = probs_low
+            att[0, 0, rows, cols] = jnp.dot(
+                probs_low, v, preferred_element_type=F32
+            ).astype(BF16)
+        value_t = lax.dot_general(g[0, 0, :, cols], low[head], TN, preferred_element_type=F32)
+        vgt[cols, :] = value_t.astype(BF16)
+        vg[:, cols] = value_t.T.astype(BF16)
+
+
+def backward_body(q, g, k0, k1, k2, k3, v0, v1, v2, v3, att, probs, dq, kg, kgt, dlow):
     scale = HEAD_DIM ** (-0.5)
     total = q.shape[2]
     chunk = total // 2
@@ -113,25 +139,15 @@
         for part in range(2):
             rows = slice(part * chunk, (part + 1) * chunk)
             g_rows = g[0, 0, rows, cols]
-            scores = scale * lax.dot_general(
-                q[0, 0, rows, cols], k, NT, preferred_element_type=F32
+            dprobs = lax.dot_general(g_rows, v, NT, preferred_element_type=F32)
+            delta = jnp.sum(
+                g_rows.astype(F32) * att[0, 0, rows, cols].astype(F32), axis=-1, keepdims=True
             )
-            expd = jnp.exp(scores - jnp.max(scores, axis=-1, keepdims=True))
-            probs = expd * (1.0 / jnp.sum(expd, axis=-1, keepdims=True))
-            probs_low = probs.astype(BF16)
-            low[head, rows, :] = probs_low
-            out = jnp.dot(probs_low, v, preferred_element_type=F32).astype(BF16)
-            att[0, 0, rows, cols] = out
-            dprobs = lax.dot_general(g_rows, v, NT, preferred_element_type=F32)
-            delta = jnp.sum(g_rows.astype(F32) * out.astype(F32), axis=-1, keepdims=True)
-            ds_low = (probs * (dprobs - delta)).astype(BF16)
+            ds_low = (probs[head, rows, :] * (dprobs - delta)).astype(BF16)
             dlow[head, rows, :] = ds_low
             dq[0, 0, rows, cols] = (
                 scale * jnp.dot(ds_low, k, preferred_element_type=F32)
             ).astype(BF16)
-        value_t = lax.dot_general(g[0, 0, :, cols], low[head], TN, preferred_element_type=F32)
-        vgt[cols, :] = value_t.astype(BF16)
-        vg[:, cols] = value_t.T.astype(BF16)
         key_t = scale * lax.dot_general(
             q[0, 0, :, cols], dlow[head], TN, preferred_element_type=F32
         )
@@ -139,16 +155,33 @@
         kg[:, cols] = key_t.T.astype(BF16)
 
 
-def attend(queries, cotangent, keys, values):
+def forward(queries, cotangent, keys, values):
     _, _, total, width = queries.shape
-    span = 4 * keys[0].shape[0]
-    same = bf16(*queries.shape)
+    span, heads = 4 * keys[0].shape[0], width // HEAD_DIM
     return call(
-        attend_body,
+        forward_body,
         [queries, cotangent, *keys, *values],
-        [same, same, bf16(span, width), bf16(span, width), bf16(width, span), bf16(width, span)],
-        [pltpu.VMEM((width // HEAD_DIM, total, span), BF16)] * 2,
-        room=16,
+        [
+            bf16(*queries.shape),
+            jax.ShapeDtypeStruct((heads, total, span), F32),
+            bf16(span, width),
+            bf16(width, span),
+        ],
+        [pltpu.VMEM((heads, total, span), BF16)],
+        room=12,
+    )
+
+
+def backward(queries, cotangent, keys, values, attended, probs, after):
+    _, _, total, width = queries.shape
+    span, heads = 4 * keys[0].shape[0], width // HEAD_DIM
+    return call(
+        backward_body,
+        [queries, cotangent, *keys, *values, attended, probs],
+        [bf16(*queries.shape), bf16(span, width), bf16(width, span)],
+        [pltpu.VMEM((heads, total, span), BF16)],
+        after=after,
+        room=12,
     )
 
 
@@ -218,31 +251,32 @@
     )(keep, first, second, *given)
 
 
-def place_body(core, mine, theirs, out, sems):
-    half = mine.shape[0]
+def place_body(core, *refs):
+    parts, out, sems = refs[:4], refs[4], refs[5]
+    half, span = parts[0].shape
     low = pl.multiple_of(core[0] * half, half)
     high = pl.multiple_of((1 - core[0]) * half, half)
-    copies = [
-        pltpu.make_async_copy(mine, out.at[0, pl.ds(low, half), :], sems.at[0]),
-        pltpu.make_async_copy(theirs, out.at[0, pl.ds(high, half), :], sems.at[1]),
-    ]
-    for copy in copies:
-        copy.start()
+    copies = []
+    for i, part in enumerate(parts):
+        rows = pl.ds(low if i < 2 else high, half)
+        cols = slice(i % 2 * span, (i % 2 + 1) * span)
+        copies.append(pltpu.make_async_copy(part, out.at[0, rows, cols], sems.at[i]))
+        copies[-1].start()
     for copy in copies:
         copy.wait()
 
 
 def place(core, mine, theirs):
-    half, depth = mine.shape
+    half, span = mine[0].shape
     return pl.pallas_call(
         place_body,
-        in_specs=[SCALARS, WHOLE, WHOLE],
+        in_specs=[SCALARS] + [WHOLE] * 4,
         out_specs=pl.BlockSpec(memory_space=pl.ANY),
-        out_shape=bf16(1, 2 * half, depth),
-        scratch_shapes=[pltpu.SemaphoreType.DMA((2,))],
+        out_shape=bf16(1, 2 * half, 2 * span),
+        scratch_shapes=[pltpu.SemaphoreType.DMA((4,))],
         compiler_params=pltpu.CompilerParams(vmem_limit_bytes=4 * 1024 * 1024),
         cost_estimate=LITTLE,
-    )(core[None], mine, theirs)
+    )(core[None], *mine, *theirs)
 
 
 def load_body(*refs):
@@ -270,9 +304,9 @@
 
 
 def encoder_body(low, left, kg, vg, w, *refs):
-    outs = refs[-1:] if len(refs) == 1 else refs[-2:]
-    rows = slice(low, low + kg.shape[0] // 2)
+    moved, outs = refs[:-2], refs[-2:]
     half = outs[0].shape[0]
+    rows = slice(low, low + 2 * half)
     for i in range(outs[0].shape[1] // TILE):
         cols = slice(i * TILE, (i + 1) * TILE)
         from_w = slice(left + i * TILE, left + (i + 1) * TILE)
@@ -280,18 +314,19 @@
         total = total + lax.dot_general(
             vg[rows, :], w[0, 1, from_w, :], NT, preferred_element_type=F32
         )
-        if len(refs) > 1:
-            total = total + refs[0][:, cols].astype(F32)
         for j, out in enumerate(outs):
-            out[:, cols] = total[j * half : (j + 1) * half].astype(BF16)
-
-
-def encoder_part(key_grad, value_grad, kv_weight, side, columns, moved=None, after=()):
-    rows, depth = key_grad.shape[0] // 2, kv_weight.shape[2] // 2
+            part = total[j * half : (j + 1) * half]
+            if moved:
+                part = part + moved[j][:, cols].astype(F32)
+            out[:, cols] = part.astype(BF16)
+
+
+def encoder_part(key_grad, value_grad, kv_weight, side, columns, moved=(), after=()):
+    rows, depth = key_grad.shape[0] // 4, kv_weight.shape[2] // 2
     return call(
-        functools.partial(encoder_body, side * rows, columns * depth),
-        [key_grad, value_grad, kv_weight] + ([] if moved is None else [moved]),
-        bf16(rows, depth) if moved is None else [bf16(rows // 2, depth)] * 2,
+        functools.partial(encoder_body, 2 * side * rows, columns * depth),
+        [key_grad, value_grad, kv_weight, *moved],
+        [bf16(rows, depth)] * 2,
         after=after,
         room=12,
     )
@@ -348,16 +383,14 @@
     pieces = [{"h": h, "g": g}[name[0]][name[1]] for name in order]
     pieces += [{"h": h_too, "g": g_too}[name[0]][name[1]] for name in order]
 
-    attended, query_grad, key_grad, value_grad, key_grad_t, value_grad_t = attend(
-        queries, cotangent, keys, values
-    )
+    inputs = (queries, cotangent, keys, values)
+    attended, probs, value_grad, value_grad_t = forward(*inputs)
+    value_out = weight_part(go, value_grad_t, pieces)
+    query_grad, key_grad, key_grad_t = backward(*inputs, attended, probs, (value_out,))
 
     grads = (key_grad, value_grad, kv_weight)
-    moved = [encoder_part(*grads, 1, i) for i in range(2)]
-    value_out = weight_part(go, value_grad_t, pieces, moved)
-    moved = [send(part, SWAP) for part in moved]
-    early = (value_out,)
-    kept, x_out = zip(*[encoder_part(*grads, 0, i, moved[i], early) for i in range(2)])
+    moved = [[send(part, SWAP) for part in encoder_part(*grads, 1, i)] for i in range(2)]
+    kept, x_out = zip(*[encoder_part(*grads, 0, i, moved[i]) for i in range(2)])
     key_out = weight_part(go, key_grad_t, pieces, x_out)
     value_keep = weight_part(stay, value_grad_t, pieces, (key_out,))
     key_keep = weight_part(stay, key_grad_t, pieces, (value_keep,))
@@ -381,8 +414,7 @@
         here = here.astype(BF16)
         came = send(here, ACROSS_Z)
         last.append((tie(here, key_in).astype(F32) + came.astype(F32)).astype(BF16))
-    last = jnp.concatenate(last, 1)
-    enc_grad = place(core, last, send(last, SWAP))
+    enc_grad = place(core, last, [send(part, SWAP) for part in last])
 
     weight_grad = share(1, value_keep, value_in, value_two)
     weight_grad = share(0, key_keep, key_in, key_two, weight_grad)

time: 147 us -> 146 us (level)
  waiting for transfers between devices: 61.3 us -> 58.9 us
    ppermute x29 -> x32, waiting for transfers between devices: 61.3 us -> 58.9 us  [send(): return lax.ppermute(array, ALL, route)]
    ppermute x29 -> x32, starting transfers between devices: 35.5 us -> 36.9 us  [send(): return lax.ppermute(array, ALL, route)]
    pallas_call x13 -> x14, Pallas kernels: 36.3 us -> 36.5 us  [call(): pl.pallas_call(reads, in_specs=[SCALARS] * index + [WHOLE] * (count - ind...]
    unnamed x6 -> x8, local copies, waits for them, and re-layouts: 3.39 us -> 3.39 us
  transfers between devices with their start and end apart: 29 -> 32, of which waited for: 16 -> 18; matrix products, arithmetic and copies ran while one was open for 2% -> 1% of each run, Pallas kernels for 20% -> 21%
where the time goes in v1:
time: 146 us
  waiting for transfers between devices  58.9 us (40%)
  Pallas kernels  41.7 us (29%)
  starting transfers between devices  36.9 us (25%)
  local copies, waits for them, and re-layouts  4.95 us (3%)
  other arithmetic  2.01 us (1%)
    ppermute x32, waiting for transfers between devices, send(): return lax.ppermute(array, ALL, route)  58.9 us
    ppermute x32, starting transfers between devices, send(): return lax.ppermute(array, ALL, route)  36.9 us
    pallas_call x14, Pallas kernels, call(): pl.pallas_call(reads, in_specs=[SCALARS] * index + [WHOLE] * (count - ind...  36.5 us
    pallas_call x2, Pallas kernels, share(): pl.pallas_call(functools.partial(share_body, part), in_specs=[pl.BlockSpe...  3.54 us
    unnamed x8, local copies, waits for them, and re-layouts  3.39 us
  transfers between devices with their start and end apart: 32, of which 18 were waited for; matrix products, arithmetic and copies ran while one was open for 1% of the time, Pallas kernels for 21%

profile of v1, /device:TPU:0, one launch (start us, length us, event | category | flops | bytes accessed | tf_op | source)
XLA Modules:
  0.0 145.7 jit_solution(10813017976934054671)
XLA Ops:
  0.7 1.4 dynamic-slice_bitcast_fusion
  2.2 2.9 %collective-permute-start.4 = (bf16[64,4096]{1,0:T(8,128)(2,1)S(1)}, bf16[64,4096]{1,0:T(8,128)(2,1)S(1)}, u32[]{:S(2)}, u32[]{:S(2)}) collective-permute-start(bf16[64,4096]{1,0:T(8,128)(2,1)S(1)} %get-tuple-element.46.refs_0_.refs_2_), channel_id=1, source_target_pairs={{0,48},{4,20},{64,112},{68,84},{8,56},{12,28},{72,120},{76,92},{1,... | collective-permute-start | bytes 1572872 | tf_op jit(solution)/shard_map/ppermute | solution.py:79
  5.0 1.9 %collective-permute-start.2 = (bf16[64,4096]{1,0:T(8,128)(2,1)S(1)}, bf16[64,4096]{1,0:T(8,128)(2,1)S(1)}, u32[]{:S(2)}, u32[]{:S(2)}) collective-permute-start(bf16[64,4096]{1,0:T(8,128)(2,1)S(1)} %get-tuple-element.46.refs_0_.refs_2_), channel_id=1, source_target_pairs={{0,64},{4,76},{64,8},{68,4},{8,72},{12,68},{72,0},{76,12},{1,65},{... | collective-permute-start | bytes 1572872 | tf_op jit(solution)/shard_map/ppermute | solution.py:79
  7.2 3.4 %copy-done = bf16[1,2,4096,512]{3,2,1,0:T(8,128)(2,1)S(1)} copy-done((bf16[1,2,4096,512]{3,2,1,0:T(8,128)(2,1)S(1)}, bf16[1,2,4096,512]{3,2,1,0:T(8,128)(2,1)}, u32[]{:S(2)}) %copy-start) | copy-done | bytes 8388632
  11.2 3.0 %collective-permute-done.4.refs_2_.refs_4_ = bf16[64,4096]{1,0:T(8,128)(2,1)S(1)} collective-permute-done((bf16[64,4096]{1,0:T(8,128)(2,1)S(1)}, bf16[64,4096]{1,0:T(8,128)(2,1)S(1)}, u32[]{:S(2)}, u32[]{:S(2)}) %collective-permute-start.4) | collective-permute-done | bytes 524320 | tf_op jit(solution)/shard_map/ppermute | solution.py:79
  14.2 2.0 %collective-permute-done.2.refs_0_.refs_3_ = bf16[64,4096]{1,0:T(8,128)(2,1)S(1)} collective-permute-done((bf16[64,4096]{1,0:T(8,128)(2,1)S(1)}, bf16[64,4096]{1,0:T(8,128)(2,1)S(1)}, u32[]{:S(2)}, u32[]{:S(2)}) %collective-permute-start.2) | collective-permute-done | bytes 524320 | tf_op jit(solution)/shard_map/ppermute | solution.py:79
  16.2 1.8 %collective-permute-start.1 = (bf16[64,4096]{1,0:T(8,128)(2,1)S(1)}, bf16[64,4096]{1,0:T(8,128)(2,1)S(1)}, u32[]{:S(2)}, u32[]{:S(2)}) collective-permute-start(bf16[64,4096]{1,0:T(8,128)(2,1)S(1)} %collective-permute-done.refs_2_.refs_6_), channel_id=1, source_target_pairs={{0,4},{4,0},{64,68},{68,64},{8,12},{12,8},{72,76},{76,72},{1,5},{5... | collective-permute-start | bytes 1572872 | tf_op jit(solution)/shard_map/ppermute | solution.py:79
  18.0 2.7 %collective-permute-start.6 = (bf16[64,4096]{1,0:T(8,128)(2,1)S(1)}, bf16[64,4096]{1,0:T(8,128)(2,1)S(1)}, u32[]{:S(2)}, u32[]{:S(2)}) collective-permute-start(bf16[64,4096]{1,0:T(8,128)(2,1)S(1)} %collective-permute-done.refs_2_.refs_6_), channel_id=1, source_target_pairs={{0,64},{4,76},{64,8},{68,4},{8,72},{12,68},{72,0},{76,12},{1,65},{... | collective-permute-start | bytes 1572872 | tf_op jit(solution)/shard_map/ppermute | solution.py:79
  20.7 2.3 %collective-permute-start.8 = (bf16[64,4096]{1,0:T(8,128)(2,1)S(1)}, bf16[64,4096]{1,0:T(8,128)(2,1)S(1)}, u32[]{:S(2)}, u32[]{:S(2)}) collective-permute-start(bf16[64,4096]{1,0:T(8,128)(2,1)S(1)} %collective-permute-done.refs_2_.refs_6_), channel_id=1, source_target_pairs={{0,48},{4,20},{64,112},{68,84},{8,56},{12,28},{72,120},{76,92},{1,... | collective-permute-start | bytes 1572872 | tf_op jit(solution)/shard_map/ppermute | solution.py:79
  23.0 1.9 %collective-permute-start.10 = (bf16[64,4096]{1,0:T(8,128)(2,1)S(1)}, bf16[64,4096]{1,0:T(8,128)(2,1)S(1)}, u32[]{:S(2)}, u32[]{:S(2)}) collective-permute-start(bf16[64,4096]{1,0:T(8,128)(2,1)S(1)} %collective-permute-done.4.refs_2_.refs_4_), channel_id=1, source_target_pairs={{0,64},{4,76},{64,8},{68,4},{8,72},{12,68},{72,0},{76,12},{1,65},{... | collective-permute-start | bytes 1572872 | tf_op jit(solution)/shard_map/ppermute | solution.py:79
  24.9 2.3 %shard_map.77 = (bf16[256,512]{1,0:T(8,128)(2,1)S(1)}, bf16[256,512]{1,0:T(8,128)(2,1)S(1)}) custom-call(bf16[64,4096]{1,0:T(8,128)(2,1)S(1)} %collective-permute-done.2.refs_0_.refs_3_, bf16[64,4096]{1,0:T(8,128)(2,1)S(1)} %collective-permute-done.3.refs_1_.refs_11_, bf16[64,4096]{1,0:T(8,128)(2,1)S(1)} %collective-permute-done.4.refs_2_.refs_4_, ...), custom_call_target="tpu_custom_call" | custom-call | flops 1000 | bytes 1000 | tf_op jit(solution)/shard_map/pallas_call | solution.py:31
  27.2 2.3 %shard_map.76 = (bf16[256,512]{1,0:T(8,128)(2,1)S(1)}, bf16[256,512]{1,0:T(8,128)(2,1)S(1)}) custom-call(bf16[64,4096]{1,0:T(8,128)(2,1)S(1)} %get-tuple-element.46.refs_0_.refs_2_, bf16[64,4096]{1,0:T(8,128)(2,1)S(1)} %get-tuple-element.47.refs_1_.refs_10_, bf16[64,4096]{1,0:T(8,128)(2,1)S(1)} %collective-permute-done.refs_2_.refs_6_, ...), custom_call_target="tpu_custom_call" | custom-call | flops 1000 | bytes 1000 | tf_op jit(solution)/shard_map/pallas_call | solution.py:31
  29.9 1.2 collective-permute-done.8.refs_2_.refs_8_
  31.6 2.3 %collective-permute-start.12 = (bf16[64,4096]{1,0:T(8,128)(2,1)S(1)}, bf16[64,4096]{1,0:T(8,128)(2,1)S(1)}, u32[]{:S(2)}, u32[]{:S(2)}) collective-permute-start(bf16[64,4096]{1,0:T(8,128)(2,1)S(1)} %collective-permute-done.6.refs_0_.refs_7_), channel_id=1, source_target_pairs={{0,48},{4,20},{64,112},{68,84},{8,56},{12,28},{72,120},{76,92},{1,... | collective-permute-start | bytes 1572872 | tf_op jit(solution)/shard_map/ppermute | solution.py:79
  33.9 1.6 %collective-permute-done.10.refs_0_.refs_5_ = bf16[64,4096]{1,0:T(8,128)(2,1)S(1)} collective-permute-done((bf16[64,4096]{1,0:T(8,128)(2,1)S(1)}, bf16[64,4096]{1,0:T(8,128)(2,1)S(1)}, u32[]{:S(2)}, u32[]{:S(2)}) %collective-permute-start.10) | collective-permute-done | bytes 524320 | tf_op jit(solution)/shard_map/ppermute | solution.py:79
  35.5 2.3 %shard_map.78 = (bf16[256,512]{1,0:T(8,128)(2,1)S(1)}, bf16[256,512]{1,0:T(8,128)(2,1)S(1)}) custom-call(bf16[64,4096]{1,0:T(8,128)(2,1)S(1)} %collective-permute-done.6.refs_0_.refs_7_, bf16[64,4096]{1,0:T(8,128)(2,1)S(1)} %collective-permute-done.7.refs_1_.refs_15_, bf16[64,4096]{1,0:T(8,128)(2,1)S(1)} %collective-permute-done.8.refs_2_.refs_8_, ...), custom_call_target="tpu_custom_call" | custom-call | flops 1000 | bytes 1000 | tf_op jit(solution)/shard_map/pallas_call | solution.py:31
  37.8 4.2 %collective-permute-done.12.refs_2_.refs_9_ = bf16[64,4096]{1,0:T(8,128)(2,1)S(1)} collective-permute-done((bf16[64,4096]{1,0:T(8,128)(2,1)S(1)}, bf16[64,4096]{1,0:T(8,128)(2,1)S(1)}, u32[]{:S(2)}, u32[]{:S(2)}) %collective-permute-start.12) | collective-permute-done | bytes 524320 | tf_op jit(solution)/shard_map/ppermute | solution.py:79
  42.0 1.9 %collective-permute-done.13.refs_3_.refs_17_ = bf16[64,4096]{1,0:T(8,128)(2,1)S(1)} collective-permute-done((bf16[64,4096]{1,0:T(8,128)(2,1)S(1)}, bf16[64,4096]{1,0:T(8,128)(2,1)S(1)}, u32[]{:S(2)}, u32[]{:S(2)}) %collective-permute-start.13) | collective-permute-done | bytes 524320 | tf_op jit(solution)/shard_map/ppermute | solution.py:79
  43.9 2.3 %shard_map.79 = (bf16[256,512]{1,0:T(8,128)(2,1)S(1)}, bf16[256,512]{1,0:T(8,128)(2,1)S(1)}) custom-call(bf16[64,4096]{1,0:T(8,128)(2,1)S(1)} %collective-permute-done.10.refs_0_.refs_5_, bf16[64,4096]{1,0:T(8,128)(2,1)S(1)} %collective-permute-done.11.refs_1_.refs_13_, bf16[64,4096]{1,0:T(8,128)(2,1)S(1)} %collective-permute-done.12.refs_2_.refs_9_, ...), custom_call_target="tpu_custom_call" | custom-call | flops 1000 | bytes 1000 | tf_op jit(solution)/shard_map/pallas_call | solution.py:31
  46.2 3.5 %shard_map.80 = (bf16[1,1,512,512]{3,2,1,0:T(8,128)(2,1)}, f32[2,512,1024]{2,1,0:T(8,128)S(1)}, bf16[1024,512]{1,0:T(8,128)(2,1)S(1)}, bf16[512,1024]{1,0:T(8,128)(2,1)S(1)}) custom-call(bf16[1,1,512,512]{3,2,1,0:T(8,128)(2,1)S(1)} %get-tuple-element.44.refs_0_, bf16[1,1,512,512]{3,2,1,0:T(8,128)(2,1)S(1)} %get-tuple-element.45.refs_1_, ...), custom_call_target="tpu_custom_call" | custom-call | flops 1000 | bytes 1000 | tf_op jit(solution)/shard_map/pallas_call | solution.py:31
  49.8 2.9 %shard_map.81.refs_12_ = bf16[512,2048]{1,0:T(8,128)(2,1)S(1)} custom-call(s32[4]{0:T(128)S(1)} %get-tuple-element.62.refs_0_, bf16[512,1024]{1,0:T(8,128)(2,1)S(1)} %get-tuple-element.63.refs_1_, bf16[64,4096]{1,0:T(8,128)(2,1)S(1)} %get-tuple-element.46.refs_0_.refs_2_, bf16[64,4096]{1,0:T(8,128)(2,1)S(1)} %collective-permute-done.2.refs_0_.refs_3_, ...), custom_call_target="tpu_custom_call" | custom-call | flops 1000 | bytes 1000 | tf_op jit(solution)/shard_map/pallas_call | solution.py:31
  52.7 1.7 %collective-permute-start.21 = (bf16[512,2048]{1,0:T(8,128)(2,1)S(1)}, bf16[512,2048]{1,0:T(8,128)(2,1)S(1)}, u32[]{:S(2)}, u32[]{:S(2)}) collective-permute-start(bf16[512,2048]{1,0:T(8,128)(2,1)S(1)} %shard_map.81.refs_12_), channel_id=1, source_target_pairs={{0,1},{4,7},{64,65},{68,71},{8,9},{12,15},{72,73},{76,79},{1,0},{5... | collective-permute-start | bytes 6291464 | tf_op jit(solution)/shard_map/ppermute | solution.py:79
  54.3 2.6 %shard_map.82 = (bf16[1,1,512,512]{3,2,1,0:T(8,128)(2,1)}, bf16[1024,512]{1,0:T(8,128)(2,1)S(1)}, bf16[512,1024]{1,0:T(8,128)(2,1)S(1)}) custom-call(bf16[1,1,512,512]{3,2,1,0:T(8,128)(2,1)S(1)} %get-tuple-element.44.refs_0_, bf16[1,1,512,512]{3,2,1,0:T(8,128)(2,1)S(1)} %get-tuple-element.45.refs_1_, bf16[256,512]{1,0:T(8,128)(2,1)S(1)} %get-tuple-element.49.refs_2_, ...), custom_call_target="tpu_custom_call" | custom-call | flops 1000 | bytes 1000 | tf_op jit(solution)/shard_map/pallas_call | solution.py:31
  56.9 2.4 %shard_map.85 = (bf16[256,2048]{1,0:T(8,128)(2,1)S(1)}, bf16[256,2048]{1,0:T(8,128)(2,1)S(1)}) custom-call(bf16[1024,512]{1,0:T(8,128)(2,1)S(1)} %get-tuple-element.65.refs_0_, bf16[1024,512]{1,0:T(8,128)(2,1)S(1)} %get-tuple-element.66.refs_1_, bf16[1,2,4096,512]{3,2,1,0:T(8,128)(2,1)S(1)} %get-tuple-element.48.refs_4_.refs_2_), custom_call_target="tpu_custom_call" | custom-call | flops 1000 | bytes 1000 | tf_op jit(solution)/shard_map/pallas_call | solution.py:31
  59.3 1.4 collective-permute-start.16
  60.8 2.4 %shard_map.83 = (bf16[256,2048]{1,0:T(8,128)(2,1)S(1)}, bf16[256,2048]{1,0:T(8,128)(2,1)S(1)}) custom-call(bf16[1024,512]{1,0:T(8,128)(2,1)S(1)} %get-tuple-element.65.refs_0_, bf16[1024,512]{1,0:T(8,128)(2,1)S(1)} %get-tuple-element.66.refs_1_, bf16[1,2,4096,512]{3,2,1,0:T(8,128)(2,1)S(1)} %get-tuple-element.48.refs_4_.refs_2_), custom_call_target="tpu_custom_call" | custom-call | flops 1000 | bytes 1000 | tf_op jit(solution)/shard_map/pallas_call | solution.py:31
  64.4 2.4 %shard_map.86 = (bf16[256,2048]{1,0:T(8,128)(2,1)S(1)}, bf16[256,2048]{1,0:T(8,128)(2,1)S(1)}) custom-call(bf16[1024,512]{1,0:T(8,128)(2,1)S(1)} %get-tuple-element.65.refs_0_, bf16[1024,512]{1,0:T(8,128)(2,1)S(1)} %get-tuple-element.66.refs_1_, bf16[1,2,4096,512]{3,2,1,0:T(8,128)(2,1)S(1)} %get-tuple-element.48.refs_4_.refs_2_, ...), custom_call_target="tpu_custom_call" | custom-call | flops 1000 | bytes 1000 | tf_op jit(solution)/shard_map/pallas_call | solution.py:31
  67.4 2.4 %shard_map.84 = (bf16[256,2048]{1,0:T(8,128)(2,1)S(1)}, bf16[256,2048]{1,0:T(8,128)(2,1)S(1)}) custom-call(bf16[1024,512]{1,0:T(8,128)(2,1)S(1)} %get-tuple-element.65.refs_0_, bf16[1024,512]{1,0:T(8,128)(2,1)S(1)} %get-tuple-element.66.refs_1_, bf16[1,2,4096,512]{3,2,1,0:T(8,128)(2,1)S(1)} %get-tuple-element.48.refs_4_.refs_2_, ...), custom_call_target="tpu_custom_call" | custom-call | flops 1000 | bytes 1000 | tf_op jit(solution)/shard_map/pallas_call | solution.py:31
  69.9 1.6 %collective-permute-start.18 = (bf16[256,2048]{1,0:T(8,128)(2,1)S(1)}, bf16[256,2048]{1,0:T(8,128)(2,1)S(1)}, u32[]{:S(2)}, u32[]{:S(2)}) collective-permute-start(bf16[256,2048]{1,0:T(8,128)(2,1)S(1)} %get-tuple-element.72.refs_18_), channel_id=1, source_target_pairs={{0,16},{4,52},{64,80},{68,116},{8,24},{12,60},{72,88},{76,124},{1,... | collective-permute-start | bytes 3145736 | tf_op jit(solution)/shard_map/ppermute | solution.py:79
  71.4 2.9 %shard_map.87.refs_18_ = bf16[512,2048]{1,0:T(8,128)(2,1)S(1)} custom-call(s32[4]{0:T(128)S(1)} %get-tuple-element.62.refs_0_, bf16[512,1024]{1,0:T(8,128)(2,1)S(1)} %get-tuple-element.71.refs_1_, bf16[64,4096]{1,0:T(8,128)(2,1)S(1)} %get-tuple-element.46.refs_0_.refs_2_, bf16[64,4096]{1,0:T(8,128)(2,1)S(1)} %collective-permute-done.2.refs_0_.refs_3_, ...), custom_call_target="tpu_custom_call" | custom-call | flops 1000 | bytes 1000 | tf_op jit(solution)/shard_map/pallas_call | solution.py:31
  74.3 2.9 %shard_map.88.refs_18_.keep = bf16[512,2048]{1,0:T(8,128)(2,1)S(1)} custom-call(s32[4]{0:T(128)S(1)} %get-tuple-element.70.refs_0_, bf16[512,1024]{1,0:T(8,128)(2,1)S(1)} %get-tuple-element.63.refs_1_, bf16[64,4096]{1,0:T(8,128)(2,1)S(1)} %get-tuple-element.46.refs_0_.refs_2_, bf16[64,4096]{1,0:T(8,128)(2,1)S(1)} %collective-permute-done.2.refs_0_.refs_3_, ...), custom_call_target="tpu_custom_call" | custom-call | flops 1000 | bytes 1000 | tf_op jit(solution)/shard_map/pallas_call | solution.py:31
  77.3 2.9 %shard_map.89.keep = bf16[512,2048]{1,0:T(8,128)(2,1)S(1)} custom-call(s32[4]{0:T(128)S(1)} %get-tuple-element.70.refs_0_, bf16[512,1024]{1,0:T(8,128)(2,1)S(1)} %get-tuple-element.71.refs_1_, bf16[64,4096]{1,0:T(8,128)(2,1)S(1)} %get-tuple-element.46.refs_0_.refs_2_, bf16[64,4096]{1,0:T(8,128)(2,1)S(1)} %collective-permute-done.2.refs_0_.refs_3_, ...), custom_call_target="tpu_custom_call" | custom-call | flops 1000 | bytes 1000 | tf_op jit(solution)/shard_map/pallas_call | solution.py:31
  80.4 1.3 collective-permute-done.24
  82.1 2.3 %collective-permute-start.25 = (bf16[128,2048]{1,0:T(8,128)(2,1)S(1)}, bf16[128,2048]{1,0:T(8,128)(2,1)S(1)}, u32[]{:S(2)}, u32[]{:S(2)}) collective-permute-start(bf16[128,2048]{1,0:T(8,128)(2,1)S(1)} %slice.80), channel_id=1, source_target_pairs={{0,48},{4,20},{64,112},{68,84},{8,56},{12,28},{72,120},{76,92},{1,... | collective-permute-start | bytes 1572872 | tf_op jit(solution)/shard_map/ppermute | solution.py:79
  84.5 14.1 %collective-permute-done.18 = bf16[256,2048]{1,0:T(8,128)(2,1)S(1)} collective-permute-done((bf16[256,2048]{1,0:T(8,128)(2,1)S(1)}, bf16[256,2048]{1,0:T(8,128)(2,1)S(1)}, u32[]{:S(2)}, u32[]{:S(2)}) %collective-permute-start.18) | collective-permute-done | bytes 1048608 | tf_op jit(solution)/shard_map/ppermute | solution.py:79
  99.0 2.3 %collective-permute-start.19 = (bf16[128,2048]{1,0:T(8,128)(2,1)S(1)}, bf16[128,2048]{1,0:T(8,128)(2,1)S(1)}, u32[]{:S(2)}, u32[]{:S(2)}) collective-permute-start(bf16[128,2048]{1,0:T(8,128)(2,1)S(1)} %slice.81), channel_id=1, source_target_pairs={{0,48},{4,20},{64,112},{68,84},{8,56},{12,28},{72,120},{76,92},{1,... | collective-permute-start | bytes 1572872 | tf_op jit(solution)/shard_map/ppermute | solution.py:79
  101.9 2.3 %collective-permute-start.26 = (bf16[64,2048]{1,0:T(8,128)(2,1)S(1)}, bf16[64,2048]{1,0:T(8,128)(2,1)S(1)}, u32[]{:S(2)}, u32[]{:S(2)}) collective-permute-start(bf16[64,2048]{1,0:T(8,128)(2,1)S(1)} %slice.82), channel_id=1, source_target_pairs={{0,72},{4,68},{64,0},{68,12},{8,64},{12,76},{72,8},{76,4},{1,73},{... | collective-permute-start | bytes 786440 | tf_op jit(solution)/shard_map/ppermute | solution.py:79
  104.2 5.3 %collective-permute-done.19 = bf16[128,2048]{1,0:T(8,128)(2,1)S(1)} collective-permute-done((bf16[128,2048]{1,0:T(8,128)(2,1)S(1)}, bf16[128,2048]{1,0:T(8,128)(2,1)S(1)}, u32[]{:S(2)}, u32[]{:S(2)}) %collective-permute-start.19) | collective-permute-done | bytes 524320 | tf_op jit(solution)/shard_map/ppermute | solution.py:79
  109.6 2.1 %collective-permute-start.20 = (bf16[64,2048]{1,0:T(8,128)(2,1)S(1)}, bf16[64,2048]{1,0:T(8,128)(2,1)S(1)}, u32[]{:S(2)}, u32[]{:S(2)}) collective-permute-start(bf16[64,2048]{1,0:T(8,128)(2,1)S(1)} %slice.83), channel_id=1, source_target_pairs={{0,72},{4,68},{64,0},{68,12},{8,64},{12,76},{72,8},{76,4},{1,73},{... | collective-permute-start | bytes 786440 | tf_op jit(solution)/shard_map/ppermute | solution.py:79
  111.7 1.3 collective-permute-start.30
  113.0 2.1 %collective-permute-start.27 = (bf16[64,2048]{1,0:T(8,128)(2,1)S(1)}, bf16[64,2048]{1,0:T(8,128)(2,1)S(1)}, u32[]{:S(2)}, u32[]{:S(2)}) collective-permute-start(bf16[64,2048]{1,0:T(8,128)(2,1)S(1)} %fusion), channel_id=1, source_target_pairs={{0,8},{4,12},{64,72},{68,76},{8,0},{12,4},{72,64},{76,68},{1,9},{5... | collective-permute-start | bytes 786440 | tf_op jit(solution)/shard_map/ppermute | solution.py:79
  115.0 8.1 %collective-permute-done.20 = bf16[64,2048]{1,0:T(8,128)(2,1)S(1)} collective-permute-done((bf16[64,2048]{1,0:T(8,128)(2,1)S(1)}, bf16[64,2048]{1,0:T(8,128)(2,1)S(1)}, u32[]{:S(2)}, u32[]{:S(2)}) %collective-permute-start.20) | collective-permute-done | bytes 262176 | tf_op jit(solution)/shard_map/ppermute | solution.py:79
  123.9 3.8 %collective-permute-done.30.second = bf16[512,1024]{1,0:T(8,128)(2,1)S(1)} collective-permute-done((bf16[512,1024]{1,0:T(8,128)(2,1)S(1)}, bf16[512,1024]{1,0:T(8,128)(2,1)S(1)}, u32[]{:S(2)}, u32[]{:S(2)}) %collective-permute-start.30) | collective-permute-done | bytes 1048608 | tf_op jit(solution)/shard_map/ppermute | solution.py:79
  127.7 1.3 collective-permute-start.31
  128.9 2.4 %collective-permute-done.23 = bf16[64,2048]{1,0:T(8,128)(2,1)S(1)} collective-permute-done((bf16[64,2048]{1,0:T(8,128)(2,1)S(1)}, bf16[64,2048]{1,0:T(8,128)(2,1)S(1)}, u32[]{:S(2)}, u32[]{:S(2)}) %collective-permute-start.23) | collective-permute-done | bytes 262176 | tf_op jit(solution)/shard_map/ppermute | solution.py:79
  134.4 1.8 %shard_map.91.refs_0_ = bf16[1,2,1024,512]{3,2,1,0:T(8,128)(2,1)} custom-call(bf16[512,2048]{1,0:T(8,128)(2,1)S(1)} %shard_map.88.refs_18_.keep, bf16[512,2048]{1,0:T(8,128)(2,1)S(1)} %collective-permute-done.21.first, bf16[512,1024]{1,0:T(8,128)(2,1)S(1)} %collective-permute-done.30.second), custom_call_target="tpu_custom_call" | custom-call | flops 1000 | bytes 1000 | tf_op jit(solution)/shard_map/pallas_call | solution.py:238
  136.2 7.5 %collective-permute-done.31.second = bf16[512,1024]{1,0:T(8,128)(2,1)S(1)} collective-permute-done((bf16[512,1024]{1,0:T(8,128)(2,1)S(1)}, bf16[512,1024]{1,0:T(8,128)(2,1)S(1)}, u32[]{:S(2)}, u32[]{:S(2)}) %collective-permute-start.31) | collective-permute-done | bytes 1048608 | tf_op jit(solution)/shard_map/ppermute | solution.py:79
  143.7 1.8 %shard_map.92 = bf16[1,2,1024,512]{3,2,1,0:T(8,128)(2,1)} custom-call(bf16[512,2048]{1,0:T(8,128)(2,1)S(1)} %shard_map.89.keep, bf16[512,2048]{1,0:T(8,128)(2,1)S(1)} %collective-permute-done.22.first, bf16[512,1024]{1,0:T(8,128)(2,1)S(1)} %collective-permute-done.31.second, bf16[1,2,1024,512]{3,2,1,0:T(8,128)(2,1)} %shard_map.91.refs_0_), custom_call_target="tpu_custom_call", output_to_operand_aliasing={{}: (3, {})} | custom-call | flops 1000 | bytes 1000 | tf_op jit(solution)/shard_map/pallas_call | solution.py:238
  (58 shorter events, 9.4 us)
Async XLA Ops:
  0.6 6.5 %copy-start.2 = (bf16[1,1,512,512]{3,2,1,0:T(8,128)(2,1)S(1)}, bf16[1,1,512,512]{3,2,1,0:T(8,128)(2,1)}, u32[]{:S(2)}) copy-start(bf16[1,1,512,512]{3,2,1,0:T(8,128)(2,1)} %refs_2_.1) | copy-start | bytes 1572868
  0.6 6.5 %copy-start.1 = (bf16[1,1,512,512]{3,2,1,0:T(8,128)(2,1)S(1)}, bf16[1,1,512,512]{3,2,1,0:T(8,128)(2,1)}, u32[]{:S(2)}) copy-start(bf16[1,1,512,512]{3,2,1,0:T(8,128)(2,1)} %refs_1_.1) | copy-start | bytes 1572868
  2.2 12.0 %collective-permute-start.4 = (bf16[64,4096]{1,0:T(8,128)(2,1)S(1)}, bf16[64,4096]{1,0:T(8,128)(2,1)S(1)}, u32[]{:S(2)}, u32[]{:S(2)}) collective-permute-start(bf16[64,4096]{1,0:T(8,128)(2,1)S(1)} %get-tuple-element.46.refs_0_.refs_2_), channel_id=1, source_target_pairs={{0,48},{4,20},{64,112},{68,84},{8,56},{12,28},{72,120},{76,92},{1,... | collective-permute-start | bytes 1572872 | tf_op jit(solution)/shard_map/ppermute | solution.py:79
  5.0 11.2 %collective-permute-start.2 = (bf16[64,4096]{1,0:T(8,128)(2,1)S(1)}, bf16[64,4096]{1,0:T(8,128)(2,1)S(1)}, u32[]{:S(2)}, u32[]{:S(2)}) collective-permute-start(bf16[64,4096]{1,0:T(8,128)(2,1)S(1)} %get-tuple-element.46.refs_0_.refs_2_), channel_id=1, source_target_pairs={{0,64},{4,76},{64,8},{68,4},{8,72},{12,68},{72,0},{76,12},{1,65},{... | collective-permute-start | bytes 1572872 | tf_op jit(solution)/shard_map/ppermute | solution.py:79
  7.0 9.3 %collective-permute-start = (bf16[64,4096]{1,0:T(8,128)(2,1)S(1)}, bf16[64,4096]{1,0:T(8,128)(2,1)S(1)}, u32[]{:S(2)}, u32[]{:S(2)}) collective-permute-start(bf16[64,4096]{1,0:T(8,128)(2,1)S(1)} %get-tuple-element.46.refs_0_.refs_2_), channel_id=1, source_target_pairs={{0,16},{4,52},{64,80},{68,116},{8,24},{12,60},{72,88},{76,124},{1,... | collective-permute-start | bytes 1572872 | tf_op jit(solution)/shard_map/ppermute | solution.py:79
  7.2 3.4 %copy-start = (bf16[1,2,4096,512]{3,2,1,0:T(8,128)(2,1)S(1)}, bf16[1,2,4096,512]{3,2,1,0:T(8,128)(2,1)}, u32[]{:S(2)}) copy-start(bf16[1,2,4096,512]{3,2,1,0:T(8,128)(2,1)} %refs_0_.1) | copy-start | bytes 25165828
  14.2 8.8 %collective-permute-start.5 = (bf16[64,4096]{1,0:T(8,128)(2,1)S(1)}, bf16[64,4096]{1,0:T(8,128)(2,1)S(1)}, u32[]{:S(2)}, u32[]{:S(2)}) collective-permute-start(bf16[64,4096]{1,0:T(8,128)(2,1)S(1)} %collective-permute-done.4.refs_2_.refs_4_), channel_id=1, source_target_pairs={{0,4},{4,0},{64,68},{68,64},{8,12},{12,8},{72,76},{76,72},{1,5},{5... | collective-permute-start | bytes 1572872 | tf_op jit(solution)/shard_map/ppermute | solution.py:79
  16.2 8.7 %collective-permute-start.3 = (bf16[64,4096]{1,0:T(8,128)(2,1)S(1)}, bf16[64,4096]{1,0:T(8,128)(2,1)S(1)}, u32[]{:S(2)}, u32[]{:S(2)}) collective-permute-start(bf16[64,4096]{1,0:T(8,128)(2,1)S(1)} %collective-permute-done.2.refs_0_.refs_3_), channel_id=1, source_target_pairs={{0,4},{4,0},{64,68},{68,64},{8,12},{12,8},{72,76},{76,72},{1,5},{5... | collective-permute-start | bytes 1572872 | tf_op jit(solution)/shard_map/ppermute | solution.py:79
  16.2 11.0 %collective-permute-start.1 = (bf16[64,4096]{1,0:T(8,128)(2,1)S(1)}, bf16[64,4096]{1,0:T(8,128)(2,1)S(1)}, u32[]{:S(2)}, u32[]{:S(2)}) collective-permute-start(bf16[64,4096]{1,0:T(8,128)(2,1)S(1)} %collective-permute-done.refs_2_.refs_6_), channel_id=1, source_target_pairs={{0,4},{4,0},{64,68},{68,64},{8,12},{12,8},{72,76},{76,72},{1,5},{5... | collective-permute-start | bytes 1572872 | tf_op jit(solution)/shard_map/ppermute | solution.py:79
  18.0 11.9 %collective-permute-start.6 = (bf16[64,4096]{1,0:T(8,128)(2,1)S(1)}, bf16[64,4096]{1,0:T(8,128)(2,1)S(1)}, u32[]{:S(2)}, u32[]{:S(2)}) collective-permute-start(bf16[64,4096]{1,0:T(8,128)(2,1)S(1)} %collective-permute-done.refs_2_.refs_6_), channel_id=1, source_target_pairs={{0,64},{4,76},{64,8},{68,4},{8,72},{12,68},{72,0},{76,12},{1,65},{... | collective-permute-start | bytes 1572872 | tf_op jit(solution)/shard_map/ppermute | solution.py:79
  20.7 10.4 %collective-permute-start.8 = (bf16[64,4096]{1,0:T(8,128)(2,1)S(1)}, bf16[64,4096]{1,0:T(8,128)(2,1)S(1)}, u32[]{:S(2)}, u32[]{:S(2)}) collective-permute-start(bf16[64,4096]{1,0:T(8,128)(2,1)S(1)} %collective-permute-done.refs_2_.refs_6_), channel_id=1, source_target_pairs={{0,48},{4,20},{64,112},{68,84},{8,56},{12,28},{72,120},{76,92},{1,... | collective-permute-start | bytes 1572872 | tf_op jit(solution)/shard_map/ppermute | solution.py:79
  23.0 12.5 %collective-permute-start.10 = (bf16[64,4096]{1,0:T(8,128)(2,1)S(1)}, bf16[64,4096]{1,0:T(8,128)(2,1)S(1)}, u32[]{:S(2)}, u32[]{:S(2)}) collective-permute-start(bf16[64,4096]{1,0:T(8,128)(2,1)S(1)} %collective-permute-done.4.refs_2_.refs_4_), channel_id=1, source_target_pairs={{0,64},{4,76},{64,8},{68,4},{8,72},{12,68},{72,0},{76,12},{1,65},{... | collective-permute-start | bytes 1572872 | tf_op jit(solution)/shard_map/ppermute | solution.py:79
  31.1 4.4 %collective-permute-start.9 = (bf16[64,4096]{1,0:T(8,128)(2,1)S(1)}, bf16[64,4096]{1,0:T(8,128)(2,1)S(1)}, u32[]{:S(2)}, u32[]{:S(2)}) collective-permute-start(bf16[64,4096]{1,0:T(8,128)(2,1)S(1)} %collective-permute-done.8.refs_2_.refs_8_), channel_id=1, source_target_pairs={{0,4},{4,0},{64,68},{68,64},{8,12},{12,8},{72,76},{76,72},{1,5},{5... | collective-permute-start | bytes 1572872 | tf_op jit(solution)/shard_map/ppermute | solution.py:79
  31.2 4.3 %collective-permute-start.7 = (bf16[64,4096]{1,0:T(8,128)(2,1)S(1)}, bf16[64,4096]{1,0:T(8,128)(2,1)S(1)}, u32[]{:S(2)}, u32[]{:S(2)}) collective-permute-start(bf16[64,4096]{1,0:T(8,128)(2,1)S(1)} %collective-permute-done.6.refs_0_.refs_7_), channel_id=1, source_target_pairs={{0,4},{4,0},{64,68},{68,64},{8,12},{12,8},{72,76},{76,72},{1,5},{5... | collective-permute-start | bytes 1572872 | tf_op jit(solution)/shard_map/ppermute | solution.py:79
  31.6 10.4 %collective-permute-start.12 = (bf16[64,4096]{1,0:T(8,128)(2,1)S(1)}, bf16[64,4096]{1,0:T(8,128)(2,1)S(1)}, u32[]{:S(2)}, u32[]{:S(2)}) collective-permute-start(bf16[64,4096]{1,0:T(8,128)(2,1)S(1)} %collective-permute-done.6.refs_0_.refs_7_), channel_id=1, source_target_pairs={{0,48},{4,20},{64,112},{68,84},{8,56},{12,28},{72,120},{76,92},{1,... | collective-permute-start | bytes 1572872 | tf_op jit(solution)/shard_map/ppermute | solution.py:79
  35.5 6.5 %collective-permute-start.11 = (bf16[64,4096]{1,0:T(8,128)(2,1)S(1)}, bf16[64,4096]{1,0:T(8,128)(2,1)S(1)}, u32[]{:S(2)}, u32[]{:S(2)}) collective-permute-start(bf16[64,4096]{1,0:T(8,128)(2,1)S(1)} %collective-permute-done.10.refs_0_.refs_5_), channel_id=1, source_target_pairs={{0,4},{4,0},{64,68},{68,64},{8,12},{12,8},{72,76},{76,72},{1,5},{5... | collective-permute-start | bytes 1572872 | tf_op jit(solution)/shard_map/ppermute | solution.py:79
  42.0 1.9 %collective-permute-start.13 = (bf16[64,4096]{1,0:T(8,128)(2,1)S(1)}, bf16[64,4096]{1,0:T(8,128)(2,1)S(1)}, u32[]{:S(2)}, u32[]{:S(2)}) collective-permute-start(bf16[64,4096]{1,0:T(8,128)(2,1)S(1)} %collective-permute-done.12.refs_2_.refs_9_), channel_id=1, source_target_pairs={{0,4},{4,0},{64,68},{68,64},{8,12},{12,8},{72,76},{76,72},{1,5},{5... | collective-permute-start | bytes 1572872 | tf_op jit(solution)/shard_map/ppermute | solution.py:79
  49.8 4.6 %copy-start.3 = (bf16[1,1,512,512]{3,2,1,0:T(8,128)(2,1)S(1)}, bf16[1,1,512,512]{3,2,1,0:T(8,128)(2,1)}, u32[]{:S(2)}) copy-start(bf16[1,1,512,512]{3,2,1,0:T(8,128)(2,1)} %get-tuple-element.40.refs_10_) | copy-start | bytes 1572868
  52.7 27.5 %collective-permute-start.21 = (bf16[512,2048]{1,0:T(8,128)(2,1)S(1)}, bf16[512,2048]{1,0:T(8,128)(2,1)S(1)}, u32[]{:S(2)}, u32[]{:S(2)}) collective-permute-start(bf16[512,2048]{1,0:T(8,128)(2,1)S(1)} %shard_map.81.refs_12_), channel_id=1, source_target_pairs={{0,1},{4,7},{64,65},{68,71},{8,9},{12,15},{72,73},{76,79},{1,0},{5... | collective-permute-start | bytes 6291464 | tf_op jit(solution)/shard_map/ppermute | solution.py:79
  59.3 4.7 %collective-permute-start.16 = (bf16[256,2048]{1,0:T(8,128)(2,1)S(1)}, bf16[256,2048]{1,0:T(8,128)(2,1)S(1)}, u32[]{:S(2)}, u32[]{:S(2)}) collective-permute-start(bf16[256,2048]{1,0:T(8,128)(2,1)S(1)} %get-tuple-element.73), channel_id=1, source_target_pairs={{0,4},{4,0},{64,68},{68,64},{8,12},{12,8},{72,76},{76,72},{1,5},{5... | collective-permute-start | bytes 3145736 | tf_op jit(solution)/shard_map/ppermute | solution.py:79
  60.7 3.8 %collective-permute-start.17 = (bf16[256,2048]{1,0:T(8,128)(2,1)S(1)}, bf16[256,2048]{1,0:T(8,128)(2,1)S(1)}, u32[]{:S(2)}, u32[]{:S(2)}) collective-permute-start(bf16[256,2048]{1,0:T(8,128)(2,1)S(1)} %get-tuple-element.74), channel_id=1, source_target_pairs={{0,4},{4,0},{64,68},{68,64},{8,12},{12,8},{72,76},{76,72},{1,5},{5... | collective-permute-start | bytes 3145736 | tf_op jit(solution)/shard_map/ppermute | solution.py:79
  63.1 3.8 %collective-permute-start.14 = (bf16[256,2048]{1,0:T(8,128)(2,1)S(1)}, bf16[256,2048]{1,0:T(8,128)(2,1)S(1)}, u32[]{:S(2)}, u32[]{:S(2)}) collective-permute-start(bf16[256,2048]{1,0:T(8,128)(2,1)S(1)} %get-tuple-element.67), channel_id=1, source_target_pairs={{0,4},{4,0},{64,68},{68,64},{8,12},{12,8},{72,76},{76,72},{1,5},{5... | collective-permute-start | bytes 3145736 | tf_op jit(solution)/shard_map/ppermute | solution.py:79
  63.6 3.8 %collective-permute-start.15 = (bf16[256,2048]{1,0:T(8,128)(2,1)S(1)}, bf16[256,2048]{1,0:T(8,128)(2,1)S(1)}, u32[]{:S(2)}, u32[]{:S(2)}) collective-permute-start(bf16[256,2048]{1,0:T(8,128)(2,1)S(1)} %get-tuple-element.68), channel_id=1, source_target_pairs={{0,4},{4,0},{64,68},{68,64},{8,12},{12,8},{72,76},{76,72},{1,5},{5... | collective-permute-start | bytes 3145736 | tf_op jit(solution)/shard_map/ppermute | solution.py:79
  66.8 14.9 %collective-permute-start.24 = (bf16[256,2048]{1,0:T(8,128)(2,1)S(1)}, bf16[256,2048]{1,0:T(8,128)(2,1)S(1)}, u32[]{:S(2)}, u32[]{:S(2)}) collective-permute-start(bf16[256,2048]{1,0:T(8,128)(2,1)S(1)} %get-tuple-element.75.refs_19_), channel_id=1, source_target_pairs={{0,16},{4,52},{64,80},{68,116},{8,24},{12,60},{72,88},{76,124},{1,... | collective-permute-start | bytes 3145736 | tf_op jit(solution)/shard_map/ppermute | solution.py:79
  69.9 28.7 %collective-permute-start.18 = (bf16[256,2048]{1,0:T(8,128)(2,1)S(1)}, bf16[256,2048]{1,0:T(8,128)(2,1)S(1)}, u32[]{:S(2)}, u32[]{:S(2)}) collective-permute-start(bf16[256,2048]{1,0:T(8,128)(2,1)S(1)} %get-tuple-element.72.refs_18_), channel_id=1, source_target_pairs={{0,16},{4,52},{64,80},{68,116},{8,24},{12,60},{72,88},{76,124},{1,... | collective-permute-start | bytes 3145736 | tf_op jit(solution)/shard_map/ppermute | solution.py:79
  80.2 31.5 %collective-permute-start.22 = (bf16[512,2048]{1,0:T(8,128)(2,1)S(1)}, bf16[512,2048]{1,0:T(8,128)(2,1)S(1)}, u32[]{:S(2)}, u32[]{:S(2)}) collective-permute-start(bf16[512,2048]{1,0:T(8,128)(2,1)S(1)} %shard_map.87.refs_18_), channel_id=1, source_target_pairs={{0,1},{4,7},{64,65},{68,71},{8,9},{12,15},{72,73},{76,79},{1,0},{5... | collective-permute-start | bytes 6291464 | tf_op jit(solution)/shard_map/ppermute | solution.py:79
  82.1 19.6 %collective-permute-start.25 = (bf16[128,2048]{1,0:T(8,128)(2,1)S(1)}, bf16[128,2048]{1,0:T(8,128)(2,1)S(1)}, u32[]{:S(2)}, u32[]{:S(2)}) collective-permute-start(bf16[128,2048]{1,0:T(8,128)(2,1)S(1)} %slice.80), channel_id=1, source_target_pairs={{0,48},{4,20},{64,112},{68,84},{8,56},{12,28},{72,120},{76,92},{1,... | collective-permute-start | bytes 1572872 | tf_op jit(solution)/shard_map/ppermute | solution.py:79
  99.0 10.5 %collective-permute-start.19 = (bf16[128,2048]{1,0:T(8,128)(2,1)S(1)}, bf16[128,2048]{1,0:T(8,128)(2,1)S(1)}, u32[]{:S(2)}, u32[]{:S(2)}) collective-permute-start(bf16[128,2048]{1,0:T(8,128)(2,1)S(1)} %slice.81), channel_id=1, source_target_pairs={{0,48},{4,20},{64,112},{68,84},{8,56},{12,28},{72,120},{76,92},{1,... | collective-permute-start | bytes 1572872 | tf_op jit(solution)/shard_map/ppermute | solution.py:79
  101.9 11.1 %collective-permute-start.26 = (bf16[64,2048]{1,0:T(8,128)(2,1)S(1)}, bf16[64,2048]{1,0:T(8,128)(2,1)S(1)}, u32[]{:S(2)}, u32[]{:S(2)}) collective-permute-start(bf16[64,2048]{1,0:T(8,128)(2,1)S(1)} %slice.82), channel_id=1, source_target_pairs={{0,72},{4,68},{64,0},{68,12},{8,64},{12,76},{72,8},{76,4},{1,73},{... | collective-permute-start | bytes 786440 | tf_op jit(solution)/shard_map/ppermute | solution.py:79
  109.6 13.5 %collective-permute-start.20 = (bf16[64,2048]{1,0:T(8,128)(2,1)S(1)}, bf16[64,2048]{1,0:T(8,128)(2,1)S(1)}, u32[]{:S(2)}, u32[]{:S(2)}) collective-permute-start(bf16[64,2048]{1,0:T(8,128)(2,1)S(1)} %slice.83), channel_id=1, source_target_pairs={{0,72},{4,68},{64,0},{68,12},{8,64},{12,76},{72,8},{76,4},{1,73},{... | collective-permute-start | bytes 786440 | tf_op jit(solution)/shard_map/ppermute | solution.py:79
  111.7 16.0 %collective-permute-start.30 = (bf16[512,1024]{1,0:T(8,128)(2,1)S(1)}, bf16[512,1024]{1,0:T(8,128)(2,1)S(1)}, u32[]{:S(2)}, u32[]{:S(2)}) collective-permute-start(bf16[512,1024]{1,0:T(8,128)(2,1)S(1)} %add_convert_fusion), channel_id=1, source_target_pairs={{0,3},{4,5},{64,67},{68,69},{8,11},{12,13},{72,75},{76,77},{1,2},{... | collective-permute-start | bytes 3145736 | tf_op jit(solution)/shard_map/ppermute | solution.py:79
  113.0 18.6 %collective-permute-start.27 = (bf16[64,2048]{1,0:T(8,128)(2,1)S(1)}, bf16[64,2048]{1,0:T(8,128)(2,1)S(1)}, u32[]{:S(2)}, u32[]{:S(2)}) collective-permute-start(bf16[64,2048]{1,0:T(8,128)(2,1)S(1)} %fusion), channel_id=1, source_target_pairs={{0,8},{4,12},{64,72},{68,76},{8,0},{12,4},{72,64},{76,68},{1,9},{5... | collective-permute-start | bytes 786440 | tf_op jit(solution)/shard_map/ppermute | solution.py:79
  123.2 8.2 %collective-permute-start.23 = (bf16[64,2048]{1,0:T(8,128)(2,1)S(1)}, bf16[64,2048]{1,0:T(8,128)(2,1)S(1)}, u32[]{:S(2)}, u32[]{:S(2)}) collective-permute-start(bf16[64,2048]{1,0:T(8,128)(2,1)S(1)} %fusion.1), channel_id=1, source_target_pairs={{0,8},{4,12},{64,72},{68,76},{8,0},{12,4},{72,64},{76,68},{1,9},{5... | collective-permute-start | bytes 786440 | tf_op jit(solution)/shard_map/ppermute | solution.py:79
  127.7 16.0 %collective-permute-start.31 = (bf16[512,1024]{1,0:T(8,128)(2,1)S(1)}, bf16[512,1024]{1,0:T(8,128)(2,1)S(1)}, u32[]{:S(2)}, u32[]{:S(2)}) collective-permute-start(bf16[512,1024]{1,0:T(8,128)(2,1)S(1)} %add_convert_fusion.1), channel_id=1, source_target_pairs={{0,3},{4,5},{64,67},{68,69},{8,11},{12,13},{72,75},{76,77},{1,2},{... | collective-permute-start | bytes 3145736 | tf_op jit(solution)/shard_map/ppermute | solution.py:79
  131.4 1.6 %collective-permute-start.28 = (bf16[64,2048]{1,0:T(8,128)(2,1)S(1)}, bf16[64,2048]{1,0:T(8,128)(2,1)S(1)}, u32[]{:S(2)}, u32[]{:S(2)}) collective-permute-start(bf16[64,2048]{1,0:T(8,128)(2,1)S(1)} %add_convert_fusion.3.refs_0_), channel_id=1, source_target_pairs={{0,4},{4,0},{64,68},{68,64},{8,12},{12,8},{72,76},{76,72},{1,5},{5... | collective-permute-start | bytes 786440 | tf_op jit(solution)/shard_map/ppermute | solution.py:79
  131.6 1.8 %collective-permute-start.29 = (bf16[64,2048]{1,0:T(8,128)(2,1)S(1)}, bf16[64,2048]{1,0:T(8,128)(2,1)S(1)}, u32[]{:S(2)}, u32[]{:S(2)}) collective-permute-start(bf16[64,2048]{1,0:T(8,128)(2,1)S(1)} %add_convert_fusion.2.refs_1_), channel_id=1, source_target_pairs={{0,4},{4,0},{64,68},{68,64},{8,12},{12,8},{72,76},{76,72},{1,5},{5... | collective-permute-start | bytes 786440 | tf_op jit(solution)/shard_map/ppermute | solution.py:79

commit v2 on v1

--- a/solution.py
+++ b/solution.py
@@ -14,6 +14,7 @@
 TN = (((0,), (0,)), ((), ()))
 TILE = 512
 WHOLE = pl.BlockSpec(memory_space=pltpu.VMEM)
+ANY = pl.BlockSpec(memory_space=pl.ANY)
 SCALARS = pl.BlockSpec(memory_space=pltpu.SMEM)
 
 
@@ -205,14 +206,17 @@
     )
 
 
-def share_body(part, keep, first, second, *refs):
-    out, terms, turned, sems = refs[-4:]
-    span = second.shape[1]
+def share_body(part, count, keep, first, *refs):
+    seconds, (out, terms, turned, sems) = refs[:count], refs[-4:]
+    span = turned.shape[0]
     step = TILE // 2
-    sources = (keep.at[:, span:], first.at[:, :span], second)
+    sources = [(keep.at[:, span:], terms.at[0]), (first.at[:, :span], terms.at[1])]
+    for i, second in enumerate(seconds):
+        cols = slice(i * second.shape[1], (i + 1) * second.shape[1])
+        sources.append((second, terms.at[2, :, cols]))
     coming = [
-        pltpu.make_async_copy(source, terms.at[i], sems.at[i])
-        for i, source in enumerate(sources)
+        pltpu.make_async_copy(source, target, sems.at[i])
+        for i, (source, target) in enumerate(sources)
     ]
     for copy in coming:
         copy.start()
@@ -225,30 +229,30 @@
         total = total + terms[2, :, cols].astype(F32)
         turned[cols, :] = total.T.astype(BF16)
         going.append(
-            pltpu.make_async_copy(turned.at[cols, :], out.at[0, part, cols, :], sems.at[3 + i])
+            pltpu.make_async_copy(turned.at[cols, :], out.at[0, part, cols, :], sems.at[4 + i])
         )
         going[-1].start()
     for copy in going:
         copy.wait()
 
 
-def share(part, keep, first, second, into=None):
-    width, span = second.shape
+def share(part, keep, first, seconds, into=None):
+    width, span = keep.shape[0], keep.shape[1] // 2
     given = [] if into is None else [into]
     return pl.pallas_call(
-        functools.partial(share_body, part),
-        in_specs=[pl.BlockSpec(memory_space=pl.ANY)] * (3 + len(given)),
-        out_specs=pl.BlockSpec(memory_space=pl.ANY),
+        functools.partial(share_body, part, len(seconds)),
+        in_specs=[ANY] * (2 + len(seconds) + len(given)),
+        out_specs=ANY,
         out_shape=bf16(1, 2, span, width),
         scratch_shapes=[
             pltpu.VMEM((3, width, span), BF16),
             pltpu.VMEM((span, width), BF16),
-            pltpu.SemaphoreType.DMA((3 + 2 * span // TILE,)),
+            pltpu.SemaphoreType.DMA((4 + 2 * span // TILE,)),
         ],
-        input_output_aliases={3: 0} if given else {},
+        input_output_aliases={2 + len(seconds): 0} if given else {},
         compiler_params=pltpu.CompilerParams(vmem_limit_bytes=40 * 1024 * 1024),
         cost_estimate=LITTLE,
-    )(keep, first, second, *given)
+    )(keep, first, *seconds, *given)
 
 
 def place_body(core, *refs):
@@ -332,6 +336,21 @@
     )
 
 
+def add_body(held, came, stay, out):
+    half = stay.shape[0]
+    for i in range(held.shape[1] // TILE):
+        cols = slice(i * TILE, (i + 1) * TILE)
+        total = held[:, cols].astype(F32) + came[:, cols].astype(F32)
+        stay[:, cols] = total[:half]
+        out[:, cols] = total[half:].astype(BF16)
+
+
+def add(held, came, after=()):
+    rows, span = held.shape
+    shapes = [jax.ShapeDtypeStruct((rows // 2, span), F32), bf16(rows // 2, span)]
+    return call(add_body, [held, came], shapes, after=after, room=6)
+
+
 def tie(array, *others):
     return lax.optimization_barrier((array, *others))[0]
 
@@ -363,19 +382,17 @@
     kv_weight, queries, cotangent = load(kv_weight, queries, cotangent)
     g["a"] = send(tie(h["a"], kv_weight, queries), ALONG_Z)
     h["d"] = send(h["a"], X_SECOND)
-    g["b"] = send(h["b"], ALONG_Z)
+    g["d"] = send(g["a"], X_SECOND)
     h_too["a"] = send(h["a"], SWAP)
     h_too["b"] = send(h["b"], SWAP)
     g_too["o"] = send(g["o"], SWAP)
-    done = [
-        project((h["o"], h_too["o"], h["a"], h_too["a"]), kv_weight),
-        project((g["o"], g_too["o"], h["b"], h_too["b"]), kv_weight),
-    ]
-    g["d"] = send(tie(g["a"], done[0][0], done[1][0]), X_SECOND)
     h_too["d"] = send(h["d"], SWAP)
     g_too["a"] = send(g["a"], SWAP)
-    g_too["b"] = send(g["b"], SWAP)
+    done = [project((h["o"], h_too["o"], h["a"], h_too["a"]), kv_weight)]
+    g["b"] = send(tie(h["b"], g["a"], done[0][0]), ALONG_Z)
+    done.append(project((g["o"], g_too["o"], h["b"], h_too["b"]), kv_weight))
     done.append(project((g["a"], g_too["a"], h["d"], h_too["d"]), kv_weight))
+    g_too["b"] = send(tie(g["b"], done[1][0]), SWAP)
     g_too["d"] = send(tie(g["d"], done[2][0]), SWAP)
     done.append(project((g["b"], g_too["b"], g["d"], g_too["d"]), kv_weight))
     keys, values = zip(*done)
@@ -402,21 +419,22 @@
     value_in = send(value_out, Y_FIRST)
     key_in = send(tie(key_out, value_in), Y_FIRST)
     value_two = send(tie(onward(value_keep, value_in), key_in), Y_SECOND)
-    key_two = send(tie(onward(key_keep, key_in), value_two), Y_SECOND)
-
-    last = []
+    key_two = jnp.split(onward(key_keep, key_in), 2, 1)
+    key_two[0] = send(key_two[0], Y_SECOND)
+    key_two[1] = send(tie(key_two[1], key_two[0]), Y_SECOND)
+
+    mine, theirs = [], []
     for keep, out in zip(kept, x_out):
-        came = send(out, X_FIRST)
-        total = tie(keep, key_keep).astype(F32) + came.astype(F32)
-        came = send(total[2 * half :].astype(BF16), X_SECOND)
-        total = total[: 2 * half] + came.astype(F32)
+        held, going = add(keep, send(out, X_FIRST), (key_keep,))
+        total = held + send(going, X_SECOND).astype(F32)
         here = total[:half] + send(total[half:].astype(BF16), BACK_Z).astype(F32)
         here = here.astype(BF16)
         came = send(here, ACROSS_Z)
-        last.append((tie(here, key_in).astype(F32) + came.astype(F32)).astype(BF16))
-    enc_grad = place(core, last, [send(part, SWAP) for part in last])
-
-    weight_grad = share(1, value_keep, value_in, value_two)
+        mine.append((here.astype(F32) + came.astype(F32)).astype(BF16))
+        theirs.append(send(mine[-1], SWAP))
+    enc_grad = place(core, mine, theirs)
+
+    weight_grad = share(1, value_keep, value_in, [value_two])
     weight_grad = share(0, key_keep, key_in, key_two, weight_grad)
     return (attended, query_grad, enc_grad, weight_grad)
 

time: 146 us -> 143 us (0.979)
  the two profiles are of different devices: /device:TPU:0 before, /device:TPU:62 now
where the time goes in v2:
time: 143 us
  waiting for transfers between devices  63.4 us (44%)
  Pallas kernels  42.3 us (30%)
  starting transfers between devices  29.5 us (21%)
  local copies, waits for them, and re-layouts  4.89 us (3%)
    ppermute x33, waiting for transfers between devices, send(): return lax.ppermute(array, ALL, route)  63.4 us
    pallas_call x16, Pallas kernels, call(): pl.pallas_call(reads, in_specs=[SCALARS] * index + [WHOLE] * (count - ind...  37 us
    ppermute x33, starting transfers between devices, send(): return lax.ppermute(array, ALL, route)  29.5 us
    pallas_call x2, Pallas kernels, share(): pl.pallas_call(functools.partial(share_body, part, len(seconds)), in_spec...  3.64 us
    unnamed x8, local copies, waits for them, and re-layouts  3.39 us
  transfers between devices with their start and end apart: 33, of which 17 were waited for; matrix products, arithmetic and copies ran while one was open for 1% of the time, Pallas kernels for 22%

profile of v2, /device:TPU:62, one launch (start us, length us, event | category | flops | bytes accessed | tf_op | source)
XLA Modules:
  0.0 142.6 jit_solution(14211171949903360012)
XLA Ops:
  0.7 1.4 dynamic-slice_bitcast_fusion
  2.2 0.9 collective-permute-start
  3.0 1.1 collective-permute-start.4
  4.2 1.9 %collective-permute-start.2 = (bf16[64,4096]{1,0:T(8,128)(2,1)S(1)}, bf16[64,4096]{1,0:T(8,128)(2,1)S(1)}, u32[]{:S(2)}, u32[]{:S(2)}) collective-permute-start(bf16[64,4096]{1,0:T(8,128)(2,1)S(1)} %get-tuple-element.47.refs_0_.refs_2_), channel_id=1, source_target_pairs={{0,64},{4,76},{64,8},{68,4},{8,72},{12,68},{72,0},{76,12},{1,65},{... | collective-permute-start | bytes 1572872 | tf_op jit(solution)/shard_map/ppermute | solution.py:80
  6.1 3.4 %copy-done = bf16[1,2,4096,512]{3,2,1,0:T(8,128)(2,1)S(1)} copy-done((bf16[1,2,4096,512]{3,2,1,0:T(8,128)(2,1)S(1)}, bf16[1,2,4096,512]{3,2,1,0:T(8,128)(2,1)}, u32[]{:S(2)}) %copy-start) | copy-done | bytes 8388632
  10.1 5.9 %collective-permute-done.refs_2_.refs_6_ = bf16[64,4096]{1,0:T(8,128)(2,1)S(1)} collective-permute-done((bf16[64,4096]{1,0:T(8,128)(2,1)S(1)}, bf16[64,4096]{1,0:T(8,128)(2,1)S(1)}, u32[]{:S(2)}, u32[]{:S(2)}) %collective-permute-start) | collective-permute-done | bytes 524320 | tf_op jit(solution)/shard_map/ppermute | solution.py:80
  16.0 1.9 %collective-permute-start.6 = (bf16[64,4096]{1,0:T(8,128)(2,1)S(1)}, bf16[64,4096]{1,0:T(8,128)(2,1)S(1)}, u32[]{:S(2)}, u32[]{:S(2)}) collective-permute-start(bf16[64,4096]{1,0:T(8,128)(2,1)S(1)} %collective-permute-done.refs_2_.refs_6_), channel_id=1, source_target_pairs={{0,64},{4,76},{64,8},{68,4},{8,72},{12,68},{72,0},{76,12},{1,65},{... | collective-permute-start | bytes 1572872 | tf_op jit(solution)/shard_map/ppermute | solution.py:80
  18.8 2.3 %shard_map.76 = (bf16[256,512]{1,0:T(8,128)(2,1)S(1)}, bf16[256,512]{1,0:T(8,128)(2,1)S(1)}) custom-call(bf16[64,4096]{1,0:T(8,128)(2,1)S(1)} %get-tuple-element.47.refs_0_.refs_2_, bf16[64,4096]{1,0:T(8,128)(2,1)S(1)} %get-tuple-element.48.refs_1_.refs_10_, bf16[64,4096]{1,0:T(8,128)(2,1)S(1)} %collective-permute-done.refs_2_.refs_6_, ...), custom_call_target="tpu_custom_call" | custom-call | flops 1000 | bytes 1000 | tf_op jit(solution)/shard_map/pallas_call | solution.py:32
  21.1 4.1 %collective-permute-done.6.refs_0_.refs_7_ = bf16[64,4096]{1,0:T(8,128)(2,1)S(1)} collective-permute-done((bf16[64,4096]{1,0:T(8,128)(2,1)S(1)}, bf16[64,4096]{1,0:T(8,128)(2,1)S(1)}, u32[]{:S(2)}, u32[]{:S(2)}) %collective-permute-start.6) | collective-permute-done | bytes 524320 | tf_op jit(solution)/shard_map/ppermute | solution.py:80
  25.2 1.9 %collective-permute-start.10 = (bf16[64,4096]{1,0:T(8,128)(2,1)S(1)}, bf16[64,4096]{1,0:T(8,128)(2,1)S(1)}, u32[]{:S(2)}, u32[]{:S(2)}) collective-permute-start(bf16[64,4096]{1,0:T(8,128)(2,1)S(1)} %collective-permute-done.4.refs_2_.refs_4_), channel_id=1, source_target_pairs={{0,64},{4,76},{64,8},{68,4},{8,72},{12,68},{72,0},{76,12},{1,65},{... | collective-permute-start | bytes 1572872 | tf_op jit(solution)/shard_map/ppermute | solution.py:80
  27.1 1.2 collective-permute-done.8.refs_2_.refs_8_
  29.2 2.3 %shard_map.77 = (bf16[256,512]{1,0:T(8,128)(2,1)S(1)}, bf16[256,512]{1,0:T(8,128)(2,1)S(1)}) custom-call(bf16[64,4096]{1,0:T(8,128)(2,1)S(1)} %collective-permute-done.2.refs_0_.refs_3_, bf16[64,4096]{1,0:T(8,128)(2,1)S(1)} %collective-permute-done.3.refs_1_.refs_11_, bf16[64,4096]{1,0:T(8,128)(2,1)S(1)} %collective-permute-done.4.refs_2_.refs_4_, ...), custom_call_target="tpu_custom_call" | custom-call | flops 1000 | bytes 1000 | tf_op jit(solution)/shard_map/pallas_call | solution.py:32
  31.5 3.0 %collective-permute-done.10.refs_0_.refs_5_ = bf16[64,4096]{1,0:T(8,128)(2,1)S(1)} collective-permute-done((bf16[64,4096]{1,0:T(8,128)(2,1)S(1)}, bf16[64,4096]{1,0:T(8,128)(2,1)S(1)}, u32[]{:S(2)}, u32[]{:S(2)}) %collective-permute-start.10) | collective-permute-done | bytes 524320 | tf_op jit(solution)/shard_map/ppermute | solution.py:80
  34.5 2.3 %shard_map.78 = (bf16[256,512]{1,0:T(8,128)(2,1)S(1)}, bf16[256,512]{1,0:T(8,128)(2,1)S(1)}) custom-call(bf16[64,4096]{1,0:T(8,128)(2,1)S(1)} %collective-permute-done.6.refs_0_.refs_7_, bf16[64,4096]{1,0:T(8,128)(2,1)S(1)} %collective-permute-done.7.refs_1_.refs_15_, bf16[64,4096]{1,0:T(8,128)(2,1)S(1)} %collective-permute-done.8.refs_2_.refs_8_, ...), custom_call_target="tpu_custom_call" | custom-call | flops 1000 | bytes 1000 | tf_op jit(solution)/shard_map/pallas_call | solution.py:32
  36.9 2.4 %collective-permute-done.12.refs_2_.refs_9_ = bf16[64,4096]{1,0:T(8,128)(2,1)S(1)} collective-permute-done((bf16[64,4096]{1,0:T(8,128)(2,1)S(1)}, bf16[64,4096]{1,0:T(8,128)(2,1)S(1)}, u32[]{:S(2)}, u32[]{:S(2)}) %collective-permute-start.12) | collective-permute-done | bytes 524320 | tf_op jit(solution)/shard_map/ppermute | solution.py:80
  39.3 1.9 %collective-permute-done.13.refs_3_.refs_17_ = bf16[64,4096]{1,0:T(8,128)(2,1)S(1)} collective-permute-done((bf16[64,4096]{1,0:T(8,128)(2,1)S(1)}, bf16[64,4096]{1,0:T(8,128)(2,1)S(1)}, u32[]{:S(2)}, u32[]{:S(2)}) %collective-permute-start.13) | collective-permute-done | bytes 524320 | tf_op jit(solution)/shard_map/ppermute | solution.py:80
  41.2 2.3 %shard_map.79 = (bf16[256,512]{1,0:T(8,128)(2,1)S(1)}, bf16[256,512]{1,0:T(8,128)(2,1)S(1)}) custom-call(bf16[64,4096]{1,0:T(8,128)(2,1)S(1)} %collective-permute-done.10.refs_0_.refs_5_, bf16[64,4096]{1,0:T(8,128)(2,1)S(1)} %collective-permute-done.11.refs_1_.refs_13_, bf16[64,4096]{1,0:T(8,128)(2,1)S(1)} %collective-permute-done.12.refs_2_.refs_9_, ...), custom_call_target="tpu_custom_call" | custom-call | flops 1000 | bytes 1000 | tf_op jit(solution)/shard_map/pallas_call | solution.py:32
  43.5 3.6 %shard_map.80 = (bf16[1,1,512,512]{3,2,1,0:T(8,128)(2,1)}, f32[2,512,1024]{2,1,0:T(8,128)S(1)}, bf16[1024,512]{1,0:T(8,128)(2,1)S(1)}, bf16[512,1024]{1,0:T(8,128)(2,1)S(1)}) custom-call(bf16[1,1,512,512]{3,2,1,0:T(8,128)(2,1)S(1)} %get-tuple-element.45.refs_0_, bf16[1,1,512,512]{3,2,1,0:T(8,128)(2,1)S(1)} %get-tuple-element.46.refs_1_, ...), custom_call_target="tpu_custom_call" | custom-call | flops 1000 | bytes 1000 | tf_op jit(solution)/shard_map/pallas_call | solution.py:32
  47.1 2.9 %shard_map.81.refs_12_ = bf16[512,2048]{1,0:T(8,128)(2,1)S(1)} custom-call(s32[4]{0:T(128)S(1)} %get-tuple-element.64.refs_0_, bf16[512,1024]{1,0:T(8,128)(2,1)S(1)} %get-tuple-element.65.refs_1_, bf16[64,4096]{1,0:T(8,128)(2,1)S(1)} %get-tuple-element.47.refs_0_.refs_2_, bf16[64,4096]{1,0:T(8,128)(2,1)S(1)} %collective-permute-done.2.refs_0_.refs_3_, ...), custom_call_target="tpu_custom_call" | custom-call | flops 1000 | bytes 1000 | tf_op jit(solution)/shard_map/pallas_call | solution.py:32
  50.0 0.8 collective-permute-start.28
  50.8 2.6 %shard_map.82 = (bf16[1,1,512,512]{3,2,1,0:T(8,128)(2,1)}, bf16[1024,512]{1,0:T(8,128)(2,1)S(1)}, bf16[512,1024]{1,0:T(8,128)(2,1)S(1)}) custom-call(bf16[1,1,512,512]{3,2,1,0:T(8,128)(2,1)S(1)} %get-tuple-element.45.refs_0_, bf16[1,1,512,512]{3,2,1,0:T(8,128)(2,1)S(1)} %get-tuple-element.46.refs_1_, bf16[256,512]{1,0:T(8,128)(2,1)S(1)} %get-tuple-element.50.refs_2_, ...), custom_call_target="tpu_custom_call" | custom-call | flops 1000 | bytes 1000 | tf_op jit(solution)/shard_map/pallas_call | solution.py:32
  53.4 2.4 %shard_map.85 = (bf16[256,2048]{1,0:T(8,128)(2,1)S(1)}, bf16[256,2048]{1,0:T(8,128)(2,1)S(1)}) custom-call(bf16[1024,512]{1,0:T(8,128)(2,1)S(1)} %get-tuple-element.67.refs_0_, bf16[1024,512]{1,0:T(8,128)(2,1)S(1)} %get-tuple-element.68.refs_1_, bf16[1,2,4096,512]{3,2,1,0:T(8,128)(2,1)S(1)} %get-tuple-element.49.refs_4_.refs_2_), custom_call_target="tpu_custom_call" | custom-call | flops 1000 | bytes 1000 | tf_op jit(solution)/shard_map/pallas_call | solution.py:32
  56.3 2.4 %shard_map.83 = (bf16[256,2048]{1,0:T(8,128)(2,1)S(1)}, bf16[256,2048]{1,0:T(8,128)(2,1)S(1)}) custom-call(bf16[1024,512]{1,0:T(8,128)(2,1)S(1)} %get-tuple-element.67.refs_0_, bf16[1024,512]{1,0:T(8,128)(2,1)S(1)} %get-tuple-element.68.refs_1_, bf16[1,2,4096,512]{3,2,1,0:T(8,128)(2,1)S(1)} %get-tuple-element.49.refs_4_.refs_2_), custom_call_target="tpu_custom_call" | custom-call | flops 1000 | bytes 1000 | tf_op jit(solution)/shard_map/pallas_call | solution.py:32
  60.0 2.4 %shard_map.86 = (bf16[256,2048]{1,0:T(8,128)(2,1)S(1)}, bf16[256,2048]{1,0:T(8,128)(2,1)S(1)}) custom-call(bf16[1024,512]{1,0:T(8,128)(2,1)S(1)} %get-tuple-element.67.refs_0_, bf16[1024,512]{1,0:T(8,128)(2,1)S(1)} %get-tuple-element.68.refs_1_, bf16[1,2,4096,512]{3,2,1,0:T(8,128)(2,1)S(1)} %get-tuple-element.49.refs_4_.refs_2_, ...), custom_call_target="tpu_custom_call" | custom-call | flops 1000 | bytes 1000 | tf_op jit(solution)/shard_map/pallas_call | solution.py:32
  63.0 2.4 %shard_map.84 = (bf16[256,2048]{1,0:T(8,128)(2,1)S(1)}, bf16[256,2048]{1,0:T(8,128)(2,1)S(1)}) custom-call(bf16[1024,512]{1,0:T(8,128)(2,1)S(1)} %get-tuple-element.67.refs_0_, bf16[1024,512]{1,0:T(8,128)(2,1)S(1)} %get-tuple-element.68.refs_1_, bf16[1,2,4096,512]{3,2,1,0:T(8,128)(2,1)S(1)} %get-tuple-element.49.refs_4_.refs_2_, ...), custom_call_target="tpu_custom_call" | custom-call | flops 1000 | bytes 1000 | tf_op jit(solution)/shard_map/pallas_call | solution.py:32
  65.4 1.6 %collective-permute-start.16 = (bf16[256,2048]{1,0:T(8,128)(2,1)S(1)}, bf16[256,2048]{1,0:T(8,128)(2,1)S(1)}, u32[]{:S(2)}, u32[]{:S(2)}) collective-permute-start(bf16[256,2048]{1,0:T(8,128)(2,1)S(1)} %get-tuple-element.72.refs_18_), channel_id=1, source_target_pairs={{0,16},{4,52},{64,80},{68,116},{8,24},{12,60},{72,88},{76,124},{1,... | collective-permute-start | bytes 3145736 | tf_op jit(solution)/shard_map/ppermute | solution.py:80
  66.9 2.9 %shard_map.87.refs_18_ = bf16[512,2048]{1,0:T(8,128)(2,1)S(1)} custom-call(s32[4]{0:T(128)S(1)} %get-tuple-element.64.refs_0_, bf16[512,1024]{1,0:T(8,128)(2,1)S(1)} %get-tuple-element.74.refs_1_, bf16[64,4096]{1,0:T(8,128)(2,1)S(1)} %get-tuple-element.47.refs_0_.refs_2_, bf16[64,4096]{1,0:T(8,128)(2,1)S(1)} %collective-permute-done.2.refs_0_.refs_3_, ...), custom_call_target="tpu_custom_call" | custom-call | flops 1000 | bytes 1000 | tf_op jit(solution)/shard_map/pallas_call | solution.py:32
  69.9 6.2 %collective-permute-done.28.first = bf16[512,2048]{1,0:T(8,128)(2,1)S(1)} collective-permute-done((bf16[512,2048]{1,0:T(8,128)(2,1)S(1)}, bf16[512,2048]{1,0:T(8,128)(2,1)S(1)}, u32[]{:S(2)}, u32[]{:S(2)}) %collective-permute-start.28) | collective-permute-done | bytes 2097184 | tf_op jit(solution)/shard_map/ppermute | solution.py:80
  76.1 0.7 collective-permute-start.29
  76.8 2.9 %shard_map.88.refs_18_.keep = bf16[512,2048]{1,0:T(8,128)(2,1)S(1)} custom-call(s32[4]{0:T(128)S(1)} %get-tuple-element.73.refs_0_, bf16[512,1024]{1,0:T(8,128)(2,1)S(1)} %get-tuple-element.65.refs_1_, bf16[64,4096]{1,0:T(8,128)(2,1)S(1)} %get-tuple-element.47.refs_0_.refs_2_, bf16[64,4096]{1,0:T(8,128)(2,1)S(1)} %collective-permute-done.2.refs_0_.refs_3_, ...), custom_call_target="tpu_custom_call" | custom-call | flops 1000 | bytes 1000 | tf_op jit(solution)/shard_map/pallas_call | solution.py:32
  79.7 2.9 %shard_map.89.refs_2_.keep = bf16[512,2048]{1,0:T(8,128)(2,1)S(1)} custom-call(s32[4]{0:T(128)S(1)} %get-tuple-element.73.refs_0_, bf16[512,1024]{1,0:T(8,128)(2,1)S(1)} %get-tuple-element.74.refs_1_, bf16[64,4096]{1,0:T(8,128)(2,1)S(1)} %get-tuple-element.47.refs_0_.refs_2_, bf16[64,4096]{1,0:T(8,128)(2,1)S(1)} %collective-permute-done.2.refs_0_.refs_3_, ...), custom_call_target="tpu_custom_call" | custom-call | flops 1000 | bytes 1000 | tf_op jit(solution)/shard_map/pallas_call | solution.py:32
  83.3 8.6 %collective-permute-done.16.refs_1_ = bf16[256,2048]{1,0:T(8,128)(2,1)S(1)} collective-permute-done((bf16[256,2048]{1,0:T(8,128)(2,1)S(1)}, bf16[256,2048]{1,0:T(8,128)(2,1)S(1)}, u32[]{:S(2)}, u32[]{:S(2)}) %collective-permute-start.16) | collective-permute-done | bytes 1048608 | tf_op jit(solution)/shard_map/ppermute | solution.py:80
  92.8 1.7 %collective-permute-done.23 = bf16[128,2048]{1,0:T(8,128)(2,1)S(1)} collective-permute-done((bf16[128,2048]{1,0:T(8,128)(2,1)S(1)}, bf16[128,2048]{1,0:T(8,128)(2,1)S(1)}, u32[]{:S(2)}, u32[]{:S(2)}) %collective-permute-start.23) | collective-permute-done | bytes 524320 | tf_op jit(solution)/shard_map/ppermute | solution.py:80
  94.6 1.3 collective-permute-start.24
  95.9 6.6 %collective-permute-done.19 = bf16[128,2048]{1,0:T(8,128)(2,1)S(1)} collective-permute-done((bf16[128,2048]{1,0:T(8,128)(2,1)S(1)}, bf16[128,2048]{1,0:T(8,128)(2,1)S(1)}, u32[]{:S(2)}, u32[]{:S(2)}) %collective-permute-start.19) | collective-permute-done | bytes 524320 | tf_op jit(solution)/shard_map/ppermute | solution.py:80
  102.7 1.0 collective-permute-start.20
  103.8 2.2 %collective-permute-start.25 = (bf16[64,2048]{1,0:T(8,128)(2,1)S(1)}, bf16[64,2048]{1,0:T(8,128)(2,1)S(1)}, u32[]{:S(2)}, u32[]{:S(2)}) collective-permute-start(bf16[64,2048]{1,0:T(8,128)(2,1)S(1)} %fusion), channel_id=1, source_target_pairs={{0,8},{4,12},{64,72},{68,76},{8,0},{12,4},{72,64},{76,68},{1,9},{5... | collective-permute-start | bytes 786440 | tf_op jit(solution)/shard_map/ppermute | solution.py:80
  106.4 1.1 collective-permute-start.30
  107.5 5.4 %collective-permute-done.20 = bf16[64,2048]{1,0:T(8,128)(2,1)S(1)} collective-permute-done((bf16[64,2048]{1,0:T(8,128)(2,1)S(1)}, bf16[64,2048]{1,0:T(8,128)(2,1)S(1)}, u32[]{:S(2)}, u32[]{:S(2)}) %collective-permute-start.20) | collective-permute-done | bytes 262176 | tf_op jit(solution)/shard_map/ppermute | solution.py:80
  112.9 6.0 %collective-permute-start.21 = (bf16[64,2048]{1,0:T(8,128)(2,1)S(1)}, bf16[64,2048]{1,0:T(8,128)(2,1)S(1)}, u32[]{:S(2)}, u32[]{:S(2)}) collective-permute-start(bf16[64,2048]{1,0:T(8,128)(2,1)S(1)} %fusion.1), channel_id=1, source_target_pairs={{0,8},{4,12},{64,72},{68,76},{8,0},{12,4},{72,64},{76,68},{1,9},{5... | collective-permute-start | bytes 786440 | tf_op jit(solution)/shard_map/ppermute | solution.py:80
  119.1 3.3 %collective-permute-start.31 = (bf16[512,512]{1,0:T(8,128)(2,1)S(1)}, bf16[512,512]{1,0:T(8,128)(2,1)S(1)}, u32[]{:S(2)}, u32[]{:S(2)}) collective-permute-start(bf16[512,512]{1,0:T(8,128)(2,1)S(1)} %get-tuple-element.84), channel_id=1, source_target_pairs={{0,3},{4,5},{64,67},{68,69},{8,11},{12,13},{72,75},{76,77},{1,2},{... | collective-permute-start | bytes 1572872 | tf_op jit(solution)/shard_map/ppermute | solution.py:80
  122.4 0.9 collective-permute-done.21
  123.5 1.5 %collective-permute-done.26.refs_2_ = bf16[64,2048]{1,0:T(8,128)(2,1)S(1)} collective-permute-done((bf16[64,2048]{1,0:T(8,128)(2,1)S(1)}, bf16[64,2048]{1,0:T(8,128)(2,1)S(1)}, u32[]{:S(2)}, u32[]{:S(2)}) %collective-permute-start.26) | collective-permute-done | bytes 262176 | tf_op jit(solution)/shard_map/ppermute | solution.py:80
  125.0 1.0 shard_map.92
  126.0 9.0 %collective-permute-done.32.refs_0_ = bf16[512,1024]{1,0:T(8,128)(2,1)S(1)} collective-permute-done((bf16[512,1024]{1,0:T(8,128)(2,1)S(1)}, bf16[512,1024]{1,0:T(8,128)(2,1)S(1)}, u32[]{:S(2)}, u32[]{:S(2)}) %collective-permute-start.32) | collective-permute-done | bytes 1048608 | tf_op jit(solution)/shard_map/ppermute | solution.py:80
  134.9 1.8 %shard_map.93.refs_2_ = bf16[1,2,1024,512]{3,2,1,0:T(8,128)(2,1)} custom-call(bf16[512,2048]{1,0:T(8,128)(2,1)S(1)} %shard_map.88.refs_18_.keep, bf16[512,2048]{1,0:T(8,128)(2,1)S(1)} %collective-permute-done.28.first, bf16[512,1024]{1,0:T(8,128)(2,1)S(1)} %collective-permute-done.32.refs_0_), custom_call_target="tpu_custom_call" | custom-call | flops 1000 | bytes 1000 | tf_op jit(solution)/shard_map/pallas_call | solution.py:242
  136.7 3.8 %collective-permute-done.31.refs_1_ = bf16[512,512]{1,0:T(8,128)(2,1)S(1)} collective-permute-done((bf16[512,512]{1,0:T(8,128)(2,1)S(1)}, bf16[512,512]{1,0:T(8,128)(2,1)S(1)}, u32[]{:S(2)}, u32[]{:S(2)}) %collective-permute-start.31) | collective-permute-done | bytes 524320 | tf_op jit(solution)/shard_map/ppermute | solution.py:80
  140.6 1.9 %shard_map.94 = bf16[1,2,1024,512]{3,2,1,0:T(8,128)(2,1)} custom-call(bf16[512,2048]{1,0:T(8,128)(2,1)S(1)} %shard_map.89.refs_2_.keep, bf16[512,2048]{1,0:T(8,128)(2,1)S(1)} %collective-permute-done.29.first, bf16[512,512]{1,0:T(8,128)(2,1)S(1)} %collective-permute-done.30.refs_0_, ...), custom_call_target="tpu_custom_call", output_to_operand_aliasing={{}: (4, {})} | custom-call | flops 1000 | bytes 1000 | tf_op jit(solution)/shard_map/pallas_call | solution.py:242
  (59 shorter events, 7.6 us)
Async XLA Ops:
  0.6 5.4 %copy-start.2 = (bf16[1,1,512,512]{3,2,1,0:T(8,128)(2,1)S(1)}, bf16[1,1,512,512]{3,2,1,0:T(8,128)(2,1)}, u32[]{:S(2)}) copy-start(bf16[1,1,512,512]{3,2,1,0:T(8,128)(2,1)} %refs_2_.1) | copy-start | bytes 1572868
  0.6 5.4 %copy-start.1 = (bf16[1,1,512,512]{3,2,1,0:T(8,128)(2,1)S(1)}, bf16[1,1,512,512]{3,2,1,0:T(8,128)(2,1)}, u32[]{:S(2)}) copy-start(bf16[1,1,512,512]{3,2,1,0:T(8,128)(2,1)} %refs_1_.1) | copy-start | bytes 1572868
  2.2 13.9 %collective-permute-start = (bf16[64,4096]{1,0:T(8,128)(2,1)S(1)}, bf16[64,4096]{1,0:T(8,128)(2,1)S(1)}, u32[]{:S(2)}, u32[]{:S(2)}) collective-permute-start(bf16[64,4096]{1,0:T(8,128)(2,1)S(1)} %get-tuple-element.47.refs_0_.refs_2_), channel_id=1, source_target_pairs={{0,16},{4,52},{64,80},{68,116},{8,24},{12,60},{72,88},{76,124},{1,... | collective-permute-start | bytes 1572872 | tf_op jit(solution)/shard_map/ppermute | solution.py:80
  3.0 15.2 %collective-permute-start.4 = (bf16[64,4096]{1,0:T(8,128)(2,1)S(1)}, bf16[64,4096]{1,0:T(8,128)(2,1)S(1)}, u32[]{:S(2)}, u32[]{:S(2)}) collective-permute-start(bf16[64,4096]{1,0:T(8,128)(2,1)S(1)} %get-tuple-element.47.refs_0_.refs_2_), channel_id=1, source_target_pairs={{0,48},{4,20},{64,112},{68,84},{8,56},{12,28},{72,120},{76,92},{1,... | collective-permute-start | bytes 1572872 | tf_op jit(solution)/shard_map/ppermute | solution.py:80
  4.2 14.1 %collective-permute-start.2 = (bf16[64,4096]{1,0:T(8,128)(2,1)S(1)}, bf16[64,4096]{1,0:T(8,128)(2,1)S(1)}, u32[]{:S(2)}, u32[]{:S(2)}) collective-permute-start(bf16[64,4096]{1,0:T(8,128)(2,1)S(1)} %get-tuple-element.47.refs_0_.refs_2_), channel_id=1, source_target_pairs={{0,64},{4,76},{64,8},{68,4},{8,72},{12,68},{72,0},{76,12},{1,65},{... | collective-permute-start | bytes 1572872 | tf_op jit(solution)/shard_map/ppermute | solution.py:80
  6.1 3.4 %copy-start = (bf16[1,2,4096,512]{3,2,1,0:T(8,128)(2,1)S(1)}, bf16[1,2,4096,512]{3,2,1,0:T(8,128)(2,1)}, u32[]{:S(2)}) copy-start(bf16[1,2,4096,512]{3,2,1,0:T(8,128)(2,1)} %refs_0_.1) | copy-start | bytes 25165828
  16.0 2.7 %collective-permute-start.1 = (bf16[64,4096]{1,0:T(8,128)(2,1)S(1)}, bf16[64,4096]{1,0:T(8,128)(2,1)S(1)}, u32[]{:S(2)}, u32[]{:S(2)}) collective-permute-start(bf16[64,4096]{1,0:T(8,128)(2,1)S(1)} %collective-permute-done.refs_2_.refs_6_), channel_id=1, source_target_pairs={{0,4},{4,0},{64,68},{68,64},{8,12},{12,8},{72,76},{76,72},{1,5},{5... | collective-permute-start | bytes 1572872 | tf_op jit(solution)/shard_map/ppermute | solution.py:80
  16.0 9.2 %collective-permute-start.6 = (bf16[64,4096]{1,0:T(8,128)(2,1)S(1)}, bf16[64,4096]{1,0:T(8,128)(2,1)S(1)}, u32[]{:S(2)}, u32[]{:S(2)}) collective-permute-start(bf16[64,4096]{1,0:T(8,128)(2,1)S(1)} %collective-permute-done.refs_2_.refs_6_), channel_id=1, source_target_pairs={{0,64},{4,76},{64,8},{68,4},{8,72},{12,68},{72,0},{76,12},{1,65},{... | collective-permute-start | bytes 1572872 | tf_op jit(solution)/shard_map/ppermute | solution.py:80
  18.0 10.4 %collective-permute-start.8 = (bf16[64,4096]{1,0:T(8,128)(2,1)S(1)}, bf16[64,4096]{1,0:T(8,128)(2,1)S(1)}, u32[]{:S(2)}, u32[]{:S(2)}) collective-permute-start(bf16[64,4096]{1,0:T(8,128)(2,1)S(1)} %collective-permute-done.refs_2_.refs_6_), channel_id=1, source_target_pairs={{0,48},{4,20},{64,112},{68,84},{8,56},{12,28},{72,120},{76,92},{1,... | collective-permute-start | bytes 1572872 | tf_op jit(solution)/shard_map/ppermute | solution.py:80
  18.3 10.6 %collective-permute-start.5 = (bf16[64,4096]{1,0:T(8,128)(2,1)S(1)}, bf16[64,4096]{1,0:T(8,128)(2,1)S(1)}, u32[]{:S(2)}, u32[]{:S(2)}) collective-permute-start(bf16[64,4096]{1,0:T(8,128)(2,1)S(1)} %collective-permute-done.4.refs_2_.refs_4_), channel_id=1, source_target_pairs={{0,4},{4,0},{64,68},{68,64},{8,12},{12,8},{72,76},{76,72},{1,5},{5... | collective-permute-start | bytes 1572872 | tf_op jit(solution)/shard_map/ppermute | solution.py:80
  18.3 10.9 %collective-permute-start.3 = (bf16[64,4096]{1,0:T(8,128)(2,1)S(1)}, bf16[64,4096]{1,0:T(8,128)(2,1)S(1)}, u32[]{:S(2)}, u32[]{:S(2)}) collective-permute-start(bf16[64,4096]{1,0:T(8,128)(2,1)S(1)} %collective-permute-done.2.refs_0_.refs_3_), channel_id=1, source_target_pairs={{0,4},{4,0},{64,68},{68,64},{8,12},{12,8},{72,76},{76,72},{1,5},{5... | collective-permute-start | bytes 1572872 | tf_op jit(solution)/shard_map/ppermute | solution.py:80
  25.2 9.3 %collective-permute-start.10 = (bf16[64,4096]{1,0:T(8,128)(2,1)S(1)}, bf16[64,4096]{1,0:T(8,128)(2,1)S(1)}, u32[]{:S(2)}, u32[]{:S(2)}) collective-permute-start(bf16[64,4096]{1,0:T(8,128)(2,1)S(1)} %collective-permute-done.4.refs_2_.refs_4_), channel_id=1, source_target_pairs={{0,64},{4,76},{64,8},{68,4},{8,72},{12,68},{72,0},{76,12},{1,65},{... | collective-permute-start | bytes 1572872 | tf_op jit(solution)/shard_map/ppermute | solution.py:80
  28.4 6.2 %collective-permute-start.9 = (bf16[64,4096]{1,0:T(8,128)(2,1)S(1)}, bf16[64,4096]{1,0:T(8,128)(2,1)S(1)}, u32[]{:S(2)}, u32[]{:S(2)}) collective-permute-start(bf16[64,4096]{1,0:T(8,128)(2,1)S(1)} %collective-permute-done.8.refs_2_.refs_8_), channel_id=1, source_target_pairs={{0,4},{4,0},{64,68},{68,64},{8,12},{12,8},{72,76},{76,72},{1,5},{5... | collective-permute-start | bytes 1572872 | tf_op jit(solution)/shard_map/ppermute | solution.py:80
  28.4 6.2 %collective-permute-start.7 = (bf16[64,4096]{1,0:T(8,128)(2,1)S(1)}, bf16[64,4096]{1,0:T(8,128)(2,1)S(1)}, u32[]{:S(2)}, u32[]{:S(2)}) collective-permute-start(bf16[64,4096]{1,0:T(8,128)(2,1)S(1)} %collective-permute-done.6.refs_0_.refs_7_), channel_id=1, source_target_pairs={{0,4},{4,0},{64,68},{68,64},{8,12},{12,8},{72,76},{76,72},{1,5},{5... | collective-permute-start | bytes 1572872 | tf_op jit(solution)/shard_map/ppermute | solution.py:80
  28.9 10.4 %collective-permute-start.12 = (bf16[64,4096]{1,0:T(8,128)(2,1)S(1)}, bf16[64,4096]{1,0:T(8,128)(2,1)S(1)}, u32[]{:S(2)}, u32[]{:S(2)}) collective-permute-start(bf16[64,4096]{1,0:T(8,128)(2,1)S(1)} %collective-permute-done.6.refs_0_.refs_7_), channel_id=1, source_target_pairs={{0,48},{4,20},{64,112},{68,84},{8,56},{12,28},{72,120},{76,92},{1,... | collective-permute-start | bytes 1572872 | tf_op jit(solution)/shard_map/ppermute | solution.py:80
  34.5 4.8 %collective-permute-start.11 = (bf16[64,4096]{1,0:T(8,128)(2,1)S(1)}, bf16[64,4096]{1,0:T(8,128)(2,1)S(1)}, u32[]{:S(2)}, u32[]{:S(2)}) collective-permute-start(bf16[64,4096]{1,0:T(8,128)(2,1)S(1)} %collective-permute-done.10.refs_0_.refs_5_), channel_id=1, source_target_pairs={{0,4},{4,0},{64,68},{68,64},{8,12},{12,8},{72,76},{76,72},{1,5},{5... | collective-permute-start | bytes 1572872 | tf_op jit(solution)/shard_map/ppermute | solution.py:80
  39.3 1.9 %collective-permute-start.13 = (bf16[64,4096]{1,0:T(8,128)(2,1)S(1)}, bf16[64,4096]{1,0:T(8,128)(2,1)S(1)}, u32[]{:S(2)}, u32[]{:S(2)}) collective-permute-start(bf16[64,4096]{1,0:T(8,128)(2,1)S(1)} %collective-permute-done.12.refs_2_.refs_9_), channel_id=1, source_target_pairs={{0,4},{4,0},{64,68},{68,64},{8,12},{12,8},{72,76},{76,72},{1,5},{5... | collective-permute-start | bytes 1572872 | tf_op jit(solution)/shard_map/ppermute | solution.py:80
  47.1 3.7 %copy-start.3 = (bf16[1,1,512,512]{3,2,1,0:T(8,128)(2,1)S(1)}, bf16[1,1,512,512]{3,2,1,0:T(8,128)(2,1)}, u32[]{:S(2)}) copy-start(bf16[1,1,512,512]{3,2,1,0:T(8,128)(2,1)} %get-tuple-element.41.refs_10_) | copy-start | bytes 1572868
  50.0 26.1 %collective-permute-start.28 = (bf16[512,2048]{1,0:T(8,128)(2,1)S(1)}, bf16[512,2048]{1,0:T(8,128)(2,1)S(1)}, u32[]{:S(2)}, u32[]{:S(2)}) collective-permute-start(bf16[512,2048]{1,0:T(8,128)(2,1)S(1)} %shard_map.81.refs_12_), channel_id=1, source_target_pairs={{0,1},{4,7},{64,65},{68,71},{8,9},{12,15},{72,73},{76,79},{1,0},{5... | collective-permute-start | bytes 6291464 | tf_op jit(solution)/shard_map/ppermute | solution.py:80
  55.7 3.6 %collective-permute-start.17 = (bf16[256,2048]{1,0:T(8,128)(2,1)S(1)}, bf16[256,2048]{1,0:T(8,128)(2,1)S(1)}, u32[]{:S(2)}, u32[]{:S(2)}) collective-permute-start(bf16[256,2048]{1,0:T(8,128)(2,1)S(1)} %get-tuple-element.75), channel_id=1, source_target_pairs={{0,4},{4,0},{64,68},{68,64},{8,12},{12,8},{72,76},{76,72},{1,5},{5... | collective-permute-start | bytes 3145736 | tf_op jit(solution)/shard_map/ppermute | solution.py:80
  55.8 4.1 %collective-permute-start.18 = (bf16[256,2048]{1,0:T(8,128)(2,1)S(1)}, bf16[256,2048]{1,0:T(8,128)(2,1)S(1)}, u32[]{:S(2)}, u32[]{:S(2)}) collective-permute-start(bf16[256,2048]{1,0:T(8,128)(2,1)S(1)} %get-tuple-element.76), channel_id=1, source_target_pairs={{0,4},{4,0},{64,68},{68,64},{8,12},{12,8},{72,76},{76,72},{1,5},{5... | collective-permute-start | bytes 3145736 | tf_op jit(solution)/shard_map/ppermute | solution.py:80
  58.7 3.7 %collective-permute-start.14 = (bf16[256,2048]{1,0:T(8,128)(2,1)S(1)}, bf16[256,2048]{1,0:T(8,128)(2,1)S(1)}, u32[]{:S(2)}, u32[]{:S(2)}) collective-permute-start(bf16[256,2048]{1,0:T(8,128)(2,1)S(1)} %get-tuple-element.69), channel_id=1, source_target_pairs={{0,4},{4,0},{64,68},{68,64},{8,12},{12,8},{72,76},{76,72},{1,5},{5... | collective-permute-start | bytes 3145736 | tf_op jit(solution)/shard_map/ppermute | solution.py:80
  58.9 4.1 %collective-permute-start.15 = (bf16[256,2048]{1,0:T(8,128)(2,1)S(1)}, bf16[256,2048]{1,0:T(8,128)(2,1)S(1)}, u32[]{:S(2)}, u32[]{:S(2)}) collective-permute-start(bf16[256,2048]{1,0:T(8,128)(2,1)S(1)} %get-tuple-element.70), channel_id=1, source_target_pairs={{0,4},{4,0},{64,68},{68,64},{8,12},{12,8},{72,76},{76,72},{1,5},{5... | collective-permute-start | bytes 3145736 | tf_op jit(solution)/shard_map/ppermute | solution.py:80
  62.3 20.3 %collective-permute-start.22 = (bf16[256,2048]{1,0:T(8,128)(2,1)S(1)}, bf16[256,2048]{1,0:T(8,128)(2,1)S(1)}, u32[]{:S(2)}, u32[]{:S(2)}) collective-permute-start(bf16[256,2048]{1,0:T(8,128)(2,1)S(1)} %get-tuple-element.77.refs_19_), channel_id=1, source_target_pairs={{0,16},{4,52},{64,80},{68,116},{8,24},{12,60},{72,88},{76,124},{1,... | collective-permute-start | bytes 3145736 | tf_op jit(solution)/shard_map/ppermute | solution.py:80
  65.4 26.4 %collective-permute-start.16 = (bf16[256,2048]{1,0:T(8,128)(2,1)S(1)}, bf16[256,2048]{1,0:T(8,128)(2,1)S(1)}, u32[]{:S(2)}, u32[]{:S(2)}) collective-permute-start(bf16[256,2048]{1,0:T(8,128)(2,1)S(1)} %get-tuple-element.72.refs_18_), channel_id=1, source_target_pairs={{0,16},{4,52},{64,80},{68,116},{8,24},{12,60},{72,88},{76,124},{1,... | collective-permute-start | bytes 3145736 | tf_op jit(solution)/shard_map/ppermute | solution.py:80
  76.1 29.9 %collective-permute-start.29 = (bf16[512,2048]{1,0:T(8,128)(2,1)S(1)}, bf16[512,2048]{1,0:T(8,128)(2,1)S(1)}, u32[]{:S(2)}, u32[]{:S(2)}) collective-permute-start(bf16[512,2048]{1,0:T(8,128)(2,1)S(1)} %shard_map.87.refs_18_), channel_id=1, source_target_pairs={{0,1},{4,7},{64,65},{68,71},{8,9},{12,15},{72,73},{76,79},{1,0},{5... | collective-permute-start | bytes 6291464 | tf_op jit(solution)/shard_map/ppermute | solution.py:80
  82.9 11.6 %collective-permute-start.23 = (bf16[128,2048]{1,0:T(8,128)(2,1)S(1)}, bf16[128,2048]{1,0:T(8,128)(2,1)S(1)}, u32[]{:S(2)}, u32[]{:S(2)}) collective-permute-start(bf16[128,2048]{1,0:T(8,128)(2,1)S(1)} %get-tuple-element.82), channel_id=1, source_target_pairs={{0,48},{4,20},{64,112},{68,84},{8,56},{12,28},{72,120},{76,92},{1,... | collective-permute-start | bytes 1572872 | tf_op jit(solution)/shard_map/ppermute | solution.py:80
  92.0 10.5 %collective-permute-start.19 = (bf16[128,2048]{1,0:T(8,128)(2,1)S(1)}, bf16[128,2048]{1,0:T(8,128)(2,1)S(1)}, u32[]{:S(2)}, u32[]{:S(2)}) collective-permute-start(bf16[128,2048]{1,0:T(8,128)(2,1)S(1)} %get-tuple-element.79), channel_id=1, source_target_pairs={{0,48},{4,20},{64,112},{68,84},{8,56},{12,28},{72,120},{76,92},{1,... | collective-permute-start | bytes 1572872 | tf_op jit(solution)/shard_map/ppermute | solution.py:80
  94.6 9.1 %collective-permute-start.24 = (bf16[64,2048]{1,0:T(8,128)(2,1)S(1)}, bf16[64,2048]{1,0:T(8,128)(2,1)S(1)}, u32[]{:S(2)}, u32[]{:S(2)}) collective-permute-start(bf16[64,2048]{1,0:T(8,128)(2,1)S(1)} %slice.54), channel_id=1, source_target_pairs={{0,72},{4,68},{64,0},{68,12},{8,64},{12,76},{72,8},{76,4},{1,73},{... | collective-permute-start | bytes 786440 | tf_op jit(solution)/shard_map/ppermute | solution.py:80
  102.7 10.2 %collective-permute-start.20 = (bf16[64,2048]{1,0:T(8,128)(2,1)S(1)}, bf16[64,2048]{1,0:T(8,128)(2,1)S(1)}, u32[]{:S(2)}, u32[]{:S(2)}) collective-permute-start(bf16[64,2048]{1,0:T(8,128)(2,1)S(1)} %slice.55), channel_id=1, source_target_pairs={{0,72},{4,68},{64,0},{68,12},{8,64},{12,76},{72,8},{76,4},{1,73},{... | collective-permute-start | bytes 786440 | tf_op jit(solution)/shard_map/ppermute | solution.py:80
  103.8 15.2 %collective-permute-start.25 = (bf16[64,2048]{1,0:T(8,128)(2,1)S(1)}, bf16[64,2048]{1,0:T(8,128)(2,1)S(1)}, u32[]{:S(2)}, u32[]{:S(2)}) collective-permute-start(bf16[64,2048]{1,0:T(8,128)(2,1)S(1)} %fusion), channel_id=1, source_target_pairs={{0,8},{4,12},{64,72},{68,76},{8,0},{12,4},{72,64},{76,68},{1,9},{5... | collective-permute-start | bytes 786440 | tf_op jit(solution)/shard_map/ppermute | solution.py:80
  106.4 12.7 %collective-permute-start.30 = (bf16[512,512]{1,0:T(8,128)(2,1)S(1)}, bf16[512,512]{1,0:T(8,128)(2,1)S(1)}, u32[]{:S(2)}, u32[]{:S(2)}) collective-permute-start(bf16[512,512]{1,0:T(8,128)(2,1)S(1)} %get-tuple-element.87), channel_id=1, source_target_pairs={{0,3},{4,5},{64,67},{68,69},{8,11},{12,13},{72,75},{76,77},{1,2},{... | collective-permute-start | bytes 1572872 | tf_op jit(solution)/shard_map/ppermute | solution.py:80
  112.9 10.3 %collective-permute-start.21 = (bf16[64,2048]{1,0:T(8,128)(2,1)S(1)}, bf16[64,2048]{1,0:T(8,128)(2,1)S(1)}, u32[]{:S(2)}, u32[]{:S(2)}) collective-permute-start(bf16[64,2048]{1,0:T(8,128)(2,1)S(1)} %fusion.1), channel_id=1, source_target_pairs={{0,8},{4,12},{64,72},{68,76},{8,0},{12,4},{72,64},{76,68},{1,9},{5... | collective-permute-start | bytes 786440 | tf_op jit(solution)/shard_map/ppermute | solution.py:80
  118.9 16.0 %collective-permute-start.32 = (bf16[512,1024]{1,0:T(8,128)(2,1)S(1)}, bf16[512,1024]{1,0:T(8,128)(2,1)S(1)}, u32[]{:S(2)}, u32[]{:S(2)}) collective-permute-start(bf16[512,1024]{1,0:T(8,128)(2,1)S(1)} %add_convert_fusion), channel_id=1, source_target_pairs={{0,3},{4,5},{64,67},{68,69},{8,11},{12,13},{72,75},{76,77},{1,2},{... | collective-permute-start | bytes 3145736 | tf_op jit(solution)/shard_map/ppermute | solution.py:80
  119.0 4.4 %collective-permute-start.27 = (bf16[64,2048]{1,0:T(8,128)(2,1)S(1)}, bf16[64,2048]{1,0:T(8,128)(2,1)S(1)}, u32[]{:S(2)}, u32[]{:S(2)}) collective-permute-start(bf16[64,2048]{1,0:T(8,128)(2,1)S(1)} %add_convert_fusion.2.refs_1_), channel_id=1, source_target_pairs={{0,4},{4,0},{64,68},{68,64},{8,12},{12,8},{72,76},{76,72},{1,5},{5... | collective-permute-start | bytes 786440 | tf_op jit(solution)/shard_map/ppermute | solution.py:80
  119.1 21.4 %collective-permute-start.31 = (bf16[512,512]{1,0:T(8,128)(2,1)S(1)}, bf16[512,512]{1,0:T(8,128)(2,1)S(1)}, u32[]{:S(2)}, u32[]{:S(2)}) collective-permute-start(bf16[512,512]{1,0:T(8,128)(2,1)S(1)} %get-tuple-element.84), channel_id=1, source_target_pairs={{0,3},{4,5},{64,67},{68,69},{8,11},{12,13},{72,75},{76,77},{1,2},{... | collective-permute-start | bytes 1572872 | tf_op jit(solution)/shard_map/ppermute | solution.py:80
  123.4 1.6 %collective-permute-start.26 = (bf16[64,2048]{1,0:T(8,128)(2,1)S(1)}, bf16[64,2048]{1,0:T(8,128)(2,1)S(1)}, u32[]{:S(2)}, u32[]{:S(2)}) collective-permute-start(bf16[64,2048]{1,0:T(8,128)(2,1)S(1)} %add_convert_fusion.3.refs_0_), channel_id=1, source_target_pairs={{0,4},{4,0},{64,68},{68,64},{8,12},{12,8},{72,76},{76,72},{1,5},{5... | collective-permute-start | bytes 786440 | tf_op jit(solution)/shard_map/ppermute | solution.py:80

commit v3 on v2

--- a/solution.py
+++ b/solution.py
@@ -72,6 +72,7 @@
 Y_SECOND = pairs(lambda x, y, z, core: (x, partner(y, core, 1), z, core))
 ALONG_Z = pairs(lambda x, y, z, core: (x, y, z + 1 - 2 * core, core))
 BACK_Z = pairs(lambda x, y, z, core: (x, y, z - 1 + 2 * core, core))
+DIAGONAL = pairs(lambda x, y, z, core: (partner(x, core, 1), y, z + 1 - 2 * core, core))
 ACROSS_Z = pairs(lambda x, y, z, core: (x, y, z + 2, core))
 SWAP = pairs(lambda x, y, z, core: (x, y, z, 1 - core))
 
@@ -382,17 +383,17 @@
     kv_weight, queries, cotangent = load(kv_weight, queries, cotangent)
     g["a"] = send(tie(h["a"], kv_weight, queries), ALONG_Z)
     h["d"] = send(h["a"], X_SECOND)
-    g["d"] = send(g["a"], X_SECOND)
+    g["b"] = send(h["b"], ALONG_Z)
+    g["d"] = send(h["a"], DIAGONAL)
     h_too["a"] = send(h["a"], SWAP)
     h_too["b"] = send(h["b"], SWAP)
     g_too["o"] = send(g["o"], SWAP)
-    h_too["d"] = send(h["d"], SWAP)
-    g_too["a"] = send(g["a"], SWAP)
     done = [project((h["o"], h_too["o"], h["a"], h_too["a"]), kv_weight)]
-    g["b"] = send(tie(h["b"], g["a"], done[0][0]), ALONG_Z)
     done.append(project((g["o"], g_too["o"], h["b"], h_too["b"]), kv_weight))
+    h_too["d"] = send(tie(h["d"], done[0][0]), SWAP)
+    g_too["a"] = send(tie(g["a"], done[1][0]), SWAP)
     done.append(project((g["a"], g_too["a"], h["d"], h_too["d"]), kv_weight))
-    g_too["b"] = send(tie(g["b"], done[1][0]), SWAP)
+    g_too["b"] = send(g["b"], SWAP)
     g_too["d"] = send(tie(g["d"], done[2][0]), SWAP)
     done.append(project((g["b"], g_too["b"], g["d"], g_too["d"]), kv_weight))
     keys, values = zip(*done)
@@ -418,10 +419,14 @@
 
     value_in = send(value_out, Y_FIRST)
     key_in = send(tie(key_out, value_in), Y_FIRST)
-    value_two = send(tie(onward(value_keep, value_in), key_in), Y_SECOND)
-    key_two = jnp.split(onward(key_keep, key_in), 2, 1)
-    key_two[0] = send(key_two[0], Y_SECOND)
-    key_two[1] = send(tie(key_two[1], key_two[0]), Y_SECOND)
+
+    def last_two(part):
+        one, two = jnp.split(part, 2, 1)
+        one = send(one, Y_SECOND)
+        return [one, send(tie(two, one), Y_SECOND)]
+
+    value_two = last_two(tie(onward(value_keep, value_in), key_in))
+    key_two = last_two(onward(key_keep, key_in))
 
     mine, theirs = [], []
     for keep, out in zip(kept, x_out):
@@ -434,7 +439,7 @@
         theirs.append(send(mine[-1], SWAP))
     enc_grad = place(core, mine, theirs)
 
-    weight_grad = share(1, value_keep, value_in, [value_two])
+    weight_grad = share(1, value_keep, value_in, value_two)
     weight_grad = share(0, key_keep, key_in, key_two, weight_grad)
     return (attended, query_grad, enc_grad, weight_grad)
 

time: 143 us -> 148 us (1.035)
  the two profiles are of different devices: /device:TPU:62 before, /device:TPU:0 now
where the time goes in v3:
time: 148 us; the launch traced here: 145 us
  waiting for transfers between devices  49.2 us (33%)
  starting transfers between devices  46 us (31%)
  Pallas kernels  42.4 us (29%)
  local copies, waits for them, and re-layouts  4.97 us (3%)
    ppermute x34, waiting for transfers between devices, send(): return lax.ppermute(array, ALL, route)  49.2 us
    ppermute x34, starting transfers between devices, send(): return lax.ppermute(array, ALL, route)  46 us
    pallas_call x16, Pallas kernels, call(): pl.pallas_call(reads, in_specs=[SCALARS] * index + [WHOLE] * (count - ind...  37 us
    pallas_call x2, Pallas kernels, share(): pl.pallas_call(functools.partial(share_body, part, len(seconds)), in_spec...  3.73 us
    unnamed x8, local copies, waits for them, and re-layouts  3.39 us
  transfers between devices with their start and end apart: 34, of which 18 were waited for; matrix products, arithmetic and copies ran while one was open for 1% of the time, Pallas kernels for 22%

profile of v3, /device:TPU:0, one launch (start us, length us, event | category | flops | bytes accessed | tf_op | source)
XLA Modules:
  0.0 145.1 jit_solution(14716162719798845141)
XLA Ops:
  2.2 1.6 %collective-permute-start = (bf16[64,4096]{1,0:T(8,128)(2,1)S(1)}, bf16[64,4096]{1,0:T(8,128)(2,1)S(1)}, u32[]{:S(2)}, u32[]{:S(2)}) collective-permute-start(bf16[64,4096]{1,0:T(8,128)(2,1)S(1)} %get-tuple-element.48.refs_0_.refs_2_), channel_id=1, source_target_pairs={{0,16},{4,52},{64,80},{68,116},{8,24},{12,60},{72,88},{76,124},{1,... | collective-permute-start | bytes 1572872 | tf_op jit(solution)/shard_map/ppermute | solution.py:81
  3.8 2.1 %collective-permute-start.4 = (bf16[64,4096]{1,0:T(8,128)(2,1)S(1)}, bf16[64,4096]{1,0:T(8,128)(2,1)S(1)}, u32[]{:S(2)}, u32[]{:S(2)}) collective-permute-start(bf16[64,4096]{1,0:T(8,128)(2,1)S(1)} %get-tuple-element.48.refs_0_.refs_2_), channel_id=1, source_target_pairs={{0,48},{4,20},{64,112},{68,84},{8,56},{12,28},{72,120},{76,92},{1,... | collective-permute-start | bytes 1572872 | tf_op jit(solution)/shard_map/ppermute | solution.py:81
  5.9 1.9 %collective-permute-start.2 = (bf16[64,4096]{1,0:T(8,128)(2,1)S(1)}, bf16[64,4096]{1,0:T(8,128)(2,1)S(1)}, u32[]{:S(2)}, u32[]{:S(2)}) collective-permute-start(bf16[64,4096]{1,0:T(8,128)(2,1)S(1)} %get-tuple-element.48.refs_0_.refs_2_), channel_id=1, source_target_pairs={{0,64},{4,76},{64,8},{68,4},{8,72},{12,68},{72,0},{76,12},{1,65},{... | collective-permute-start | bytes 1572872 | tf_op jit(solution)/shard_map/ppermute | solution.py:81
  7.8 8.2 %collective-permute-done.refs_2_.refs_6_ = bf16[64,4096]{1,0:T(8,128)(2,1)S(1)} collective-permute-done((bf16[64,4096]{1,0:T(8,128)(2,1)S(1)}, bf16[64,4096]{1,0:T(8,128)(2,1)S(1)}, u32[]{:S(2)}, u32[]{:S(2)}) %collective-permute-start) | collective-permute-done | bytes 524320 | tf_op jit(solution)/shard_map/ppermute | solution.py:81
  16.0 3.4 %copy-done = bf16[1,2,4096,512]{3,2,1,0:T(8,128)(2,1)S(1)} copy-done((bf16[1,2,4096,512]{3,2,1,0:T(8,128)(2,1)S(1)}, bf16[1,2,4096,512]{3,2,1,0:T(8,128)(2,1)}, u32[]{:S(2)}) %copy-start) | copy-done | bytes 8388632
  20.0 2.9 %collective-permute-start.8 = (bf16[64,4096]{1,0:T(8,128)(2,1)S(1)}, bf16[64,4096]{1,0:T(8,128)(2,1)S(1)}, u32[]{:S(2)}, u32[]{:S(2)}) collective-permute-start(bf16[64,4096]{1,0:T(8,128)(2,1)S(1)} %collective-permute-done.refs_2_.refs_6_), channel_id=1, source_target_pairs={{0,48},{4,20},{64,112},{68,84},{8,56},{12,28},{72,120},{76,92},{1,... | collective-permute-start | bytes 1572872 | tf_op jit(solution)/shard_map/ppermute | solution.py:81
  23.4 2.0 %collective-permute-start.6 = (bf16[64,4096]{1,0:T(8,128)(2,1)S(1)}, bf16[64,4096]{1,0:T(8,128)(2,1)S(1)}, u32[]{:S(2)}, u32[]{:S(2)}) collective-permute-start(bf16[64,4096]{1,0:T(8,128)(2,1)S(1)} %collective-permute-done.refs_2_.refs_6_), channel_id=1, source_target_pairs={{0,64},{4,76},{64,8},{68,4},{8,72},{12,68},{72,0},{76,12},{1,65},{... | collective-permute-start | bytes 1572872 | tf_op jit(solution)/shard_map/ppermute | solution.py:81
  25.5 1.9 %collective-permute-start.10 = (bf16[64,4096]{1,0:T(8,128)(2,1)S(1)}, bf16[64,4096]{1,0:T(8,128)(2,1)S(1)}, u32[]{:S(2)}, u32[]{:S(2)}) collective-permute-start(bf16[64,4096]{1,0:T(8,128)(2,1)S(1)} %collective-permute-done.4.refs_2_.refs_4_), channel_id=1, source_target_pairs={{0,64},{4,76},{64,8},{68,4},{8,72},{12,68},{72,0},{76,12},{1,65},{... | collective-permute-start | bytes 1572872 | tf_op jit(solution)/shard_map/ppermute | solution.py:81
  27.4 2.3 %shard_map.76 = (bf16[256,512]{1,0:T(8,128)(2,1)S(1)}, bf16[256,512]{1,0:T(8,128)(2,1)S(1)}) custom-call(bf16[64,4096]{1,0:T(8,128)(2,1)S(1)} %get-tuple-element.48.refs_0_.refs_2_, bf16[64,4096]{1,0:T(8,128)(2,1)S(1)} %get-tuple-element.49.refs_1_.refs_10_, bf16[64,4096]{1,0:T(8,128)(2,1)S(1)} %collective-permute-done.refs_2_.refs_6_, ...), custom_call_target="tpu_custom_call" | custom-call | flops 1000 | bytes 1000 | tf_op jit(solution)/shard_map/pallas_call | solution.py:32
  30.5 2.3 %shard_map.77 = (bf16[256,512]{1,0:T(8,128)(2,1)S(1)}, bf16[256,512]{1,0:T(8,128)(2,1)S(1)}) custom-call(bf16[64,4096]{1,0:T(8,128)(2,1)S(1)} %collective-permute-done.2.refs_0_.refs_3_, bf16[64,4096]{1,0:T(8,128)(2,1)S(1)} %collective-permute-done.3.refs_1_.refs_11_, bf16[64,4096]{1,0:T(8,128)(2,1)S(1)} %collective-permute-done.4.refs_2_.refs_4_, ...), custom_call_target="tpu_custom_call" | custom-call | flops 1000 | bytes 1000 | tf_op jit(solution)/shard_map/pallas_call | solution.py:32
  32.8 1.9 %collective-permute-done.6.refs_0_.refs_7_ = bf16[64,4096]{1,0:T(8,128)(2,1)S(1)} collective-permute-done((bf16[64,4096]{1,0:T(8,128)(2,1)S(1)}, bf16[64,4096]{1,0:T(8,128)(2,1)S(1)}, u32[]{:S(2)}, u32[]{:S(2)}) %collective-permute-start.6) | collective-permute-done | bytes 524320 | tf_op jit(solution)/shard_map/ppermute | solution.py:81
  34.7 3.0 %collective-permute-start.12 = (bf16[64,4096]{1,0:T(8,128)(2,1)S(1)}, bf16[64,4096]{1,0:T(8,128)(2,1)S(1)}, u32[]{:S(2)}, u32[]{:S(2)}) collective-permute-start(bf16[64,4096]{1,0:T(8,128)(2,1)S(1)} %collective-permute-done.refs_2_.refs_6_), channel_id=1, source_target_pairs={{0,112},{4,92},{64,56},{68,20},{8,120},{12,84},{72,48},{76,28},{1,... | collective-permute-start | bytes 1572872 | tf_op jit(solution)/shard_map/ppermute | solution.py:81
  37.7 2.7 %collective-permute-done.10.refs_0_.refs_5_ = bf16[64,4096]{1,0:T(8,128)(2,1)S(1)} collective-permute-done((bf16[64,4096]{1,0:T(8,128)(2,1)S(1)}, bf16[64,4096]{1,0:T(8,128)(2,1)S(1)}, u32[]{:S(2)}, u32[]{:S(2)}) %collective-permute-start.10) | collective-permute-done | bytes 524320 | tf_op jit(solution)/shard_map/ppermute | solution.py:81
  40.4 4.4 %collective-permute-start.11 = (bf16[64,4096]{1,0:T(8,128)(2,1)S(1)}, bf16[64,4096]{1,0:T(8,128)(2,1)S(1)}, u32[]{:S(2)}, u32[]{:S(2)}) collective-permute-start(bf16[64,4096]{1,0:T(8,128)(2,1)S(1)} %collective-permute-done.10.refs_0_.refs_5_), channel_id=1, source_target_pairs={{0,4},{4,0},{64,68},{68,64},{8,12},{12,8},{72,76},{76,72},{1,5},{5... | collective-permute-start | bytes 1572872 | tf_op jit(solution)/shard_map/ppermute | solution.py:81
  44.8 2.3 %shard_map.78 = (bf16[256,512]{1,0:T(8,128)(2,1)S(1)}, bf16[256,512]{1,0:T(8,128)(2,1)S(1)}) custom-call(bf16[64,4096]{1,0:T(8,128)(2,1)S(1)} %collective-permute-done.6.refs_0_.refs_7_, bf16[64,4096]{1,0:T(8,128)(2,1)S(1)} %collective-permute-done.7.refs_1_.refs_15_, bf16[64,4096]{1,0:T(8,128)(2,1)S(1)} %collective-permute-done.8.refs_2_.refs_8_, ...), custom_call_target="tpu_custom_call" | custom-call | flops 1000 | bytes 1000 | tf_op jit(solution)/shard_map/pallas_call | solution.py:32
  47.4 1.9 %collective-permute-done.13.refs_3_.refs_17_ = bf16[64,4096]{1,0:T(8,128)(2,1)S(1)} collective-permute-done((bf16[64,4096]{1,0:T(8,128)(2,1)S(1)}, bf16[64,4096]{1,0:T(8,128)(2,1)S(1)}, u32[]{:S(2)}, u32[]{:S(2)}) %collective-permute-start.13) | collective-permute-done | bytes 524320 | tf_op jit(solution)/shard_map/ppermute | solution.py:81
  49.3 2.3 %shard_map.79 = (bf16[256,512]{1,0:T(8,128)(2,1)S(1)}, bf16[256,512]{1,0:T(8,128)(2,1)S(1)}) custom-call(bf16[64,4096]{1,0:T(8,128)(2,1)S(1)} %collective-permute-done.10.refs_0_.refs_5_, bf16[64,4096]{1,0:T(8,128)(2,1)S(1)} %collective-permute-done.11.refs_1_.refs_13_, bf16[64,4096]{1,0:T(8,128)(2,1)S(1)} %collective-permute-done.12.refs_2_.refs_9_, ...), custom_call_target="tpu_custom_call" | custom-call | flops 1000 | bytes 1000 | tf_op jit(solution)/shard_map/pallas_call | solution.py:32
  51.6 3.6 %shard_map.80 = (bf16[1,1,512,512]{3,2,1,0:T(8,128)(2,1)}, f32[2,512,1024]{2,1,0:T(8,128)S(1)}, bf16[1024,512]{1,0:T(8,128)(2,1)S(1)}, bf16[512,1024]{1,0:T(8,128)(2,1)S(1)}) custom-call(bf16[1,1,512,512]{3,2,1,0:T(8,128)(2,1)S(1)} %get-tuple-element.46.refs_0_, bf16[1,1,512,512]{3,2,1,0:T(8,128)(2,1)S(1)} %get-tuple-element.47.refs_1_, ...), custom_call_target="tpu_custom_call" | custom-call | flops 1000 | bytes 1000 | tf_op jit(solution)/shard_map/pallas_call | solution.py:32
  55.2 2.9 %shard_map.81.refs_12_ = bf16[512,2048]{1,0:T(8,128)(2,1)S(1)} custom-call(s32[4]{0:T(128)S(1)} %get-tuple-element.65.refs_0_, bf16[512,1024]{1,0:T(8,128)(2,1)S(1)} %get-tuple-element.66.refs_1_, bf16[64,4096]{1,0:T(8,128)(2,1)S(1)} %get-tuple-element.48.refs_0_.refs_2_, bf16[64,4096]{1,0:T(8,128)(2,1)S(1)} %collective-permute-done.2.refs_0_.refs_3_, ...), custom_call_target="tpu_custom_call" | custom-call | flops 1000 | bytes 1000 | tf_op jit(solution)/shard_map/pallas_call | solution.py:32
  58.1 1.7 %collective-permute-start.28 = (bf16[512,2048]{1,0:T(8,128)(2,1)S(1)}, bf16[512,2048]{1,0:T(8,128)(2,1)S(1)}, u32[]{:S(2)}, u32[]{:S(2)}) collective-permute-start(bf16[512,2048]{1,0:T(8,128)(2,1)S(1)} %shard_map.81.refs_12_), channel_id=1, source_target_pairs={{0,1},{4,7},{64,65},{68,71},{8,9},{12,15},{72,73},{76,79},{1,0},{5... | collective-permute-start | bytes 6291464 | tf_op jit(solution)/shard_map/ppermute | solution.py:81
  59.7 2.6 %shard_map.82 = (bf16[1,1,512,512]{3,2,1,0:T(8,128)(2,1)}, bf16[1024,512]{1,0:T(8,128)(2,1)S(1)}, bf16[512,1024]{1,0:T(8,128)(2,1)S(1)}) custom-call(bf16[1,1,512,512]{3,2,1,0:T(8,128)(2,1)S(1)} %get-tuple-element.46.refs_0_, bf16[1,1,512,512]{3,2,1,0:T(8,128)(2,1)S(1)} %get-tuple-element.47.refs_1_, bf16[256,512]{1,0:T(8,128)(2,1)S(1)} %get-tuple-element.51.refs_2_, ...), custom_call_target="tpu_custom_call" | custom-call | flops 1000 | bytes 1000 | tf_op jit(solution)/shard_map/pallas_call | solution.py:32
  62.3 2.4 %shard_map.85 = (bf16[256,2048]{1,0:T(8,128)(2,1)S(1)}, bf16[256,2048]{1,0:T(8,128)(2,1)S(1)}) custom-call(bf16[1024,512]{1,0:T(8,128)(2,1)S(1)} %get-tuple-element.68.refs_0_, bf16[1024,512]{1,0:T(8,128)(2,1)S(1)} %get-tuple-element.69.refs_1_, bf16[1,2,4096,512]{3,2,1,0:T(8,128)(2,1)S(1)} %get-tuple-element.50.refs_4_.refs_2_), custom_call_target="tpu_custom_call" | custom-call | flops 1000 | bytes 1000 | tf_op jit(solution)/shard_map/pallas_call | solution.py:32
  64.7 1.4 collective-permute-start.17
  66.1 2.4 %shard_map.83 = (bf16[256,2048]{1,0:T(8,128)(2,1)S(1)}, bf16[256,2048]{1,0:T(8,128)(2,1)S(1)}) custom-call(bf16[1024,512]{1,0:T(8,128)(2,1)S(1)} %get-tuple-element.68.refs_0_, bf16[1024,512]{1,0:T(8,128)(2,1)S(1)} %get-tuple-element.69.refs_1_, bf16[1,2,4096,512]{3,2,1,0:T(8,128)(2,1)S(1)} %get-tuple-element.50.refs_4_.refs_2_), custom_call_target="tpu_custom_call" | custom-call | flops 1000 | bytes 1000 | tf_op jit(solution)/shard_map/pallas_call | solution.py:32
  69.8 2.4 %shard_map.86 = (bf16[256,2048]{1,0:T(8,128)(2,1)S(1)}, bf16[256,2048]{1,0:T(8,128)(2,1)S(1)}) custom-call(bf16[1024,512]{1,0:T(8,128)(2,1)S(1)} %get-tuple-element.68.refs_0_, bf16[1024,512]{1,0:T(8,128)(2,1)S(1)} %get-tuple-element.69.refs_1_, bf16[1,2,4096,512]{3,2,1,0:T(8,128)(2,1)S(1)} %get-tuple-element.50.refs_4_.refs_2_, ...), custom_call_target="tpu_custom_call" | custom-call | flops 1000 | bytes 1000 | tf_op jit(solution)/shard_map/pallas_call | solution.py:32
  72.8 2.4 %shard_map.84 = (bf16[256,2048]{1,0:T(8,128)(2,1)S(1)}, bf16[256,2048]{1,0:T(8,128)(2,1)S(1)}) custom-call(bf16[1024,512]{1,0:T(8,128)(2,1)S(1)} %get-tuple-element.68.refs_0_, bf16[1024,512]{1,0:T(8,128)(2,1)S(1)} %get-tuple-element.69.refs_1_, bf16[1,2,4096,512]{3,2,1,0:T(8,128)(2,1)S(1)} %get-tuple-element.50.refs_4_.refs_2_, ...), custom_call_target="tpu_custom_call" | custom-call | flops 1000 | bytes 1000 | tf_op jit(solution)/shard_map/pallas_call | solution.py:32
  75.2 1.6 %collective-permute-start.16 = (bf16[256,2048]{1,0:T(8,128)(2,1)S(1)}, bf16[256,2048]{1,0:T(8,128)(2,1)S(1)}, u32[]{:S(2)}, u32[]{:S(2)}) collective-permute-start(bf16[256,2048]{1,0:T(8,128)(2,1)S(1)} %get-tuple-element.73.refs_18_), channel_id=1, source_target_pairs={{0,16},{4,52},{64,80},{68,116},{8,24},{12,60},{72,88},{76,124},{1,... | collective-permute-start | bytes 3145736 | tf_op jit(solution)/shard_map/ppermute | solution.py:81
  76.8 2.9 %shard_map.87.refs_18_ = bf16[512,2048]{1,0:T(8,128)(2,1)S(1)} custom-call(s32[4]{0:T(128)S(1)} %get-tuple-element.65.refs_0_, bf16[512,1024]{1,0:T(8,128)(2,1)S(1)} %get-tuple-element.75.refs_1_, bf16[64,4096]{1,0:T(8,128)(2,1)S(1)} %get-tuple-element.48.refs_0_.refs_2_, bf16[64,4096]{1,0:T(8,128)(2,1)S(1)} %collective-permute-done.2.refs_0_.refs_3_, ...), custom_call_target="tpu_custom_call" | custom-call | flops 1000 | bytes 1000 | tf_op jit(solution)/shard_map/pallas_call | solution.py:32
  79.7 4.5 %collective-permute-done.28.first = bf16[512,2048]{1,0:T(8,128)(2,1)S(1)} collective-permute-done((bf16[512,2048]{1,0:T(8,128)(2,1)S(1)}, bf16[512,2048]{1,0:T(8,128)(2,1)S(1)}, u32[]{:S(2)}, u32[]{:S(2)}) %collective-permute-start.28) | collective-permute-done | bytes 2097184 | tf_op jit(solution)/shard_map/ppermute | solution.py:81
  84.2 1.6 %collective-permute-start.29 = (bf16[512,2048]{1,0:T(8,128)(2,1)S(1)}, bf16[512,2048]{1,0:T(8,128)(2,1)S(1)}, u32[]{:S(2)}, u32[]{:S(2)}) collective-permute-start(bf16[512,2048]{1,0:T(8,128)(2,1)S(1)} %shard_map.87.refs_18_), channel_id=1, source_target_pairs={{0,1},{4,7},{64,65},{68,71},{8,9},{12,15},{72,73},{76,79},{1,0},{5... | collective-permute-start | bytes 6291464 | tf_op jit(solution)/shard_map/ppermute | solution.py:81
  85.7 2.9 %shard_map.88.refs_18_.keep = bf16[512,2048]{1,0:T(8,128)(2,1)S(1)} custom-call(s32[4]{0:T(128)S(1)} %get-tuple-element.74.refs_0_, bf16[512,1024]{1,0:T(8,128)(2,1)S(1)} %get-tuple-element.66.refs_1_, bf16[64,4096]{1,0:T(8,128)(2,1)S(1)} %get-tuple-element.48.refs_0_.refs_2_, bf16[64,4096]{1,0:T(8,128)(2,1)S(1)} %collective-permute-done.2.refs_0_.refs_3_, ...), custom_call_target="tpu_custom_call" | custom-call | flops 1000 | bytes 1000 | tf_op jit(solution)/shard_map/pallas_call | solution.py:32
  88.6 2.9 %shard_map.89.refs_2_.keep = bf16[512,2048]{1,0:T(8,128)(2,1)S(1)} custom-call(s32[4]{0:T(128)S(1)} %get-tuple-element.74.refs_0_, bf16[512,1024]{1,0:T(8,128)(2,1)S(1)} %get-tuple-element.75.refs_1_, bf16[64,4096]{1,0:T(8,128)(2,1)S(1)} %get-tuple-element.48.refs_0_.refs_2_, bf16[64,4096]{1,0:T(8,128)(2,1)S(1)} %collective-permute-done.2.refs_0_.refs_3_, ...), custom_call_target="tpu_custom_call" | custom-call | flops 1000 | bytes 1000 | tf_op jit(solution)/shard_map/pallas_call | solution.py:32
  91.8 1.6 %collective-permute-start.23 = (bf16[128,2048]{1,0:T(8,128)(2,1)S(1)}, bf16[128,2048]{1,0:T(8,128)(2,1)S(1)}, u32[]{:S(2)}, u32[]{:S(2)}) collective-permute-start(bf16[128,2048]{1,0:T(8,128)(2,1)S(1)} %get-tuple-element.83), channel_id=1, source_target_pairs={{0,48},{4,20},{64,112},{68,84},{8,56},{12,28},{72,120},{76,92},{1,... | collective-permute-start | bytes 1572872 | tf_op jit(solution)/shard_map/ppermute | solution.py:81
  93.4 7.3 %collective-permute-done.16.refs_1_ = bf16[256,2048]{1,0:T(8,128)(2,1)S(1)} collective-permute-done((bf16[256,2048]{1,0:T(8,128)(2,1)S(1)}, bf16[256,2048]{1,0:T(8,128)(2,1)S(1)}, u32[]{:S(2)}, u32[]{:S(2)}) %collective-permute-start.16) | collective-permute-done | bytes 1048608 | tf_op jit(solution)/shard_map/ppermute | solution.py:81
  100.9 1.6 %collective-permute-start.19 = (bf16[128,2048]{1,0:T(8,128)(2,1)S(1)}, bf16[128,2048]{1,0:T(8,128)(2,1)S(1)}, u32[]{:S(2)}, u32[]{:S(2)}) collective-permute-start(bf16[128,2048]{1,0:T(8,128)(2,1)S(1)} %get-tuple-element.80), channel_id=1, source_target_pairs={{0,48},{4,20},{64,112},{68,84},{8,56},{12,28},{72,120},{76,92},{1,... | collective-permute-start | bytes 1572872 | tf_op jit(solution)/shard_map/ppermute | solution.py:81
  102.9 1.6 %collective-permute-done.23 = bf16[128,2048]{1,0:T(8,128)(2,1)S(1)} collective-permute-done((bf16[128,2048]{1,0:T(8,128)(2,1)S(1)}, bf16[128,2048]{1,0:T(8,128)(2,1)S(1)}, u32[]{:S(2)}, u32[]{:S(2)}) %collective-permute-start.23) | collective-permute-done | bytes 524320 | tf_op jit(solution)/shard_map/ppermute | solution.py:81
  104.7 3.8 %collective-permute-start.24 = (bf16[64,2048]{1,0:T(8,128)(2,1)S(1)}, bf16[64,2048]{1,0:T(8,128)(2,1)S(1)}, u32[]{:S(2)}, u32[]{:S(2)}) collective-permute-start(bf16[64,2048]{1,0:T(8,128)(2,1)S(1)} %slice.54), channel_id=1, source_target_pairs={{0,72},{4,68},{64,0},{68,12},{8,64},{12,76},{72,8},{76,4},{1,73},{... | collective-permute-start | bytes 786440 | tf_op jit(solution)/shard_map/ppermute | solution.py:81
  108.5 2.9 %collective-permute-done.19 = bf16[128,2048]{1,0:T(8,128)(2,1)S(1)} collective-permute-done((bf16[128,2048]{1,0:T(8,128)(2,1)S(1)}, bf16[128,2048]{1,0:T(8,128)(2,1)S(1)}, u32[]{:S(2)}, u32[]{:S(2)}) %collective-permute-start.19) | collective-permute-done | bytes 524320 | tf_op jit(solution)/shard_map/ppermute | solution.py:81
  111.5 3.8 %collective-permute-start.20 = (bf16[64,2048]{1,0:T(8,128)(2,1)S(1)}, bf16[64,2048]{1,0:T(8,128)(2,1)S(1)}, u32[]{:S(2)}, u32[]{:S(2)}) collective-permute-start(bf16[64,2048]{1,0:T(8,128)(2,1)S(1)} %slice.55), channel_id=1, source_target_pairs={{0,72},{4,68},{64,0},{68,12},{8,64},{12,76},{72,8},{76,4},{1,73},{... | collective-permute-start | bytes 786440 | tf_op jit(solution)/shard_map/ppermute | solution.py:81
  115.5 2.3 %collective-permute-start.32 = (bf16[512,512]{1,0:T(8,128)(2,1)S(1)}, bf16[512,512]{1,0:T(8,128)(2,1)S(1)}, u32[]{:S(2)}, u32[]{:S(2)}) collective-permute-start(bf16[512,512]{1,0:T(8,128)(2,1)S(1)} %get-tuple-element.89), channel_id=1, source_target_pairs={{0,3},{4,5},{64,67},{68,69},{8,11},{12,13},{72,75},{76,77},{1,2},{... | collective-permute-start | bytes 1572872 | tf_op jit(solution)/shard_map/ppermute | solution.py:81
  119.7 6.9 %collective-permute-done.20 = bf16[64,2048]{1,0:T(8,128)(2,1)S(1)} collective-permute-done((bf16[64,2048]{1,0:T(8,128)(2,1)S(1)}, bf16[64,2048]{1,0:T(8,128)(2,1)S(1)}, u32[]{:S(2)}, u32[]{:S(2)}) %collective-permute-start.20) | collective-permute-done | bytes 262176 | tf_op jit(solution)/shard_map/ppermute | solution.py:81
  126.9 1.5 %collective-permute-start.33 = (bf16[512,512]{1,0:T(8,128)(2,1)S(1)}, bf16[512,512]{1,0:T(8,128)(2,1)S(1)}, u32[]{:S(2)}, u32[]{:S(2)}) collective-permute-start(bf16[512,512]{1,0:T(8,128)(2,1)S(1)} %get-tuple-element.87), channel_id=1, source_target_pairs={{0,3},{4,5},{64,67},{68,69},{8,11},{12,13},{72,75},{76,77},{1,2},{... | collective-permute-start | bytes 1572872 | tf_op jit(solution)/shard_map/ppermute | solution.py:81
  128.4 3.2 %collective-permute-done.30.refs_0_ = bf16[512,512]{1,0:T(8,128)(2,1)S(1)} collective-permute-done((bf16[512,512]{1,0:T(8,128)(2,1)S(1)}, bf16[512,512]{1,0:T(8,128)(2,1)S(1)}, u32[]{:S(2)}, u32[]{:S(2)}) %collective-permute-start.30) | collective-permute-done | bytes 524320 | tf_op jit(solution)/shard_map/ppermute | solution.py:81
  131.6 2.2 %collective-permute-start.31 = (bf16[512,512]{1,0:T(8,128)(2,1)S(1)}, bf16[512,512]{1,0:T(8,128)(2,1)S(1)}, u32[]{:S(2)}, u32[]{:S(2)}) collective-permute-start(bf16[512,512]{1,0:T(8,128)(2,1)S(1)} %get-tuple-element.85), channel_id=1, source_target_pairs={{0,3},{4,5},{64,67},{68,69},{8,11},{12,13},{72,75},{76,77},{1,2},{... | collective-permute-start | bytes 1572872 | tf_op jit(solution)/shard_map/ppermute | solution.py:81
  134.8 1.5 %collective-permute-done.26.refs_2_ = bf16[64,2048]{1,0:T(8,128)(2,1)S(1)} collective-permute-done((bf16[64,2048]{1,0:T(8,128)(2,1)S(1)}, bf16[64,2048]{1,0:T(8,128)(2,1)S(1)}, u32[]{:S(2)}, u32[]{:S(2)}) %collective-permute-start.26) | collective-permute-done | bytes 262176 | tf_op jit(solution)/shard_map/ppermute | solution.py:81
  137.4 1.9 %shard_map.93.refs_2_ = bf16[1,2,1024,512]{3,2,1,0:T(8,128)(2,1)} custom-call(bf16[512,2048]{1,0:T(8,128)(2,1)S(1)} %shard_map.88.refs_18_.keep, bf16[512,2048]{1,0:T(8,128)(2,1)S(1)} %collective-permute-done.28.first, bf16[512,512]{1,0:T(8,128)(2,1)S(1)} %collective-permute-done.32.refs_0_, bf16[512,512]{1,0:T(8,128)(2,1)S(1)} %collective-permute-done.33.refs_1_), custom_call_target="tpu_custom_call" | custom-call | flops 1000 | bytes 1000 | tf_op jit(solution)/shard_map/pallas_call | solution.py:243
  139.3 3.7 %collective-permute-done.31.refs_1_ = bf16[512,512]{1,0:T(8,128)(2,1)S(1)} collective-permute-done((bf16[512,512]{1,0:T(8,128)(2,1)S(1)}, bf16[512,512]{1,0:T(8,128)(2,1)S(1)}, u32[]{:S(2)}, u32[]{:S(2)}) %collective-permute-start.31) | collective-permute-done | bytes 524320 | tf_op jit(solution)/shard_map/ppermute | solution.py:81
  143.0 1.9 %shard_map.94 = bf16[1,2,1024,512]{3,2,1,0:T(8,128)(2,1)} custom-call(bf16[512,2048]{1,0:T(8,128)(2,1)S(1)} %shard_map.89.refs_2_.keep, bf16[512,2048]{1,0:T(8,128)(2,1)S(1)} %collective-permute-done.29.first, bf16[512,512]{1,0:T(8,128)(2,1)S(1)} %collective-permute-done.30.refs_0_, ...), custom_call_target="tpu_custom_call", output_to_operand_aliasing={{}: (4, {})} | custom-call | flops 1000 | bytes 1000 | tf_op jit(solution)/shard_map/pallas_call | solution.py:243
  (62 shorter events, 11.2 us)
Async XLA Ops:
  0.6 15.3 %copy-start.2 = (bf16[1,1,512,512]{3,2,1,0:T(8,128)(2,1)S(1)}, bf16[1,1,512,512]{3,2,1,0:T(8,128)(2,1)}, u32[]{:S(2)}) copy-start(bf16[1,1,512,512]{3,2,1,0:T(8,128)(2,1)} %refs_2_.1) | copy-start | bytes 1572868
  0.6 15.3 %copy-start.1 = (bf16[1,1,512,512]{3,2,1,0:T(8,128)(2,1)S(1)}, bf16[1,1,512,512]{3,2,1,0:T(8,128)(2,1)}, u32[]{:S(2)}) copy-start(bf16[1,1,512,512]{3,2,1,0:T(8,128)(2,1)} %refs_1_.1) | copy-start | bytes 1572868
  2.2 13.8 %collective-permute-start = (bf16[64,4096]{1,0:T(8,128)(2,1)S(1)}, bf16[64,4096]{1,0:T(8,128)(2,1)S(1)}, u32[]{:S(2)}, u32[]{:S(2)}) collective-permute-start(bf16[64,4096]{1,0:T(8,128)(2,1)S(1)} %get-tuple-element.48.refs_0_.refs_2_), channel_id=1, source_target_pairs={{0,16},{4,52},{64,80},{68,116},{8,24},{12,60},{72,88},{76,124},{1,... | collective-permute-start | bytes 1572872 | tf_op jit(solution)/shard_map/ppermute | solution.py:81
  3.8 19.2 %collective-permute-start.4 = (bf16[64,4096]{1,0:T(8,128)(2,1)S(1)}, bf16[64,4096]{1,0:T(8,128)(2,1)S(1)}, u32[]{:S(2)}, u32[]{:S(2)}) collective-permute-start(bf16[64,4096]{1,0:T(8,128)(2,1)S(1)} %get-tuple-element.48.refs_0_.refs_2_), channel_id=1, source_target_pairs={{0,48},{4,20},{64,112},{68,84},{8,56},{12,28},{72,120},{76,92},{1,... | collective-permute-start | bytes 1572872 | tf_op jit(solution)/shard_map/ppermute | solution.py:81
  5.9 17.1 %collective-permute-start.2 = (bf16[64,4096]{1,0:T(8,128)(2,1)S(1)}, bf16[64,4096]{1,0:T(8,128)(2,1)S(1)}, u32[]{:S(2)}, u32[]{:S(2)}) collective-permute-start(bf16[64,4096]{1,0:T(8,128)(2,1)S(1)} %get-tuple-element.48.refs_0_.refs_2_), channel_id=1, source_target_pairs={{0,64},{4,76},{64,8},{68,4},{8,72},{12,68},{72,0},{76,12},{1,65},{... | collective-permute-start | bytes 1572872 | tf_op jit(solution)/shard_map/ppermute | solution.py:81
  15.9 9.5 %collective-permute-start.1 = (bf16[64,4096]{1,0:T(8,128)(2,1)S(1)}, bf16[64,4096]{1,0:T(8,128)(2,1)S(1)}, u32[]{:S(2)}, u32[]{:S(2)}) collective-permute-start(bf16[64,4096]{1,0:T(8,128)(2,1)S(1)} %collective-permute-done.refs_2_.refs_6_), channel_id=1, source_target_pairs={{0,4},{4,0},{64,68},{68,64},{8,12},{12,8},{72,76},{76,72},{1,5},{5... | collective-permute-start | bytes 1572872 | tf_op jit(solution)/shard_map/ppermute | solution.py:81
  15.9 3.4 %copy-start = (bf16[1,2,4096,512]{3,2,1,0:T(8,128)(2,1)S(1)}, bf16[1,2,4096,512]{3,2,1,0:T(8,128)(2,1)}, u32[]{:S(2)}) copy-start(bf16[1,2,4096,512]{3,2,1,0:T(8,128)(2,1)} %refs_0_.1) | copy-start | bytes 25165828
  20.0 10.5 %collective-permute-start.8 = (bf16[64,4096]{1,0:T(8,128)(2,1)S(1)}, bf16[64,4096]{1,0:T(8,128)(2,1)S(1)}, u32[]{:S(2)}, u32[]{:S(2)}) collective-permute-start(bf16[64,4096]{1,0:T(8,128)(2,1)S(1)} %collective-permute-done.refs_2_.refs_6_), channel_id=1, source_target_pairs={{0,48},{4,20},{64,112},{68,84},{8,56},{12,28},{72,120},{76,92},{1,... | collective-permute-start | bytes 1572872 | tf_op jit(solution)/shard_map/ppermute | solution.py:81
  22.9 7.5 %collective-permute-start.5 = (bf16[64,4096]{1,0:T(8,128)(2,1)S(1)}, bf16[64,4096]{1,0:T(8,128)(2,1)S(1)}, u32[]{:S(2)}, u32[]{:S(2)}) collective-permute-start(bf16[64,4096]{1,0:T(8,128)(2,1)S(1)} %collective-permute-done.4.refs_2_.refs_4_), channel_id=1, source_target_pairs={{0,4},{4,0},{64,68},{68,64},{8,12},{12,8},{72,76},{76,72},{1,5},{5... | collective-permute-start | bytes 1572872 | tf_op jit(solution)/shard_map/ppermute | solution.py:81
  22.9 7.5 %collective-permute-start.3 = (bf16[64,4096]{1,0:T(8,128)(2,1)S(1)}, bf16[64,4096]{1,0:T(8,128)(2,1)S(1)}, u32[]{:S(2)}, u32[]{:S(2)}) collective-permute-start(bf16[64,4096]{1,0:T(8,128)(2,1)S(1)} %collective-permute-done.2.refs_0_.refs_3_), channel_id=1, source_target_pairs={{0,4},{4,0},{64,68},{68,64},{8,12},{12,8},{72,76},{76,72},{1,5},{5... | collective-permute-start | bytes 1572872 | tf_op jit(solution)/shard_map/ppermute | solution.py:81
  23.4 11.3 %collective-permute-start.6 = (bf16[64,4096]{1,0:T(8,128)(2,1)S(1)}, bf16[64,4096]{1,0:T(8,128)(2,1)S(1)}, u32[]{:S(2)}, u32[]{:S(2)}) collective-permute-start(bf16[64,4096]{1,0:T(8,128)(2,1)S(1)} %collective-permute-done.refs_2_.refs_6_), channel_id=1, source_target_pairs={{0,64},{4,76},{64,8},{68,4},{8,72},{12,68},{72,0},{76,12},{1,65},{... | collective-permute-start | bytes 1572872 | tf_op jit(solution)/shard_map/ppermute | solution.py:81
  25.5 14.9 %collective-permute-start.10 = (bf16[64,4096]{1,0:T(8,128)(2,1)S(1)}, bf16[64,4096]{1,0:T(8,128)(2,1)S(1)}, u32[]{:S(2)}, u32[]{:S(2)}) collective-permute-start(bf16[64,4096]{1,0:T(8,128)(2,1)S(1)} %collective-permute-done.4.refs_2_.refs_4_), channel_id=1, source_target_pairs={{0,64},{4,76},{64,8},{68,4},{8,72},{12,68},{72,0},{76,12},{1,65},{... | collective-permute-start | bytes 1572872 | tf_op jit(solution)/shard_map/ppermute | solution.py:81
  30.5 14.3 %collective-permute-start.9 = (bf16[64,4096]{1,0:T(8,128)(2,1)S(1)}, bf16[64,4096]{1,0:T(8,128)(2,1)S(1)}, u32[]{:S(2)}, u32[]{:S(2)}) collective-permute-start(bf16[64,4096]{1,0:T(8,128)(2,1)S(1)} %collective-permute-done.8.refs_2_.refs_8_), channel_id=1, source_target_pairs={{0,4},{4,0},{64,68},{68,64},{8,12},{12,8},{72,76},{76,72},{1,5},{5... | collective-permute-start | bytes 1572872 | tf_op jit(solution)/shard_map/ppermute | solution.py:81
  34.7 10.0 %collective-permute-start.7 = (bf16[64,4096]{1,0:T(8,128)(2,1)S(1)}, bf16[64,4096]{1,0:T(8,128)(2,1)S(1)}, u32[]{:S(2)}, u32[]{:S(2)}) collective-permute-start(bf16[64,4096]{1,0:T(8,128)(2,1)S(1)} %collective-permute-done.6.refs_0_.refs_7_), channel_id=1, source_target_pairs={{0,4},{4,0},{64,68},{68,64},{8,12},{12,8},{72,76},{76,72},{1,5},{5... | collective-permute-start | bytes 1572872 | tf_op jit(solution)/shard_map/ppermute | solution.py:81
  34.7 12.5 %collective-permute-start.12 = (bf16[64,4096]{1,0:T(8,128)(2,1)S(1)}, bf16[64,4096]{1,0:T(8,128)(2,1)S(1)}, u32[]{:S(2)}, u32[]{:S(2)}) collective-permute-start(bf16[64,4096]{1,0:T(8,128)(2,1)S(1)} %collective-permute-done.refs_2_.refs_6_), channel_id=1, source_target_pairs={{0,112},{4,92},{64,56},{68,20},{8,120},{12,84},{72,48},{76,28},{1,... | collective-permute-start | bytes 1572872 | tf_op jit(solution)/shard_map/ppermute | solution.py:81
  40.4 7.0 %collective-permute-start.11 = (bf16[64,4096]{1,0:T(8,128)(2,1)S(1)}, bf16[64,4096]{1,0:T(8,128)(2,1)S(1)}, u32[]{:S(2)}, u32[]{:S(2)}) collective-permute-start(bf16[64,4096]{1,0:T(8,128)(2,1)S(1)} %collective-permute-done.10.refs_0_.refs_5_), channel_id=1, source_target_pairs={{0,4},{4,0},{64,68},{68,64},{8,12},{12,8},{72,76},{76,72},{1,5},{5... | collective-permute-start | bytes 1572872 | tf_op jit(solution)/shard_map/ppermute | solution.py:81
  47.2 2.0 %collective-permute-start.13 = (bf16[64,4096]{1,0:T(8,128)(2,1)S(1)}, bf16[64,4096]{1,0:T(8,128)(2,1)S(1)}, u32[]{:S(2)}, u32[]{:S(2)}) collective-permute-start(bf16[64,4096]{1,0:T(8,128)(2,1)S(1)} %collective-permute-done.12.refs_2_.refs_9_), channel_id=1, source_target_pairs={{0,4},{4,0},{64,68},{68,64},{8,12},{12,8},{72,76},{76,72},{1,5},{5... | collective-permute-start | bytes 1572872 | tf_op jit(solution)/shard_map/ppermute | solution.py:81
  55.2 4.6 %copy-start.3 = (bf16[1,1,512,512]{3,2,1,0:T(8,128)(2,1)S(1)}, bf16[1,1,512,512]{3,2,1,0:T(8,128)(2,1)}, u32[]{:S(2)}) copy-start(bf16[1,1,512,512]{3,2,1,0:T(8,128)(2,1)} %get-tuple-element.42.refs_10_) | copy-start | bytes 1572868
  58.1 26.1 %collective-permute-start.28 = (bf16[512,2048]{1,0:T(8,128)(2,1)S(1)}, bf16[512,2048]{1,0:T(8,128)(2,1)S(1)}, u32[]{:S(2)}, u32[]{:S(2)}) collective-permute-start(bf16[512,2048]{1,0:T(8,128)(2,1)S(1)} %shard_map.81.refs_12_), channel_id=1, source_target_pairs={{0,1},{4,7},{64,65},{68,71},{8,9},{12,15},{72,73},{76,79},{1,0},{5... | collective-permute-start | bytes 6291464 | tf_op jit(solution)/shard_map/ppermute | solution.py:81
  64.7 4.6 %collective-permute-start.17 = (bf16[256,2048]{1,0:T(8,128)(2,1)S(1)}, bf16[256,2048]{1,0:T(8,128)(2,1)S(1)}, u32[]{:S(2)}, u32[]{:S(2)}) collective-permute-start(bf16[256,2048]{1,0:T(8,128)(2,1)S(1)} %get-tuple-element.76), channel_id=1, source_target_pairs={{0,4},{4,0},{64,68},{68,64},{8,12},{12,8},{72,76},{76,72},{1,5},{5... | collective-permute-start | bytes 3145736 | tf_op jit(solution)/shard_map/ppermute | solution.py:81
  66.0 3.8 %collective-permute-start.18 = (bf16[256,2048]{1,0:T(8,128)(2,1)S(1)}, bf16[256,2048]{1,0:T(8,128)(2,1)S(1)}, u32[]{:S(2)}, u32[]{:S(2)}) collective-permute-start(bf16[256,2048]{1,0:T(8,128)(2,1)S(1)} %get-tuple-element.77), channel_id=1, source_target_pairs={{0,4},{4,0},{64,68},{68,64},{8,12},{12,8},{72,76},{76,72},{1,5},{5... | collective-permute-start | bytes 3145736 | tf_op jit(solution)/shard_map/ppermute | solution.py:81
  68.5 3.8 %collective-permute-start.14 = (bf16[256,2048]{1,0:T(8,128)(2,1)S(1)}, bf16[256,2048]{1,0:T(8,128)(2,1)S(1)}, u32[]{:S(2)}, u32[]{:S(2)}) collective-permute-start(bf16[256,2048]{1,0:T(8,128)(2,1)S(1)} %get-tuple-element.70), channel_id=1, source_target_pairs={{0,4},{4,0},{64,68},{68,64},{8,12},{12,8},{72,76},{76,72},{1,5},{5... | collective-permute-start | bytes 3145736 | tf_op jit(solution)/shard_map/ppermute | solution.py:81
  69.0 3.8 %collective-permute-start.15 = (bf16[256,2048]{1,0:T(8,128)(2,1)S(1)}, bf16[256,2048]{1,0:T(8,128)(2,1)S(1)}, u32[]{:S(2)}, u32[]{:S(2)}) collective-permute-start(bf16[256,2048]{1,0:T(8,128)(2,1)S(1)} %get-tuple-element.71), channel_id=1, source_target_pairs={{0,4},{4,0},{64,68},{68,64},{8,12},{12,8},{72,76},{76,72},{1,5},{5... | collective-permute-start | bytes 3145736 | tf_op jit(solution)/shard_map/ppermute | solution.py:81
  72.2 19.4 %collective-permute-start.22 = (bf16[256,2048]{1,0:T(8,128)(2,1)S(1)}, bf16[256,2048]{1,0:T(8,128)(2,1)S(1)}, u32[]{:S(2)}, u32[]{:S(2)}) collective-permute-start(bf16[256,2048]{1,0:T(8,128)(2,1)S(1)} %get-tuple-element.78.refs_19_), channel_id=1, source_target_pairs={{0,16},{4,52},{64,80},{68,116},{8,24},{12,60},{72,88},{76,124},{1,... | collective-permute-start | bytes 3145736 | tf_op jit(solution)/shard_map/ppermute | solution.py:81
  75.2 25.5 %collective-permute-start.16 = (bf16[256,2048]{1,0:T(8,128)(2,1)S(1)}, bf16[256,2048]{1,0:T(8,128)(2,1)S(1)}, u32[]{:S(2)}, u32[]{:S(2)}) collective-permute-start(bf16[256,2048]{1,0:T(8,128)(2,1)S(1)} %get-tuple-element.73.refs_18_), channel_id=1, source_target_pairs={{0,16},{4,52},{64,80},{68,116},{8,24},{12,60},{72,88},{76,124},{1,... | collective-permute-start | bytes 3145736 | tf_op jit(solution)/shard_map/ppermute | solution.py:81
  84.2 31.3 %collective-permute-start.29 = (bf16[512,2048]{1,0:T(8,128)(2,1)S(1)}, bf16[512,2048]{1,0:T(8,128)(2,1)S(1)}, u32[]{:S(2)}, u32[]{:S(2)}) collective-permute-start(bf16[512,2048]{1,0:T(8,128)(2,1)S(1)} %shard_map.87.refs_18_), channel_id=1, source_target_pairs={{0,1},{4,7},{64,65},{68,71},{8,9},{12,15},{72,73},{76,79},{1,0},{5... | collective-permute-start | bytes 6291464 | tf_op jit(solution)/shard_map/ppermute | solution.py:81
  91.8 12.7 %collective-permute-start.23 = (bf16[128,2048]{1,0:T(8,128)(2,1)S(1)}, bf16[128,2048]{1,0:T(8,128)(2,1)S(1)}, u32[]{:S(2)}, u32[]{:S(2)}) collective-permute-start(bf16[128,2048]{1,0:T(8,128)(2,1)S(1)} %get-tuple-element.83), channel_id=1, source_target_pairs={{0,48},{4,20},{64,112},{68,84},{8,56},{12,28},{72,120},{76,92},{1,... | collective-permute-start | bytes 1572872 | tf_op jit(solution)/shard_map/ppermute | solution.py:81
  100.9 10.5 %collective-permute-start.19 = (bf16[128,2048]{1,0:T(8,128)(2,1)S(1)}, bf16[128,2048]{1,0:T(8,128)(2,1)S(1)}, u32[]{:S(2)}, u32[]{:S(2)}) collective-permute-start(bf16[128,2048]{1,0:T(8,128)(2,1)S(1)} %get-tuple-element.80), channel_id=1, source_target_pairs={{0,48},{4,20},{64,112},{68,84},{8,56},{12,28},{72,120},{76,92},{1,... | collective-permute-start | bytes 1572872 | tf_op jit(solution)/shard_map/ppermute | solution.py:81
  104.7 10.6 %collective-permute-start.24 = (bf16[64,2048]{1,0:T(8,128)(2,1)S(1)}, bf16[64,2048]{1,0:T(8,128)(2,1)S(1)}, u32[]{:S(2)}, u32[]{:S(2)}) collective-permute-start(bf16[64,2048]{1,0:T(8,128)(2,1)S(1)} %slice.54), channel_id=1, source_target_pairs={{0,72},{4,68},{64,0},{68,12},{8,64},{12,76},{72,8},{76,4},{1,73},{... | collective-permute-start | bytes 786440 | tf_op jit(solution)/shard_map/ppermute | solution.py:81
  111.5 15.1 %collective-permute-start.20 = (bf16[64,2048]{1,0:T(8,128)(2,1)S(1)}, bf16[64,2048]{1,0:T(8,128)(2,1)S(1)}, u32[]{:S(2)}, u32[]{:S(2)}) collective-permute-start(bf16[64,2048]{1,0:T(8,128)(2,1)S(1)} %slice.55), channel_id=1, source_target_pairs={{0,72},{4,68},{64,0},{68,12},{8,64},{12,76},{72,8},{76,4},{1,73},{... | collective-permute-start | bytes 786440 | tf_op jit(solution)/shard_map/ppermute | solution.py:81
  115.3 11.4 %collective-permute-start.25 = (bf16[64,2048]{1,0:T(8,128)(2,1)S(1)}, bf16[64,2048]{1,0:T(8,128)(2,1)S(1)}, u32[]{:S(2)}, u32[]{:S(2)}) collective-permute-start(bf16[64,2048]{1,0:T(8,128)(2,1)S(1)} %fusion), channel_id=1, source_target_pairs={{0,8},{4,12},{64,72},{68,76},{8,0},{12,4},{72,64},{76,68},{1,9},{5... | collective-permute-start | bytes 786440 | tf_op jit(solution)/shard_map/ppermute | solution.py:81
  115.5 11.4 %collective-permute-start.32 = (bf16[512,512]{1,0:T(8,128)(2,1)S(1)}, bf16[512,512]{1,0:T(8,128)(2,1)S(1)}, u32[]{:S(2)}, u32[]{:S(2)}) collective-permute-start(bf16[512,512]{1,0:T(8,128)(2,1)S(1)} %get-tuple-element.89), channel_id=1, source_target_pairs={{0,3},{4,5},{64,67},{68,69},{8,11},{12,13},{72,75},{76,77},{1,2},{... | collective-permute-start | bytes 1572872 | tf_op jit(solution)/shard_map/ppermute | solution.py:81
  118.3 13.3 %collective-permute-start.30 = (bf16[512,512]{1,0:T(8,128)(2,1)S(1)}, bf16[512,512]{1,0:T(8,128)(2,1)S(1)}, u32[]{:S(2)}, u32[]{:S(2)}) collective-permute-start(bf16[512,512]{1,0:T(8,128)(2,1)S(1)} %get-tuple-element.91), channel_id=1, source_target_pairs={{0,3},{4,5},{64,67},{68,69},{8,11},{12,13},{72,75},{76,77},{1,2},{... | collective-permute-start | bytes 1572872 | tf_op jit(solution)/shard_map/ppermute | solution.py:81
  126.7 8.0 %collective-permute-start.21 = (bf16[64,2048]{1,0:T(8,128)(2,1)S(1)}, bf16[64,2048]{1,0:T(8,128)(2,1)S(1)}, u32[]{:S(2)}, u32[]{:S(2)}) collective-permute-start(bf16[64,2048]{1,0:T(8,128)(2,1)S(1)} %fusion.1), channel_id=1, source_target_pairs={{0,8},{4,12},{64,72},{68,76},{8,0},{12,4},{72,64},{76,68},{1,9},{5... | collective-permute-start | bytes 786440 | tf_op jit(solution)/shard_map/ppermute | solution.py:81
  126.8 7.9 %collective-permute-start.27 = (bf16[64,2048]{1,0:T(8,128)(2,1)S(1)}, bf16[64,2048]{1,0:T(8,128)(2,1)S(1)}, u32[]{:S(2)}, u32[]{:S(2)}) collective-permute-start(bf16[64,2048]{1,0:T(8,128)(2,1)S(1)} %add_convert_fusion.2.refs_1_), channel_id=1, source_target_pairs={{0,4},{4,0},{64,68},{68,64},{8,12},{12,8},{72,76},{76,72},{1,5},{5... | collective-permute-start | bytes 786440 | tf_op jit(solution)/shard_map/ppermute | solution.py:81
  126.9 10.5 %collective-permute-start.33 = (bf16[512,512]{1,0:T(8,128)(2,1)S(1)}, bf16[512,512]{1,0:T(8,128)(2,1)S(1)}, u32[]{:S(2)}, u32[]{:S(2)}) collective-permute-start(bf16[512,512]{1,0:T(8,128)(2,1)S(1)} %get-tuple-element.87), channel_id=1, source_target_pairs={{0,3},{4,5},{64,67},{68,69},{8,11},{12,13},{72,75},{76,77},{1,2},{... | collective-permute-start | bytes 1572872 | tf_op jit(solution)/shard_map/ppermute | solution.py:81
  131.6 11.4 %collective-permute-start.31 = (bf16[512,512]{1,0:T(8,128)(2,1)S(1)}, bf16[512,512]{1,0:T(8,128)(2,1)S(1)}, u32[]{:S(2)}, u32[]{:S(2)}) collective-permute-start(bf16[512,512]{1,0:T(8,128)(2,1)S(1)} %get-tuple-element.85), channel_id=1, source_target_pairs={{0,3},{4,5},{64,67},{68,69},{8,11},{12,13},{72,75},{76,77},{1,2},{... | collective-permute-start | bytes 1572872 | tf_op jit(solution)/shard_map/ppermute | solution.py:81
  134.7 1.6 %collective-permute-start.26 = (bf16[64,2048]{1,0:T(8,128)(2,1)S(1)}, bf16[64,2048]{1,0:T(8,128)(2,1)S(1)}, u32[]{:S(2)}, u32[]{:S(2)}) collective-permute-start(bf16[64,2048]{1,0:T(8,128)(2,1)S(1)} %add_convert_fusion.3.refs_0_), channel_id=1, source_target_pairs={{0,4},{4,0},{64,68},{68,64},{8,12},{12,8},{72,76},{76,72},{1,5},{5... | collective-permute-start | bytes 786440 | tf_op jit(solution)/shard_map/ppermute | solution.py:81

commit v4 on v3

--- a/solution.py
+++ b/solution.py
@@ -72,7 +72,6 @@
 Y_SECOND = pairs(lambda x, y, z, core: (x, partner(y, core, 1), z, core))
 ALONG_Z = pairs(lambda x, y, z, core: (x, y, z + 1 - 2 * core, core))
 BACK_Z = pairs(lambda x, y, z, core: (x, y, z - 1 + 2 * core, core))
-DIAGONAL = pairs(lambda x, y, z, core: (partner(x, core, 1), y, z + 1 - 2 * core, core))
 ACROSS_Z = pairs(lambda x, y, z, core: (x, y, z + 2, core))
 SWAP = pairs(lambda x, y, z, core: (x, y, z, 1 - core))
 
@@ -383,17 +382,17 @@
     kv_weight, queries, cotangent = load(kv_weight, queries, cotangent)
     g["a"] = send(tie(h["a"], kv_weight, queries), ALONG_Z)
     h["d"] = send(h["a"], X_SECOND)
-    g["b"] = send(h["b"], ALONG_Z)
-    g["d"] = send(h["a"], DIAGONAL)
+    g["d"] = send(g["a"], X_SECOND)
     h_too["a"] = send(h["a"], SWAP)
     h_too["b"] = send(h["b"], SWAP)
     g_too["o"] = send(g["o"], SWAP)
+    h_too["d"] = send(h["d"], SWAP)
+    g_too["a"] = send(g["a"], SWAP)
     done = [project((h["o"], h_too["o"], h["a"], h_too["a"]), kv_weight)]
+    g["b"] = send(tie(h["b"], g["a"], done[0][0]), ALONG_Z)
     done.append(project((g["o"], g_too["o"], h["b"], h_too["b"]), kv_weight))
-    h_too["d"] = send(tie(h["d"], done[0][0]), SWAP)
-    g_too["a"] = send(tie(g["a"], done[1][0]), SWAP)
     done.append(project((g["a"], g_too["a"], h["d"], h_too["d"]), kv_weight))
-    g_too["b"] = send(g["b"], SWAP)
+    g_too["b"] = send(tie(g["b"], done[1][0]), SWAP)
     g_too["d"] = send(tie(g["d"], done[2][0]), SWAP)
     done.append(project((g["b"], g_too["b"], g["d"], g_too["d"]), kv_weight))
     keys, values = zip(*done)
@@ -431,6 +430,8 @@
     mine, theirs = [], []
     for keep, out in zip(kept, x_out):
         held, going = add(keep, send(out, X_FIRST), (key_keep,))
+        if mine:
+            held = tie(held, key_in)
         total = held + send(going, X_SECOND).astype(F32)
         here = total[:half] + send(total[half:].astype(BF16), BACK_Z).astype(F32)
         here = here.astype(BF16)

time: 148 us -> 138 us (0.932); the launches traced: 145 us -> 137 us
  waiting for transfers between devices: 49.2 us -> 40.7 us
    ppermute x34, waiting for transfers between devices: 49.2 us -> 40.7 us  [send(): return lax.ppermute(array, ALL, route)]
  transfers between devices with their start and end apart: 34 -> 34, of which waited for: 18 -> 17; matrix products, arithmetic and copies ran while one was open for 1% -> 1% of each run, Pallas kernels for 22% -> 23%
where the time goes in v4:
time: 138 us; the launch traced here: 137 us
  starting transfers between devices  46.8 us (34%)
  Pallas kernels  42.4 us (31%)
  waiting for transfers between devices  40.7 us (29%)
  local copies, waits for them, and re-layouts  4.97 us (4%)
    ppermute x34, starting transfers between devices, send(): return lax.ppermute(array, ALL, route)  46.8 us
    ppermute x34, waiting for transfers between devices, send(): return lax.ppermute(array, ALL, route)  40.7 us
    pallas_call x16, Pallas kernels, call(): pl.pallas_call(reads, in_specs=[SCALARS] * index + [WHOLE] * (count - ind...  37 us
    pallas_call x2, Pallas kernels, share(): pl.pallas_call(functools.partial(share_body, part, len(seconds)), in_spec...  3.73 us
    unnamed x8, local copies, waits for them, and re-layouts  3.39 us
  transfers between devices with their start and end apart: 34, of which 17 were waited for; matrix products, arithmetic and copies ran while one was open for 1% of the time, Pallas kernels for 23%

profile of v4, /device:TPU:0, one launch (start us, length us, event | category | flops | bytes accessed | tf_op | source)
XLA Modules:
  0.0 137.3 jit_solution(4663141775662509189)
XLA Ops:
  2.2 1.6 %collective-permute-start = (bf16[64,4096]{1,0:T(8,128)(2,1)S(1)}, bf16[64,4096]{1,0:T(8,128)(2,1)S(1)}, u32[]{:S(2)}, u32[]{:S(2)}) collective-permute-start(bf16[64,4096]{1,0:T(8,128)(2,1)S(1)} %get-tuple-element.49.refs_0_.refs_2_), channel_id=1, source_target_pairs={{0,16},{4,52},{64,80},{68,116},{8,24},{12,60},{72,88},{76,124},{1,... | collective-permute-start | bytes 1572872 | tf_op jit(solution)/shard_map/ppermute | solution.py:80
  3.8 2.1 %collective-permute-start.4 = (bf16[64,4096]{1,0:T(8,128)(2,1)S(1)}, bf16[64,4096]{1,0:T(8,128)(2,1)S(1)}, u32[]{:S(2)}, u32[]{:S(2)}) collective-permute-start(bf16[64,4096]{1,0:T(8,128)(2,1)S(1)} %get-tuple-element.49.refs_0_.refs_2_), channel_id=1, source_target_pairs={{0,48},{4,20},{64,112},{68,84},{8,56},{12,28},{72,120},{76,92},{1,... | collective-permute-start | bytes 1572872 | tf_op jit(solution)/shard_map/ppermute | solution.py:80
  5.9 1.9 %collective-permute-start.2 = (bf16[64,4096]{1,0:T(8,128)(2,1)S(1)}, bf16[64,4096]{1,0:T(8,128)(2,1)S(1)}, u32[]{:S(2)}, u32[]{:S(2)}) collective-permute-start(bf16[64,4096]{1,0:T(8,128)(2,1)S(1)} %get-tuple-element.49.refs_0_.refs_2_), channel_id=1, source_target_pairs={{0,64},{4,76},{64,8},{68,4},{8,72},{12,68},{72,0},{76,12},{1,65},{... | collective-permute-start | bytes 1572872 | tf_op jit(solution)/shard_map/ppermute | solution.py:80
  7.8 3.4 %copy-done = bf16[1,2,4096,512]{3,2,1,0:T(8,128)(2,1)S(1)} copy-done((bf16[1,2,4096,512]{3,2,1,0:T(8,128)(2,1)S(1)}, bf16[1,2,4096,512]{3,2,1,0:T(8,128)(2,1)}, u32[]{:S(2)}) %copy-start) | copy-done | bytes 8388632
  11.8 4.1 %collective-permute-done.refs_2_.refs_6_ = bf16[64,4096]{1,0:T(8,128)(2,1)S(1)} collective-permute-done((bf16[64,4096]{1,0:T(8,128)(2,1)S(1)}, bf16[64,4096]{1,0:T(8,128)(2,1)S(1)}, u32[]{:S(2)}, u32[]{:S(2)}) %collective-permute-start) | collective-permute-done | bytes 524320 | tf_op jit(solution)/shard_map/ppermute | solution.py:80
  15.9 1.9 %collective-permute-start.6 = (bf16[64,4096]{1,0:T(8,128)(2,1)S(1)}, bf16[64,4096]{1,0:T(8,128)(2,1)S(1)}, u32[]{:S(2)}, u32[]{:S(2)}) collective-permute-start(bf16[64,4096]{1,0:T(8,128)(2,1)S(1)} %collective-permute-done.refs_2_.refs_6_), channel_id=1, source_target_pairs={{0,64},{4,76},{64,8},{68,4},{8,72},{12,68},{72,0},{76,12},{1,65},{... | collective-permute-start | bytes 1572872 | tf_op jit(solution)/shard_map/ppermute | solution.py:80
  17.9 2.9 %collective-permute-start.8 = (bf16[64,4096]{1,0:T(8,128)(2,1)S(1)}, bf16[64,4096]{1,0:T(8,128)(2,1)S(1)}, u32[]{:S(2)}, u32[]{:S(2)}) collective-permute-start(bf16[64,4096]{1,0:T(8,128)(2,1)S(1)} %collective-permute-done.refs_2_.refs_6_), channel_id=1, source_target_pairs={{0,48},{4,20},{64,112},{68,84},{8,56},{12,28},{72,120},{76,92},{1,... | collective-permute-start | bytes 1572872 | tf_op jit(solution)/shard_map/ppermute | solution.py:80
  20.8 1.6 %collective-permute-start.5 = (bf16[64,4096]{1,0:T(8,128)(2,1)S(1)}, bf16[64,4096]{1,0:T(8,128)(2,1)S(1)}, u32[]{:S(2)}, u32[]{:S(2)}) collective-permute-start(bf16[64,4096]{1,0:T(8,128)(2,1)S(1)} %collective-permute-done.4.refs_2_.refs_4_), channel_id=1, source_target_pairs={{0,4},{4,0},{64,68},{68,64},{8,12},{12,8},{72,76},{76,72},{1,5},{5... | collective-permute-start | bytes 1572872 | tf_op jit(solution)/shard_map/ppermute | solution.py:80
  22.5 2.3 %shard_map.76 = (bf16[256,512]{1,0:T(8,128)(2,1)S(1)}, bf16[256,512]{1,0:T(8,128)(2,1)S(1)}) custom-call(bf16[64,4096]{1,0:T(8,128)(2,1)S(1)} %get-tuple-element.49.refs_0_.refs_2_, bf16[64,4096]{1,0:T(8,128)(2,1)S(1)} %get-tuple-element.50.refs_1_.refs_10_, bf16[64,4096]{1,0:T(8,128)(2,1)S(1)} %collective-permute-done.refs_2_.refs_6_, ...), custom_call_target="tpu_custom_call" | custom-call | flops 1000 | bytes 1000 | tf_op jit(solution)/shard_map/pallas_call | solution.py:32
  24.8 2.3 %collective-permute-done.6.refs_0_.refs_7_ = bf16[64,4096]{1,0:T(8,128)(2,1)S(1)} collective-permute-done((bf16[64,4096]{1,0:T(8,128)(2,1)S(1)}, bf16[64,4096]{1,0:T(8,128)(2,1)S(1)}, u32[]{:S(2)}, u32[]{:S(2)}) %collective-permute-start.6) | collective-permute-done | bytes 524320 | tf_op jit(solution)/shard_map/ppermute | solution.py:80
  28.2 1.5 %collective-permute-start.9 = (bf16[64,4096]{1,0:T(8,128)(2,1)S(1)}, bf16[64,4096]{1,0:T(8,128)(2,1)S(1)}, u32[]{:S(2)}, u32[]{:S(2)}) collective-permute-start(bf16[64,4096]{1,0:T(8,128)(2,1)S(1)} %collective-permute-done.8.refs_2_.refs_8_), channel_id=1, source_target_pairs={{0,4},{4,0},{64,68},{68,64},{8,12},{12,8},{72,76},{76,72},{1,5},{5... | collective-permute-start | bytes 1572872 | tf_op jit(solution)/shard_map/ppermute | solution.py:80
  29.8 2.9 %collective-permute-start.12 = (bf16[64,4096]{1,0:T(8,128)(2,1)S(1)}, bf16[64,4096]{1,0:T(8,128)(2,1)S(1)}, u32[]{:S(2)}, u32[]{:S(2)}) collective-permute-start(bf16[64,4096]{1,0:T(8,128)(2,1)S(1)} %collective-permute-done.6.refs_0_.refs_7_), channel_id=1, source_target_pairs={{0,48},{4,20},{64,112},{68,84},{8,56},{12,28},{72,120},{76,92},{1,... | collective-permute-start | bytes 1572872 | tf_op jit(solution)/shard_map/ppermute | solution.py:80
  32.7 2.3 %shard_map.77 = (bf16[256,512]{1,0:T(8,128)(2,1)S(1)}, bf16[256,512]{1,0:T(8,128)(2,1)S(1)}) custom-call(bf16[64,4096]{1,0:T(8,128)(2,1)S(1)} %collective-permute-done.2.refs_0_.refs_3_, bf16[64,4096]{1,0:T(8,128)(2,1)S(1)} %collective-permute-done.3.refs_1_.refs_11_, bf16[64,4096]{1,0:T(8,128)(2,1)S(1)} %collective-permute-done.4.refs_2_.refs_4_, ...), custom_call_target="tpu_custom_call" | custom-call | flops 1000 | bytes 1000 | tf_op jit(solution)/shard_map/pallas_call | solution.py:32
  35.0 2.5 %collective-permute-done.10.refs_0_.refs_5_ = bf16[64,4096]{1,0:T(8,128)(2,1)S(1)} collective-permute-done((bf16[64,4096]{1,0:T(8,128)(2,1)S(1)}, bf16[64,4096]{1,0:T(8,128)(2,1)S(1)}, u32[]{:S(2)}, u32[]{:S(2)}) %collective-permute-start.10) | collective-permute-done | bytes 524320 | tf_op jit(solution)/shard_map/ppermute | solution.py:80
  37.5 2.3 %shard_map.78 = (bf16[256,512]{1,0:T(8,128)(2,1)S(1)}, bf16[256,512]{1,0:T(8,128)(2,1)S(1)}) custom-call(bf16[64,4096]{1,0:T(8,128)(2,1)S(1)} %collective-permute-done.6.refs_0_.refs_7_, bf16[64,4096]{1,0:T(8,128)(2,1)S(1)} %collective-permute-done.7.refs_1_.refs_15_, bf16[64,4096]{1,0:T(8,128)(2,1)S(1)} %collective-permute-done.8.refs_2_.refs_8_, ...), custom_call_target="tpu_custom_call" | custom-call | flops 1000 | bytes 1000 | tf_op jit(solution)/shard_map/pallas_call | solution.py:32
  40.6 1.5 %collective-permute-done.13.refs_3_.refs_17_ = bf16[64,4096]{1,0:T(8,128)(2,1)S(1)} collective-permute-done((bf16[64,4096]{1,0:T(8,128)(2,1)S(1)}, bf16[64,4096]{1,0:T(8,128)(2,1)S(1)}, u32[]{:S(2)}, u32[]{:S(2)}) %collective-permute-start.13) | collective-permute-done | bytes 524320 | tf_op jit(solution)/shard_map/ppermute | solution.py:80
  42.2 2.3 %shard_map.79 = (bf16[256,512]{1,0:T(8,128)(2,1)S(1)}, bf16[256,512]{1,0:T(8,128)(2,1)S(1)}) custom-call(bf16[64,4096]{1,0:T(8,128)(2,1)S(1)} %collective-permute-done.10.refs_0_.refs_5_, bf16[64,4096]{1,0:T(8,128)(2,1)S(1)} %collective-permute-done.11.refs_1_.refs_13_, bf16[64,4096]{1,0:T(8,128)(2,1)S(1)} %collective-permute-done.12.refs_2_.refs_9_, ...), custom_call_target="tpu_custom_call" | custom-call | flops 1000 | bytes 1000 | tf_op jit(solution)/shard_map/pallas_call | solution.py:32
  44.5 3.6 %shard_map.80 = (bf16[1,1,512,512]{3,2,1,0:T(8,128)(2,1)}, f32[2,512,1024]{2,1,0:T(8,128)S(1)}, bf16[1024,512]{1,0:T(8,128)(2,1)S(1)}, bf16[512,1024]{1,0:T(8,128)(2,1)S(1)}) custom-call(bf16[1,1,512,512]{3,2,1,0:T(8,128)(2,1)S(1)} %get-tuple-element.47.refs_0_, bf16[1,1,512,512]{3,2,1,0:T(8,128)(2,1)S(1)} %get-tuple-element.48.refs_1_, ...), custom_call_target="tpu_custom_call" | custom-call | flops 1000 | bytes 1000 | tf_op jit(solution)/shard_map/pallas_call | solution.py:32
  48.1 2.9 %shard_map.81.refs_12_ = bf16[512,2048]{1,0:T(8,128)(2,1)S(1)} custom-call(s32[4]{0:T(128)S(1)} %get-tuple-element.66.refs_0_, bf16[512,1024]{1,0:T(8,128)(2,1)S(1)} %get-tuple-element.67.refs_1_, bf16[64,4096]{1,0:T(8,128)(2,1)S(1)} %get-tuple-element.49.refs_0_.refs_2_, bf16[64,4096]{1,0:T(8,128)(2,1)S(1)} %collective-permute-done.2.refs_0_.refs_3_, ...), custom_call_target="tpu_custom_call" | custom-call | flops 1000 | bytes 1000 | tf_op jit(solution)/shard_map/pallas_call | solution.py:32
  51.0 1.7 %collective-permute-start.23 = (bf16[512,2048]{1,0:T(8,128)(2,1)S(1)}, bf16[512,2048]{1,0:T(8,128)(2,1)S(1)}, u32[]{:S(2)}, u32[]{:S(2)}) collective-permute-start(bf16[512,2048]{1,0:T(8,128)(2,1)S(1)} %shard_map.81.refs_12_), channel_id=1, source_target_pairs={{0,1},{4,7},{64,65},{68,71},{8,9},{12,15},{72,73},{76,79},{1,0},{5... | collective-permute-start | bytes 6291464 | tf_op jit(solution)/shard_map/ppermute | solution.py:80
  52.6 2.6 %shard_map.82 = (bf16[1,1,512,512]{3,2,1,0:T(8,128)(2,1)}, bf16[1024,512]{1,0:T(8,128)(2,1)S(1)}, bf16[512,1024]{1,0:T(8,128)(2,1)S(1)}) custom-call(bf16[1,1,512,512]{3,2,1,0:T(8,128)(2,1)S(1)} %get-tuple-element.47.refs_0_, bf16[1,1,512,512]{3,2,1,0:T(8,128)(2,1)S(1)} %get-tuple-element.48.refs_1_, bf16[256,512]{1,0:T(8,128)(2,1)S(1)} %get-tuple-element.52.refs_2_, ...), custom_call_target="tpu_custom_call" | custom-call | flops 1000 | bytes 1000 | tf_op jit(solution)/shard_map/pallas_call | solution.py:32
  55.2 2.4 %shard_map.83 = (bf16[256,2048]{1,0:T(8,128)(2,1)S(1)}, bf16[256,2048]{1,0:T(8,128)(2,1)S(1)}) custom-call(bf16[1024,512]{1,0:T(8,128)(2,1)S(1)} %get-tuple-element.69.refs_0_, bf16[1024,512]{1,0:T(8,128)(2,1)S(1)} %get-tuple-element.70.refs_1_, bf16[1,2,4096,512]{3,2,1,0:T(8,128)(2,1)S(1)} %get-tuple-element.51.refs_4_.refs_2_), custom_call_target="tpu_custom_call" | custom-call | flops 1000 | bytes 1000 | tf_op jit(solution)/shard_map/pallas_call | solution.py:32
  57.6 1.6 %collective-permute-start.14 = (bf16[256,2048]{1,0:T(8,128)(2,1)S(1)}, bf16[256,2048]{1,0:T(8,128)(2,1)S(1)}, u32[]{:S(2)}, u32[]{:S(2)}) collective-permute-start(bf16[256,2048]{1,0:T(8,128)(2,1)S(1)} %get-tuple-element.71), channel_id=1, source_target_pairs={{0,4},{4,0},{64,68},{68,64},{8,12},{12,8},{72,76},{76,72},{1,5},{5... | collective-permute-start | bytes 3145736 | tf_op jit(solution)/shard_map/ppermute | solution.py:80
  59.3 2.4 %shard_map.85 = (bf16[256,2048]{1,0:T(8,128)(2,1)S(1)}, bf16[256,2048]{1,0:T(8,128)(2,1)S(1)}) custom-call(bf16[1024,512]{1,0:T(8,128)(2,1)S(1)} %get-tuple-element.69.refs_0_, bf16[1024,512]{1,0:T(8,128)(2,1)S(1)} %get-tuple-element.70.refs_1_, bf16[1,2,4096,512]{3,2,1,0:T(8,128)(2,1)S(1)} %get-tuple-element.51.refs_4_.refs_2_), custom_call_target="tpu_custom_call" | custom-call | flops 1000 | bytes 1000 | tf_op jit(solution)/shard_map/pallas_call | solution.py:32
  63.0 2.4 %shard_map.84 = (bf16[256,2048]{1,0:T(8,128)(2,1)S(1)}, bf16[256,2048]{1,0:T(8,128)(2,1)S(1)}) custom-call(bf16[1024,512]{1,0:T(8,128)(2,1)S(1)} %get-tuple-element.69.refs_0_, bf16[1024,512]{1,0:T(8,128)(2,1)S(1)} %get-tuple-element.70.refs_1_, bf16[1,2,4096,512]{3,2,1,0:T(8,128)(2,1)S(1)} %get-tuple-element.51.refs_4_.refs_2_, ...), custom_call_target="tpu_custom_call" | custom-call | flops 1000 | bytes 1000 | tf_op jit(solution)/shard_map/pallas_call | solution.py:32
  65.3 2.6 %collective-permute-start.16 = (bf16[256,2048]{1,0:T(8,128)(2,1)S(1)}, bf16[256,2048]{1,0:T(8,128)(2,1)S(1)}, u32[]{:S(2)}, u32[]{:S(2)}) collective-permute-start(bf16[256,2048]{1,0:T(8,128)(2,1)S(1)} %get-tuple-element.74.refs_18_), channel_id=1, source_target_pairs={{0,16},{4,52},{64,80},{68,116},{8,24},{12,60},{72,88},{76,124},{1,... | collective-permute-start | bytes 3145736 | tf_op jit(solution)/shard_map/ppermute | solution.py:80
  67.9 2.4 %shard_map.86 = (bf16[256,2048]{1,0:T(8,128)(2,1)S(1)}, bf16[256,2048]{1,0:T(8,128)(2,1)S(1)}) custom-call(bf16[1024,512]{1,0:T(8,128)(2,1)S(1)} %get-tuple-element.69.refs_0_, bf16[1024,512]{1,0:T(8,128)(2,1)S(1)} %get-tuple-element.70.refs_1_, bf16[1,2,4096,512]{3,2,1,0:T(8,128)(2,1)S(1)} %get-tuple-element.51.refs_4_.refs_2_, ...), custom_call_target="tpu_custom_call" | custom-call | flops 1000 | bytes 1000 | tf_op jit(solution)/shard_map/pallas_call | solution.py:32
  70.9 2.9 %shard_map.87.refs_18_ = bf16[512,2048]{1,0:T(8,128)(2,1)S(1)} custom-call(s32[4]{0:T(128)S(1)} %get-tuple-element.66.refs_0_, bf16[512,1024]{1,0:T(8,128)(2,1)S(1)} %get-tuple-element.76.refs_1_, bf16[64,4096]{1,0:T(8,128)(2,1)S(1)} %get-tuple-element.49.refs_0_.refs_2_, bf16[64,4096]{1,0:T(8,128)(2,1)S(1)} %collective-permute-done.2.refs_0_.refs_3_, ...), custom_call_target="tpu_custom_call" | custom-call | flops 1000 | bytes 1000 | tf_op jit(solution)/shard_map/pallas_call | solution.py:32
  73.9 3.2 %collective-permute-done.23.first = bf16[512,2048]{1,0:T(8,128)(2,1)S(1)} collective-permute-done((bf16[512,2048]{1,0:T(8,128)(2,1)S(1)}, bf16[512,2048]{1,0:T(8,128)(2,1)S(1)}, u32[]{:S(2)}, u32[]{:S(2)}) %collective-permute-start.23) | collective-permute-done | bytes 2097184 | tf_op jit(solution)/shard_map/ppermute | solution.py:80
  77.1 1.6 %collective-permute-start.24 = (bf16[512,2048]{1,0:T(8,128)(2,1)S(1)}, bf16[512,2048]{1,0:T(8,128)(2,1)S(1)}, u32[]{:S(2)}, u32[]{:S(2)}) collective-permute-start(bf16[512,2048]{1,0:T(8,128)(2,1)S(1)} %shard_map.87.refs_18_), channel_id=1, source_target_pairs={{0,1},{4,7},{64,65},{68,71},{8,9},{12,15},{72,73},{76,79},{1,0},{5... | collective-permute-start | bytes 6291464 | tf_op jit(solution)/shard_map/ppermute | solution.py:80
  78.7 2.9 %shard_map.88.refs_18_.keep = bf16[512,2048]{1,0:T(8,128)(2,1)S(1)} custom-call(s32[4]{0:T(128)S(1)} %get-tuple-element.75.refs_0_, bf16[512,1024]{1,0:T(8,128)(2,1)S(1)} %get-tuple-element.67.refs_1_, bf16[64,4096]{1,0:T(8,128)(2,1)S(1)} %get-tuple-element.49.refs_0_.refs_2_, bf16[64,4096]{1,0:T(8,128)(2,1)S(1)} %collective-permute-done.2.refs_0_.refs_3_, ...), custom_call_target="tpu_custom_call" | custom-call | flops 1000 | bytes 1000 | tf_op jit(solution)/shard_map/pallas_call | solution.py:32
  81.6 2.9 %shard_map.89.refs_2_.keep = bf16[512,2048]{1,0:T(8,128)(2,1)S(1)} custom-call(s32[4]{0:T(128)S(1)} %get-tuple-element.75.refs_0_, bf16[512,1024]{1,0:T(8,128)(2,1)S(1)} %get-tuple-element.76.refs_1_, bf16[64,4096]{1,0:T(8,128)(2,1)S(1)} %get-tuple-element.49.refs_0_.refs_2_, bf16[64,4096]{1,0:T(8,128)(2,1)S(1)} %collective-permute-done.2.refs_0_.refs_3_, ...), custom_call_target="tpu_custom_call" | custom-call | flops 1000 | bytes 1000 | tf_op jit(solution)/shard_map/pallas_call | solution.py:32
  84.7 3.0 %collective-permute-start.19 = (bf16[128,2048]{1,0:T(8,128)(2,1)S(1)}, bf16[128,2048]{1,0:T(8,128)(2,1)S(1)}, u32[]{:S(2)}, u32[]{:S(2)}) collective-permute-start(bf16[128,2048]{1,0:T(8,128)(2,1)S(1)} %get-tuple-element.81), channel_id=1, source_target_pairs={{0,48},{4,20},{64,112},{68,84},{8,56},{12,28},{72,120},{76,92},{1,... | collective-permute-start | bytes 1572872 | tf_op jit(solution)/shard_map/ppermute | solution.py:80
  87.8 6.2 %collective-permute-done.22.refs_1_ = bf16[256,2048]{1,0:T(8,128)(2,1)S(1)} collective-permute-done((bf16[256,2048]{1,0:T(8,128)(2,1)S(1)}, bf16[256,2048]{1,0:T(8,128)(2,1)S(1)}, u32[]{:S(2)}, u32[]{:S(2)}) %collective-permute-start.22) | collective-permute-done | bytes 1048608 | tf_op jit(solution)/shard_map/ppermute | solution.py:80
  94.2 2.8 %collective-permute-start.25 = (bf16[128,2048]{1,0:T(8,128)(2,1)S(1)}, bf16[128,2048]{1,0:T(8,128)(2,1)S(1)}, u32[]{:S(2)}, u32[]{:S(2)}) collective-permute-start(bf16[128,2048]{1,0:T(8,128)(2,1)S(1)} %get-tuple-element.86), channel_id=1, source_target_pairs={{0,48},{4,20},{64,112},{68,84},{8,56},{12,28},{72,120},{76,92},{1,... | collective-permute-start | bytes 1572872 | tf_op jit(solution)/shard_map/ppermute | solution.py:80
  97.8 1.7 %collective-permute-start.20 = (bf16[64,2048]{1,0:T(8,128)(2,1)S(1)}, bf16[64,2048]{1,0:T(8,128)(2,1)S(1)}, u32[]{:S(2)}, u32[]{:S(2)}) collective-permute-start(bf16[64,2048]{1,0:T(8,128)(2,1)S(1)} %slice.55), channel_id=1, source_target_pairs={{0,72},{4,68},{64,0},{68,12},{8,64},{12,76},{72,8},{76,4},{1,73},{... | collective-permute-start | bytes 786440 | tf_op jit(solution)/shard_map/ppermute | solution.py:80
  100.0 4.3 %collective-permute-done.20 = bf16[64,2048]{1,0:T(8,128)(2,1)S(1)} collective-permute-done((bf16[64,2048]{1,0:T(8,128)(2,1)S(1)}, bf16[64,2048]{1,0:T(8,128)(2,1)S(1)}, u32[]{:S(2)}, u32[]{:S(2)}) %collective-permute-start.20) | collective-permute-done | bytes 262176 | tf_op jit(solution)/shard_map/ppermute | solution.py:80
  104.3 2.3 %collective-permute-start.21 = (bf16[64,2048]{1,0:T(8,128)(2,1)S(1)}, bf16[64,2048]{1,0:T(8,128)(2,1)S(1)}, u32[]{:S(2)}, u32[]{:S(2)}) collective-permute-start(bf16[64,2048]{1,0:T(8,128)(2,1)S(1)} %fusion.1), channel_id=1, source_target_pairs={{0,8},{4,12},{64,72},{68,76},{8,0},{12,4},{72,64},{76,68},{1,9},{5... | collective-permute-start | bytes 786440 | tf_op jit(solution)/shard_map/ppermute | solution.py:80
  108.0 1.6 %collective-permute-start.32 = (bf16[512,512]{1,0:T(8,128)(2,1)S(1)}, bf16[512,512]{1,0:T(8,128)(2,1)S(1)}, u32[]{:S(2)}, u32[]{:S(2)}) collective-permute-start(bf16[512,512]{1,0:T(8,128)(2,1)S(1)} %get-tuple-element.91), channel_id=1, source_target_pairs={{0,3},{4,5},{64,67},{68,69},{8,11},{12,13},{72,75},{76,77},{1,2},{... | collective-permute-start | bytes 1572872 | tf_op jit(solution)/shard_map/ppermute | solution.py:80
  110.1 1.9 %collective-permute-start.30 = (bf16[512,512]{1,0:T(8,128)(2,1)S(1)}, bf16[512,512]{1,0:T(8,128)(2,1)S(1)}, u32[]{:S(2)}, u32[]{:S(2)}) collective-permute-start(bf16[512,512]{1,0:T(8,128)(2,1)S(1)} %get-tuple-element.93), channel_id=1, source_target_pairs={{0,3},{4,5},{64,67},{68,69},{8,11},{12,13},{72,75},{76,77},{1,2},{... | collective-permute-start | bytes 1572872 | tf_op jit(solution)/shard_map/ppermute | solution.py:80
  112.0 3.3 %collective-permute-done.26 = bf16[64,2048]{1,0:T(8,128)(2,1)S(1)} collective-permute-done((bf16[64,2048]{1,0:T(8,128)(2,1)S(1)}, bf16[64,2048]{1,0:T(8,128)(2,1)S(1)}, u32[]{:S(2)}, u32[]{:S(2)}) %collective-permute-start.26) | collective-permute-done | bytes 262176 | tf_op jit(solution)/shard_map/ppermute | solution.py:80
  115.4 1.7 %collective-permute-start.27 = (bf16[64,2048]{1,0:T(8,128)(2,1)S(1)}, bf16[64,2048]{1,0:T(8,128)(2,1)S(1)}, u32[]{:S(2)}, u32[]{:S(2)}) collective-permute-start(bf16[64,2048]{1,0:T(8,128)(2,1)S(1)} %fusion), channel_id=1, source_target_pairs={{0,8},{4,12},{64,72},{68,76},{8,0},{12,4},{72,64},{76,68},{1,9},{5... | collective-permute-start | bytes 786440 | tf_op jit(solution)/shard_map/ppermute | solution.py:80
  118.4 1.6 %collective-permute-start.33 = (bf16[512,512]{1,0:T(8,128)(2,1)S(1)}, bf16[512,512]{1,0:T(8,128)(2,1)S(1)}, u32[]{:S(2)}, u32[]{:S(2)}) collective-permute-start(bf16[512,512]{1,0:T(8,128)(2,1)S(1)} %get-tuple-element.89), channel_id=1, source_target_pairs={{0,3},{4,5},{64,67},{68,69},{8,11},{12,13},{72,75},{76,77},{1,2},{... | collective-permute-start | bytes 1572872 | tf_op jit(solution)/shard_map/ppermute | solution.py:80
  120.0 4.0 %collective-permute-done.30.refs_0_ = bf16[512,512]{1,0:T(8,128)(2,1)S(1)} collective-permute-done((bf16[512,512]{1,0:T(8,128)(2,1)S(1)}, bf16[512,512]{1,0:T(8,128)(2,1)S(1)}, u32[]{:S(2)}, u32[]{:S(2)}) %collective-permute-start.30) | collective-permute-done | bytes 524320 | tf_op jit(solution)/shard_map/ppermute | solution.py:80
  124.0 1.6 %collective-permute-start.31 = (bf16[512,512]{1,0:T(8,128)(2,1)S(1)}, bf16[512,512]{1,0:T(8,128)(2,1)S(1)}, u32[]{:S(2)}, u32[]{:S(2)}) collective-permute-start(bf16[512,512]{1,0:T(8,128)(2,1)S(1)} %get-tuple-element.87), channel_id=1, source_target_pairs={{0,3},{4,5},{64,67},{68,69},{8,11},{12,13},{72,75},{76,77},{1,2},{... | collective-permute-start | bytes 1572872 | tf_op jit(solution)/shard_map/ppermute | solution.py:80
  129.6 1.9 %shard_map.93.refs_2_ = bf16[1,2,1024,512]{3,2,1,0:T(8,128)(2,1)} custom-call(bf16[512,2048]{1,0:T(8,128)(2,1)S(1)} %shard_map.88.refs_18_.keep, bf16[512,2048]{1,0:T(8,128)(2,1)S(1)} %collective-permute-done.23.first, bf16[512,512]{1,0:T(8,128)(2,1)S(1)} %collective-permute-done.32.refs_0_, bf16[512,512]{1,0:T(8,128)(2,1)S(1)} %collective-permute-done.33.refs_1_), custom_call_target="tpu_custom_call" | custom-call | flops 1000 | bytes 1000 | tf_op jit(solution)/shard_map/pallas_call | solution.py:242
  131.5 3.7 %collective-permute-done.31.refs_1_ = bf16[512,512]{1,0:T(8,128)(2,1)S(1)} collective-permute-done((bf16[512,512]{1,0:T(8,128)(2,1)S(1)}, bf16[512,512]{1,0:T(8,128)(2,1)S(1)}, u32[]{:S(2)}, u32[]{:S(2)}) %collective-permute-start.31) | collective-permute-done | bytes 524320 | tf_op jit(solution)/shard_map/ppermute | solution.py:80
  135.2 1.9 %shard_map.94 = bf16[1,2,1024,512]{3,2,1,0:T(8,128)(2,1)} custom-call(bf16[512,2048]{1,0:T(8,128)(2,1)S(1)} %shard_map.89.refs_2_.keep, bf16[512,2048]{1,0:T(8,128)(2,1)S(1)} %collective-permute-done.24.first, bf16[512,512]{1,0:T(8,128)(2,1)S(1)} %collective-permute-done.30.refs_0_, ...), custom_call_target="tpu_custom_call", output_to_operand_aliasing={{}: (4, {})} | custom-call | flops 1000 | bytes 1000 | tf_op jit(solution)/shard_map/pallas_call | solution.py:242
  (62 shorter events, 14.8 us)
Async XLA Ops:
  0.6 7.1 %copy-start.2 = (bf16[1,1,512,512]{3,2,1,0:T(8,128)(2,1)S(1)}, bf16[1,1,512,512]{3,2,1,0:T(8,128)(2,1)}, u32[]{:S(2)}) copy-start(bf16[1,1,512,512]{3,2,1,0:T(8,128)(2,1)} %refs_2_.1) | copy-start | bytes 1572868
  0.6 7.1 %copy-start.1 = (bf16[1,1,512,512]{3,2,1,0:T(8,128)(2,1)S(1)}, bf16[1,1,512,512]{3,2,1,0:T(8,128)(2,1)}, u32[]{:S(2)}) copy-start(bf16[1,1,512,512]{3,2,1,0:T(8,128)(2,1)} %refs_1_.1) | copy-start | bytes 1572868
  2.2 13.8 %collective-permute-start = (bf16[64,4096]{1,0:T(8,128)(2,1)S(1)}, bf16[64,4096]{1,0:T(8,128)(2,1)S(1)}, u32[]{:S(2)}, u32[]{:S(2)}) collective-permute-start(bf16[64,4096]{1,0:T(8,128)(2,1)S(1)} %get-tuple-element.49.refs_0_.refs_2_), channel_id=1, source_target_pairs={{0,16},{4,52},{64,80},{68,116},{8,24},{12,60},{72,88},{76,124},{1,... | collective-permute-start | bytes 1572872 | tf_op jit(solution)/shard_map/ppermute | solution.py:80
  3.8 17.1 %collective-permute-start.4 = (bf16[64,4096]{1,0:T(8,128)(2,1)S(1)}, bf16[64,4096]{1,0:T(8,128)(2,1)S(1)}, u32[]{:S(2)}, u32[]{:S(2)}) collective-permute-start(bf16[64,4096]{1,0:T(8,128)(2,1)S(1)} %get-tuple-element.49.refs_0_.refs_2_), channel_id=1, source_target_pairs={{0,48},{4,20},{64,112},{68,84},{8,56},{12,28},{72,120},{76,92},{1,... | collective-permute-start | bytes 1572872 | tf_op jit(solution)/shard_map/ppermute | solution.py:80
  5.9 16.6 %collective-permute-start.2 = (bf16[64,4096]{1,0:T(8,128)(2,1)S(1)}, bf16[64,4096]{1,0:T(8,128)(2,1)S(1)}, u32[]{:S(2)}, u32[]{:S(2)}) collective-permute-start(bf16[64,4096]{1,0:T(8,128)(2,1)S(1)} %get-tuple-element.49.refs_0_.refs_2_), channel_id=1, source_target_pairs={{0,64},{4,76},{64,8},{68,4},{8,72},{12,68},{72,0},{76,12},{1,65},{... | collective-permute-start | bytes 1572872 | tf_op jit(solution)/shard_map/ppermute | solution.py:80
  7.8 3.4 %copy-start = (bf16[1,2,4096,512]{3,2,1,0:T(8,128)(2,1)S(1)}, bf16[1,2,4096,512]{3,2,1,0:T(8,128)(2,1)}, u32[]{:S(2)}) copy-start(bf16[1,2,4096,512]{3,2,1,0:T(8,128)(2,1)} %refs_0_.1) | copy-start | bytes 25165828
  15.9 6.6 %collective-permute-start.1 = (bf16[64,4096]{1,0:T(8,128)(2,1)S(1)}, bf16[64,4096]{1,0:T(8,128)(2,1)S(1)}, u32[]{:S(2)}, u32[]{:S(2)}) collective-permute-start(bf16[64,4096]{1,0:T(8,128)(2,1)S(1)} %collective-permute-done.refs_2_.refs_6_), channel_id=1, source_target_pairs={{0,4},{4,0},{64,68},{68,64},{8,12},{12,8},{72,76},{76,72},{1,5},{5... | collective-permute-start | bytes 1572872 | tf_op jit(solution)/shard_map/ppermute | solution.py:80
  15.9 11.2 %collective-permute-start.6 = (bf16[64,4096]{1,0:T(8,128)(2,1)S(1)}, bf16[64,4096]{1,0:T(8,128)(2,1)S(1)}, u32[]{:S(2)}, u32[]{:S(2)}) collective-permute-start(bf16[64,4096]{1,0:T(8,128)(2,1)S(1)} %collective-permute-done.refs_2_.refs_6_), channel_id=1, source_target_pairs={{0,64},{4,76},{64,8},{68,4},{8,72},{12,68},{72,0},{76,12},{1,65},{... | collective-permute-start | bytes 1572872 | tf_op jit(solution)/shard_map/ppermute | solution.py:80
  17.9 10.4 %collective-permute-start.8 = (bf16[64,4096]{1,0:T(8,128)(2,1)S(1)}, bf16[64,4096]{1,0:T(8,128)(2,1)S(1)}, u32[]{:S(2)}, u32[]{:S(2)}) collective-permute-start(bf16[64,4096]{1,0:T(8,128)(2,1)S(1)} %collective-permute-done.refs_2_.refs_6_), channel_id=1, source_target_pairs={{0,48},{4,20},{64,112},{68,84},{8,56},{12,28},{72,120},{76,92},{1,... | collective-permute-start | bytes 1572872 | tf_op jit(solution)/shard_map/ppermute | solution.py:80
  20.8 8.9 %collective-permute-start.5 = (bf16[64,4096]{1,0:T(8,128)(2,1)S(1)}, bf16[64,4096]{1,0:T(8,128)(2,1)S(1)}, u32[]{:S(2)}, u32[]{:S(2)}) collective-permute-start(bf16[64,4096]{1,0:T(8,128)(2,1)S(1)} %collective-permute-done.4.refs_2_.refs_4_), channel_id=1, source_target_pairs={{0,4},{4,0},{64,68},{68,64},{8,12},{12,8},{72,76},{76,72},{1,5},{5... | collective-permute-start | bytes 1572872 | tf_op jit(solution)/shard_map/ppermute | solution.py:80
  22.4 10.3 %collective-permute-start.3 = (bf16[64,4096]{1,0:T(8,128)(2,1)S(1)}, bf16[64,4096]{1,0:T(8,128)(2,1)S(1)}, u32[]{:S(2)}, u32[]{:S(2)}) collective-permute-start(bf16[64,4096]{1,0:T(8,128)(2,1)S(1)} %collective-permute-done.2.refs_0_.refs_3_), channel_id=1, source_target_pairs={{0,4},{4,0},{64,68},{68,64},{8,12},{12,8},{72,76},{76,72},{1,5},{5... | collective-permute-start | bytes 1572872 | tf_op jit(solution)/shard_map/ppermute | solution.py:80
  27.1 10.4 %collective-permute-start.10 = (bf16[64,4096]{1,0:T(8,128)(2,1)S(1)}, bf16[64,4096]{1,0:T(8,128)(2,1)S(1)}, u32[]{:S(2)}, u32[]{:S(2)}) collective-permute-start(bf16[64,4096]{1,0:T(8,128)(2,1)S(1)} %collective-permute-done.4.refs_2_.refs_4_), channel_id=1, source_target_pairs={{0,64},{4,76},{64,8},{68,4},{8,72},{12,68},{72,0},{76,12},{1,65},{... | collective-permute-start | bytes 1572872 | tf_op jit(solution)/shard_map/ppermute | solution.py:80
  28.2 9.3 %collective-permute-start.9 = (bf16[64,4096]{1,0:T(8,128)(2,1)S(1)}, bf16[64,4096]{1,0:T(8,128)(2,1)S(1)}, u32[]{:S(2)}, u32[]{:S(2)}) collective-permute-start(bf16[64,4096]{1,0:T(8,128)(2,1)S(1)} %collective-permute-done.8.refs_2_.refs_8_), channel_id=1, source_target_pairs={{0,4},{4,0},{64,68},{68,64},{8,12},{12,8},{72,76},{76,72},{1,5},{5... | collective-permute-start | bytes 1572872 | tf_op jit(solution)/shard_map/ppermute | solution.py:80
  29.7 7.8 %collective-permute-start.7 = (bf16[64,4096]{1,0:T(8,128)(2,1)S(1)}, bf16[64,4096]{1,0:T(8,128)(2,1)S(1)}, u32[]{:S(2)}, u32[]{:S(2)}) collective-permute-start(bf16[64,4096]{1,0:T(8,128)(2,1)S(1)} %collective-permute-done.6.refs_0_.refs_7_), channel_id=1, source_target_pairs={{0,4},{4,0},{64,68},{68,64},{8,12},{12,8},{72,76},{76,72},{1,5},{5... | collective-permute-start | bytes 1572872 | tf_op jit(solution)/shard_map/ppermute | solution.py:80
  29.8 10.4 %collective-permute-start.12 = (bf16[64,4096]{1,0:T(8,128)(2,1)S(1)}, bf16[64,4096]{1,0:T(8,128)(2,1)S(1)}, u32[]{:S(2)}, u32[]{:S(2)}) collective-permute-start(bf16[64,4096]{1,0:T(8,128)(2,1)S(1)} %collective-permute-done.6.refs_0_.refs_7_), channel_id=1, source_target_pairs={{0,48},{4,20},{64,112},{68,84},{8,56},{12,28},{72,120},{76,92},{1,... | collective-permute-start | bytes 1572872 | tf_op jit(solution)/shard_map/ppermute | solution.py:80
  37.5 3.1 %collective-permute-start.11 = (bf16[64,4096]{1,0:T(8,128)(2,1)S(1)}, bf16[64,4096]{1,0:T(8,128)(2,1)S(1)}, u32[]{:S(2)}, u32[]{:S(2)}) collective-permute-start(bf16[64,4096]{1,0:T(8,128)(2,1)S(1)} %collective-permute-done.10.refs_0_.refs_5_), channel_id=1, source_target_pairs={{0,4},{4,0},{64,68},{68,64},{8,12},{12,8},{72,76},{76,72},{1,5},{5... | collective-permute-start | bytes 1572872 | tf_op jit(solution)/shard_map/ppermute | solution.py:80
  40.1 2.0 %collective-permute-start.13 = (bf16[64,4096]{1,0:T(8,128)(2,1)S(1)}, bf16[64,4096]{1,0:T(8,128)(2,1)S(1)}, u32[]{:S(2)}, u32[]{:S(2)}) collective-permute-start(bf16[64,4096]{1,0:T(8,128)(2,1)S(1)} %collective-permute-done.12.refs_2_.refs_9_), channel_id=1, source_target_pairs={{0,4},{4,0},{64,68},{68,64},{8,12},{12,8},{72,76},{76,72},{1,5},{5... | collective-permute-start | bytes 1572872 | tf_op jit(solution)/shard_map/ppermute | solution.py:80
  48.1 4.6 %copy-start.3 = (bf16[1,1,512,512]{3,2,1,0:T(8,128)(2,1)S(1)}, bf16[1,1,512,512]{3,2,1,0:T(8,128)(2,1)}, u32[]{:S(2)}) copy-start(bf16[1,1,512,512]{3,2,1,0:T(8,128)(2,1)} %get-tuple-element.43.refs_10_) | copy-start | bytes 1572868
  51.0 26.1 %collective-permute-start.23 = (bf16[512,2048]{1,0:T(8,128)(2,1)S(1)}, bf16[512,2048]{1,0:T(8,128)(2,1)S(1)}, u32[]{:S(2)}, u32[]{:S(2)}) collective-permute-start(bf16[512,2048]{1,0:T(8,128)(2,1)S(1)} %shard_map.81.refs_12_), channel_id=1, source_target_pairs={{0,1},{4,7},{64,65},{68,71},{8,9},{12,15},{72,73},{76,79},{1,0},{5... | collective-permute-start | bytes 6291464 | tf_op jit(solution)/shard_map/ppermute | solution.py:80
  57.6 4.9 %collective-permute-start.14 = (bf16[256,2048]{1,0:T(8,128)(2,1)S(1)}, bf16[256,2048]{1,0:T(8,128)(2,1)S(1)}, u32[]{:S(2)}, u32[]{:S(2)}) collective-permute-start(bf16[256,2048]{1,0:T(8,128)(2,1)S(1)} %get-tuple-element.71), channel_id=1, source_target_pairs={{0,4},{4,0},{64,68},{68,64},{8,12},{12,8},{72,76},{76,72},{1,5},{5... | collective-permute-start | bytes 3145736 | tf_op jit(solution)/shard_map/ppermute | solution.py:80
  59.2 3.8 %collective-permute-start.15 = (bf16[256,2048]{1,0:T(8,128)(2,1)S(1)}, bf16[256,2048]{1,0:T(8,128)(2,1)S(1)}, u32[]{:S(2)}, u32[]{:S(2)}) collective-permute-start(bf16[256,2048]{1,0:T(8,128)(2,1)S(1)} %get-tuple-element.72), channel_id=1, source_target_pairs={{0,4},{4,0},{64,68},{68,64},{8,12},{12,8},{72,76},{76,72},{1,5},{5... | collective-permute-start | bytes 3145736 | tf_op jit(solution)/shard_map/ppermute | solution.py:80
  61.6 6.3 %collective-permute-start.17 = (bf16[256,2048]{1,0:T(8,128)(2,1)S(1)}, bf16[256,2048]{1,0:T(8,128)(2,1)S(1)}, u32[]{:S(2)}, u32[]{:S(2)}) collective-permute-start(bf16[256,2048]{1,0:T(8,128)(2,1)S(1)} %get-tuple-element.77), channel_id=1, source_target_pairs={{0,4},{4,0},{64,68},{68,64},{8,12},{12,8},{72,76},{76,72},{1,5},{5... | collective-permute-start | bytes 3145736 | tf_op jit(solution)/shard_map/ppermute | solution.py:80
  62.1 5.8 %collective-permute-start.18 = (bf16[256,2048]{1,0:T(8,128)(2,1)S(1)}, bf16[256,2048]{1,0:T(8,128)(2,1)S(1)}, u32[]{:S(2)}, u32[]{:S(2)}) collective-permute-start(bf16[256,2048]{1,0:T(8,128)(2,1)S(1)} %get-tuple-element.78), channel_id=1, source_target_pairs={{0,4},{4,0},{64,68},{68,64},{8,12},{12,8},{72,76},{76,72},{1,5},{5... | collective-permute-start | bytes 3145736 | tf_op jit(solution)/shard_map/ppermute | solution.py:80
  65.3 19.2 %collective-permute-start.16 = (bf16[256,2048]{1,0:T(8,128)(2,1)S(1)}, bf16[256,2048]{1,0:T(8,128)(2,1)S(1)}, u32[]{:S(2)}, u32[]{:S(2)}) collective-permute-start(bf16[256,2048]{1,0:T(8,128)(2,1)S(1)} %get-tuple-element.74.refs_18_), channel_id=1, source_target_pairs={{0,16},{4,52},{64,80},{68,116},{8,24},{12,60},{72,88},{76,124},{1,... | collective-permute-start | bytes 3145736 | tf_op jit(solution)/shard_map/ppermute | solution.py:80
  70.3 23.7 %collective-permute-start.22 = (bf16[256,2048]{1,0:T(8,128)(2,1)S(1)}, bf16[256,2048]{1,0:T(8,128)(2,1)S(1)}, u32[]{:S(2)}, u32[]{:S(2)}) collective-permute-start(bf16[256,2048]{1,0:T(8,128)(2,1)S(1)} %get-tuple-element.79.refs_19_), channel_id=1, source_target_pairs={{0,16},{4,52},{64,80},{68,116},{8,24},{12,60},{72,88},{76,124},{1,... | collective-permute-start | bytes 3145736 | tf_op jit(solution)/shard_map/ppermute | solution.py:80
  77.1 29.6 %collective-permute-start.24 = (bf16[512,2048]{1,0:T(8,128)(2,1)S(1)}, bf16[512,2048]{1,0:T(8,128)(2,1)S(1)}, u32[]{:S(2)}, u32[]{:S(2)}) collective-permute-start(bf16[512,2048]{1,0:T(8,128)(2,1)S(1)} %shard_map.87.refs_18_), channel_id=1, source_target_pairs={{0,1},{4,7},{64,65},{68,71},{8,9},{12,15},{72,73},{76,79},{1,0},{5... | collective-permute-start | bytes 6291464 | tf_op jit(solution)/shard_map/ppermute | solution.py:80
  84.7 12.9 %collective-permute-start.19 = (bf16[128,2048]{1,0:T(8,128)(2,1)S(1)}, bf16[128,2048]{1,0:T(8,128)(2,1)S(1)}, u32[]{:S(2)}, u32[]{:S(2)}) collective-permute-start(bf16[128,2048]{1,0:T(8,128)(2,1)S(1)} %get-tuple-element.81), channel_id=1, source_target_pairs={{0,48},{4,20},{64,112},{68,84},{8,56},{12,28},{72,120},{76,92},{1,... | collective-permute-start | bytes 1572872 | tf_op jit(solution)/shard_map/ppermute | solution.py:80
  94.2 12.5 %collective-permute-start.25 = (bf16[128,2048]{1,0:T(8,128)(2,1)S(1)}, bf16[128,2048]{1,0:T(8,128)(2,1)S(1)}, u32[]{:S(2)}, u32[]{:S(2)}) collective-permute-start(bf16[128,2048]{1,0:T(8,128)(2,1)S(1)} %get-tuple-element.86), channel_id=1, source_target_pairs={{0,48},{4,20},{64,112},{68,84},{8,56},{12,28},{72,120},{76,92},{1,... | collective-permute-start | bytes 1572872 | tf_op jit(solution)/shard_map/ppermute | solution.py:80
  97.8 6.4 %collective-permute-start.20 = (bf16[64,2048]{1,0:T(8,128)(2,1)S(1)}, bf16[64,2048]{1,0:T(8,128)(2,1)S(1)}, u32[]{:S(2)}, u32[]{:S(2)}) collective-permute-start(bf16[64,2048]{1,0:T(8,128)(2,1)S(1)} %slice.55), channel_id=1, source_target_pairs={{0,72},{4,68},{64,0},{68,12},{8,64},{12,76},{72,8},{76,4},{1,73},{... | collective-permute-start | bytes 786440 | tf_op jit(solution)/shard_map/ppermute | solution.py:80
  104.3 12.7 %collective-permute-start.21 = (bf16[64,2048]{1,0:T(8,128)(2,1)S(1)}, bf16[64,2048]{1,0:T(8,128)(2,1)S(1)}, u32[]{:S(2)}, u32[]{:S(2)}) collective-permute-start(bf16[64,2048]{1,0:T(8,128)(2,1)S(1)} %fusion.1), channel_id=1, source_target_pairs={{0,8},{4,12},{64,72},{68,76},{8,0},{12,4},{72,64},{76,68},{1,9},{5... | collective-permute-start | bytes 786440 | tf_op jit(solution)/shard_map/ppermute | solution.py:80
  106.9 8.4 %collective-permute-start.26 = (bf16[64,2048]{1,0:T(8,128)(2,1)S(1)}, bf16[64,2048]{1,0:T(8,128)(2,1)S(1)}, u32[]{:S(2)}, u32[]{:S(2)}) collective-permute-start(bf16[64,2048]{1,0:T(8,128)(2,1)S(1)} %slice.54), channel_id=1, source_target_pairs={{0,72},{4,68},{64,0},{68,12},{8,64},{12,76},{72,8},{76,4},{1,73},{... | collective-permute-start | bytes 786440 | tf_op jit(solution)/shard_map/ppermute | solution.py:80
  108.0 10.4 %collective-permute-start.32 = (bf16[512,512]{1,0:T(8,128)(2,1)S(1)}, bf16[512,512]{1,0:T(8,128)(2,1)S(1)}, u32[]{:S(2)}, u32[]{:S(2)}) collective-permute-start(bf16[512,512]{1,0:T(8,128)(2,1)S(1)} %get-tuple-element.91), channel_id=1, source_target_pairs={{0,3},{4,5},{64,67},{68,69},{8,11},{12,13},{72,75},{76,77},{1,2},{... | collective-permute-start | bytes 1572872 | tf_op jit(solution)/shard_map/ppermute | solution.py:80
  110.1 13.9 %collective-permute-start.30 = (bf16[512,512]{1,0:T(8,128)(2,1)S(1)}, bf16[512,512]{1,0:T(8,128)(2,1)S(1)}, u32[]{:S(2)}, u32[]{:S(2)}) collective-permute-start(bf16[512,512]{1,0:T(8,128)(2,1)S(1)} %get-tuple-element.93), channel_id=1, source_target_pairs={{0,3},{4,5},{64,67},{68,69},{8,11},{12,13},{72,75},{76,77},{1,2},{... | collective-permute-start | bytes 1572872 | tf_op jit(solution)/shard_map/ppermute | solution.py:80
  115.4 10.2 %collective-permute-start.27 = (bf16[64,2048]{1,0:T(8,128)(2,1)S(1)}, bf16[64,2048]{1,0:T(8,128)(2,1)S(1)}, u32[]{:S(2)}, u32[]{:S(2)}) collective-permute-start(bf16[64,2048]{1,0:T(8,128)(2,1)S(1)} %fusion), channel_id=1, source_target_pairs={{0,8},{4,12},{64,72},{68,76},{8,0},{12,4},{72,64},{76,68},{1,9},{5... | collective-permute-start | bytes 786440 | tf_op jit(solution)/shard_map/ppermute | solution.py:80
  117.1 9.0 %collective-permute-start.28 = (bf16[64,2048]{1,0:T(8,128)(2,1)S(1)}, bf16[64,2048]{1,0:T(8,128)(2,1)S(1)}, u32[]{:S(2)}, u32[]{:S(2)}) collective-permute-start(bf16[64,2048]{1,0:T(8,128)(2,1)S(1)} %add_convert_fusion.3.refs_0_), channel_id=1, source_target_pairs={{0,4},{4,0},{64,68},{68,64},{8,12},{12,8},{72,76},{76,72},{1,5},{5... | collective-permute-start | bytes 786440 | tf_op jit(solution)/shard_map/ppermute | solution.py:80
  118.4 11.2 %collective-permute-start.33 = (bf16[512,512]{1,0:T(8,128)(2,1)S(1)}, bf16[512,512]{1,0:T(8,128)(2,1)S(1)}, u32[]{:S(2)}, u32[]{:S(2)}) collective-permute-start(bf16[512,512]{1,0:T(8,128)(2,1)S(1)} %get-tuple-element.89), channel_id=1, source_target_pairs={{0,3},{4,5},{64,67},{68,69},{8,11},{12,13},{72,75},{76,77},{1,2},{... | collective-permute-start | bytes 1572872 | tf_op jit(solution)/shard_map/ppermute | solution.py:80
  124.0 11.2 %collective-permute-start.31 = (bf16[512,512]{1,0:T(8,128)(2,1)S(1)}, bf16[512,512]{1,0:T(8,128)(2,1)S(1)}, u32[]{:S(2)}, u32[]{:S(2)}) collective-permute-start(bf16[512,512]{1,0:T(8,128)(2,1)S(1)} %get-tuple-element.87), channel_id=1, source_target_pairs={{0,3},{4,5},{64,67},{68,69},{8,11},{12,13},{72,75},{76,77},{1,2},{... | collective-permute-start | bytes 1572872 | tf_op jit(solution)/shard_map/ppermute | solution.py:80
  125.7 1.6 %collective-permute-start.29 = (bf16[64,2048]{1,0:T(8,128)(2,1)S(1)}, bf16[64,2048]{1,0:T(8,128)(2,1)S(1)}, u32[]{:S(2)}, u32[]{:S(2)}) collective-permute-start(bf16[64,2048]{1,0:T(8,128)(2,1)S(1)} %add_convert_fusion.2.refs_1_), channel_id=1, source_target_pairs={{0,4},{4,0},{64,68},{68,64},{8,12},{12,8},{72,76},{76,72},{1,5},{5... | collective-permute-start | bytes 786440 | tf_op jit(solution)/shard_map/ppermute | solution.py:80
